TPU v7x, 512 devices: a whole 4x8x8 slice. The times are simulated.
512 devices in a mesh: bin: 64 (over x, y, z_lo), diag: 8 (over z_hi, core).
Axes of the slice: x: 4, y: 8, z: 8 (z_hi: 4, z_lo: 2; z = z_hi * 2 + z_lo), core: 2. Of those that a mesh axis runs over, the one named last changes fastest.
Arguments:
- embeddings: bfloat16 [256, 24576], P('diag', 'bin'), may hold values from -6 to 6
- projection: bfloat16 [256, 64], P('diag'), may hold values from -0.375 to 0.375
- dist_bias: float32 [32, 256], replicated, may hold values from -3 to 3
- conv_weight: bfloat16 [2, 9, 32, 32], replicated, may hold values from -0.375 to 0.375
- head_weight: float32 [32], replicated, may hold values from -1 to 1
- dilations: int32 [2], replicated, may hold values from 1 to 4, as said below
- band_limit: int32 [24576], P('bin'), may hold values from 64 to 256
- cotangent: float32 [256, 24576], P('diag', 'bin'), may hold values from -6 to 6
Outputs:
- predicted: float32 [256, 24576], P('diag', 'bin')
- grad_embed: float32 [256, 24576], P('diag', 'bin')
- grad_proj: float32 [256, 64], P('diag')
- grad_conv: float32 [2, 9, 32, 32], replicated
Inputs may be any that keep to these rules, and one draw needn't show every extreme that they name: `dilations`: one of the 2 layers has dilation exactly 4.
All inputs are finite; a program needn't handle non-finite values.
Results may differ from a plain program's by a relative error of at most 0.0059.
Values may be sent and summed in bfloat16 or wider, within the bound.
No kernel may reach another device: no remote copies, remote signals or barrier semaphores. Data moves between devices by JAX's collectives and lax.ppermute only.
A program may use at most 128 MiB of HBM per device.

v0:
```python
import math

import jax
import jax.numpy as jnp
from jax import lax
from jax.sharding import PartitionSpec as P

MAXDIL = 4


HIGHEST = lax.Precision.HIGHEST


def with_halo(block, sides, width):
    for axis, dim in sides:
        count = lax.axis_size(axis)
        forward = [(i, i + 1) for i in range(count - 1)]
        backward = [(target, source) for source, target in forward]
        low = lax.ppermute(
            lax.slice_in_dim(block, block.shape[dim] - width, None, axis=dim), axis, forward
        )
        high = lax.ppermute(lax.slice_in_dim(block, 0, width, axis=dim), axis, backward)
        block = jnp.concatenate([low, block, high], axis=dim)
    return block


def from_behind(x, axis, by):
    size = lax.axis_size(axis)
    pairs = [(i, i + by) for i in range(size) if 0 <= i + by < size]
    return lax.ppermute(x, axis, pairs)


def skew_read(window, diag_count, row_count):
    channels = window.shape[0]
    span_len = row_count + diag_count - 1
    tiled_rows = jnp.broadcast_to(window[:, None, :], (channels, diag_count, span_len)).reshape(
        channels, diag_count * span_len
    )
    tiled_rows = jnp.pad(tiled_rows, ((0, 0), (0, diag_count)))
    return tiled_rows.reshape(channels, diag_count, span_len + 1)[:, :, :row_count]


def skew_write(values):
    channels, diag_count, row_count = values.shape
    span_len = row_count + diag_count - 1
    padded = jnp.pad(values, ((0, 0), (0, 0), (0, span_len + 1 - row_count)))
    flat_view = padded.reshape(channels, diag_count * (span_len + 1))[:, : diag_count * span_len]
    return jnp.sum(flat_view.reshape(channels, diag_count, span_len), axis=1)


def tap_slice(padded, diag_start, row_start, diag_count, row_count):
    return lax.dynamic_slice(
        padded, (0, diag_start, row_start), (padded.shape[0], diag_count, row_count)
    )


def stacked_taps(padded, dilation, diag_count, row_count, sign):
    pieces = []
    for kernel_tap in range(9):
        along_bin = kernel_tap // 3 - 1
        along_diag = kernel_tap % 3 - 1
        pieces.append(
            tap_slice(
                padded,
                MAXDIL + sign * along_diag * dilation,
                MAXDIL + sign * along_bin * dilation,
                diag_count,
                row_count,
            )
        )
    return jnp.concatenate(pieces, axis=0)


def conv_forward(padded, weight, dilation, diag_count, row_count):
    outputs = weight.shape[1]
    flat_weight = jnp.transpose(weight, (1, 0, 2)).reshape(outputs, 9 * weight.shape[2])
    stacked = stacked_taps(padded, dilation, diag_count, row_count, 1)
    return jnp.einsum("ok,kdi->odi", flat_weight, stacked, preferred_element_type=jnp.float32)


def conv_transpose(padded, weight, dilation, diag_count, row_count):
    inputs = weight.shape[2]
    flat_weight = jnp.transpose(weight, (2, 0, 1)).reshape(inputs, 9 * weight.shape[1])
    stacked = stacked_taps(padded, dilation, diag_count, row_count, -1)
    return jnp.einsum("ck,kdi->cdi", flat_weight, stacked, preferred_element_type=jnp.float32)


def weight_grad(grad_values, padded, dilation, diag_count, row_count):
    outputs = grad_values.shape[0]
    inputs = padded.shape[0]
    stacked = stacked_taps(padded, dilation, diag_count, row_count, 1)
    product = jnp.einsum("odi,kdi->ok", grad_values, stacked, preferred_element_type=jnp.float32)
    return jnp.transpose(product.reshape(outputs, 9, inputs), (1, 0, 2))


def widen_band(values):
    return with_halo(values, (("bin", 2), ("diag", 1)), MAXDIL)


def on_device(
    embeddings, projection, dist_bias, conv_weight, head_weight, dilations, band_limit, cotangent
):
    channels = conv_weight.shape[2]
    diag_dev = cotangent.shape[0]
    rows_dev = cotangent.shape[1]
    margin = MAXDIL
    total_bins = rows_dev * lax.axis_size("bin")
    total_diags = diag_dev * lax.axis_size("diag")
    first_row = lax.axis_index("bin") * rows_dev
    first_diag = lax.axis_index("diag") * diag_dev
    dilation_one = dilations[0]
    dilation_two = dilations[1]
    projected = lax.psum(
        jnp.einsum("ek,eb->kb", projection, embeddings, preferred_element_type=jnp.float32), "diag"
    )
    left_proj = projected[:channels]
    right_proj = projected[channels:]
    right_next = from_behind(right_proj, "bin", -1)
    right_both = jnp.concatenate([right_proj, right_next], axis=1)
    bias_padded = jnp.pad(dist_bias, ((0, 0), (margin, margin)))
    row_ids = first_row + jnp.arange(rows_dev, dtype=jnp.int32)[None, :]
    diag_ids = first_diag + jnp.arange(diag_dev, dtype=jnp.int32)[:, None]
    inside = row_ids + diag_ids < total_bins
    inside_mask = inside.astype(jnp.float32)
    counted_mask = (inside & (diag_ids < band_limit[None, :])).astype(jnp.float32)
    window = lax.dynamic_slice_in_dim(right_both, first_diag, rows_dev + diag_dev - 1, 1)
    bias_cols = lax.dynamic_slice_in_dim(bias_padded, first_diag + margin, diag_dev, 1)
    tanh_zero = jnp.tanh(
        left_proj[:, None, :] + skew_read(window, diag_dev, rows_dev) + bias_cols[:, :, None]
    )
    pair_zero = (inside_mask * tanh_zero).astype(jnp.bfloat16)
    padded_zero = with_halo(pair_zero, (("bin", 2), ("diag", 1)), margin)
    act_one = conv_forward(padded_zero, conv_weight[0], dilation_one, diag_dev, rows_dev)
    tanh_one = jnp.tanh(act_one)
    pair_one = (inside_mask * (pair_zero.astype(jnp.float32) + tanh_one)).astype(jnp.bfloat16)
    padded_one = widen_band(pair_one)
    tanh_two = jnp.tanh(conv_forward(padded_one, conv_weight[1], dilation_two, diag_dev, rows_dev))
    pred_local = counted_mask * jnp.einsum("c,cdi->di", head_weight, tanh_two, precision=HIGHEST)
    grad_two = (
        (cotangent * counted_mask)[None, :, :]
        * head_weight[:, None, None]
        * (1.0 - tanh_two * tanh_two)
    ).astype(jnp.bfloat16)
    wgrad_two = weight_grad(grad_two, padded_one, dilation_two, diag_dev, rows_dev)
    back_one = conv_transpose(
        widen_band(grad_two), conv_weight[1], dilation_two, diag_dev, rows_dev
    )
    grad_one = (back_one * inside_mask * (1.0 - tanh_one * tanh_one)).astype(jnp.bfloat16)
    wgrad_one = weight_grad(grad_one, padded_zero, dilation_one, diag_dev, rows_dev)
    back_zero = inside_mask * back_one + conv_transpose(
        widen_band(grad_one), conv_weight[0], dilation_one, diag_dev, rows_dev
    )
    grad_pre = back_zero * inside_mask * (1.0 - tanh_zero * tanh_zero)
    left_local = jnp.sum(grad_pre, axis=1)
    spilled = skew_write(grad_pre)
    buffer = lax.dynamic_update_slice_in_dim(
        jnp.zeros((channels, 2 * rows_dev), jnp.float32), spilled, first_diag, 1
    )
    incoming = from_behind(buffer[:, rows_dev:].astype(jnp.bfloat16), "bin", 1).astype(jnp.float32)
    grad_right = buffer[:, :rows_dev] + incoming
    grad_both = lax.psum(jnp.concatenate([left_local, grad_right], axis=0), "diag")
    grad_embed = jnp.einsum(
        "ek,kb->eb", projection.astype(jnp.float32), grad_both, precision=HIGHEST
    )
    proj_part = jnp.einsum(
        "eb,kb->ek", embeddings.astype(jnp.float32), grad_both, precision=HIGHEST
    )
    conv_part = jnp.stack([wgrad_one, wgrad_two])
    conv_sum = lax.psum(conv_part, ("bin", "diag"))
    proj_sum = lax.psum(proj_part, "bin")
    scaling = 1.0 / math.sqrt(total_bins * total_diags)
    return (pred_local, grad_embed, scaling * proj_sum, scaling * conv_sum)


def solution(mesh):
    return jax.shard_map(
        on_device,
        mesh=mesh,
        in_specs=(
            P("diag", "bin"),
            P("diag", None),
            P(),
            P(),
            P(),
            P(),
            P("bin"),
            P("diag", "bin"),
        ),
        out_specs=(P("diag", "bin"), P("diag", "bin"), P("diag", None), P()),
        check_vma=False,
    )
```

profile of v0, /device:TPU:128, one launch (start us, length us, event | category | flops | bytes accessed | tf_op | source)
XLA Modules:
  0.0 927.2 jit_solution(16918366745017731205)
XLA Ops:
  7.9 1.5 fusion.26
  9.6 78.5 %all-reduce.7.cloned.1.call-done = f32[64,384]{1,0:T(8,128)} async-done(((f32[64,384]{1,0:T(8,128)}), f32[64,384]{1,0:T(8,128)}) %all-reduce.7.cloned.1.call-update) | async-done | bytes 98320 | tf_op jit(solution)/shard_map/psum | solution.py:113
  88.9 1.3 collective-permute-start
  91.1 3.8 collective-permute-done
  95.2 2.3 reshape.111
  97.5 1.6 pad.12
  99.1 2.9 reshape.112
  101.9 1.5 slice.109
  104.7 3.6 collective-permute-start.1
  108.3 1.3 collective-permute-start.2
  109.6 10.4 %collective-permute-done.1 = bf16[32,32,4]{2,0,1:T(8,128)(2,1)S(1)} collective-permute-done((bf16[32,32,4]{2,0,1:T(8,128)(2,1)S(1)}, bf16[32,32,4]{2,0,1:T(8,128)(2,1)S(1)}, u32[]{:S(2)}, u32[]{:S(2)}) %collective-permute-start.1) | collective-permute-done | bytes 8224 | tf_op jit(solution)/shard_map/ppermute | solution.py:19
  120.0 4.1 collective-permute-done.2
  125.0 1.9 collective-permute-start.3
  126.9 4.5 collective-permute-start.4
  135.4 1.5 pad_maximum_fusion
  141.3 3.2 fusion.11
  144.8 1.5 collective-permute-start.5
  146.3 1.3 collective-permute-start.6
  147.6 3.4 collective-permute-done.5
  150.9 10.3 %collective-permute-done.6 = bf16[32,32,4]{2,0,1:T(8,128)(2,1)S(1)} collective-permute-done((bf16[32,32,4]{2,0,1:T(8,128)(2,1)S(1)}, bf16[32,32,4]{2,0,1:T(8,128)(2,1)S(1)}, u32[]{:S(2)}, u32[]{:S(2)}) %collective-permute-start.6) | collective-permute-done | bytes 8224 | tf_op jit(solution)/shard_map/ppermute | solution.py:22
  162.1 3.4 collective-permute-start.7
  165.5 12.8 %collective-permute-start.8 = (bf16[32,4,392]{2,0,1:T(8,128)(2,1)}, bf16[32,4,392]{2,0,1:T(8,128)(2,1)}, u32[]{:S(2)}, u32[]{:S(2)}) collective-permute-start(bf16[32,4,392]{2,0,1:T(8,128)(2,1)} %get-tuple-element.13), channel_id=1, source_target_pairs={{1,0},{2,1},{3,2},{4,3},{5,4},{6,5},{7,6},{9,8},{10,9},{11,10},{12... | collective-permute-start | bytes 301064 | tf_op jit(solution)/shard_map/ppermute | solution.py:22
  181.1 1.5 pad_maximum_fusion.1
  185.9 1.4 convolution_tanh_fusion
  189.6 1.5 collective-permute-start.9
  191.0 1.3 collective-permute-start.10
  192.3 10.4 %collective-permute-done.9 = bf16[32,32,4]{2,0,1:T(8,128)(2,1)S(1)} collective-permute-done((bf16[32,32,4]{2,0,1:T(8,128)(2,1)S(1)}, bf16[32,32,4]{2,0,1:T(8,128)(2,1)S(1)}, u32[]{:S(2)}, u32[]{:S(2)}) %collective-permute-start.9) | collective-permute-done | bytes 8224 | tf_op jit(solution)/shard_map/ppermute | solution.py:19
  202.8 4.1 collective-permute-done.10
  207.0 1.9 collective-permute-start.11
  209.0 4.5 collective-permute-start.12
  214.2 2.1 collective-permute-done.12
  220.9 1.6 fusion.4
  222.6 1.3 collective-permute-start.13
  223.9 1.3 collective-permute-start.14
  225.2 1.9 fusion.28
  227.2 2.0 collective-permute-done.13
  229.2 10.2 %collective-permute-done.14 = bf16[32,32,4]{2,0,1:T(8,128)(2,1)S(1)} collective-permute-done((bf16[32,32,4]{2,0,1:T(8,128)(2,1)S(1)}, bf16[32,32,4]{2,0,1:T(8,128)(2,1)S(1)}, u32[]{:S(2)}, u32[]{:S(2)}) %collective-permute-start.14) | collective-permute-done | bytes 8224 | tf_op jit(solution)/shard_map/ppermute | solution.py:22
  239.6 2.9 collective-permute-start.15
  242.5 3.7 collective-permute-start.16
  246.2 1.9 fusion.27
  252.7 2.5 fusion.25
  256.4 2.3 reshape.117
  258.7 3.3 reshape.118
  263.1 1.3 collective-permute-start.17
  266.6 268.4 %all-reduce.11.cloned.1.call-done = f32[2,9,32,32]{2,3,1,0:T(8,128)} async-done(((f32[2,9,32,32]{2,3,1,0:T(8,128)}), f32[2,9,32,32]{2,3,1,0:T(8,128)}) %all-reduce.11.cloned.1.call-update) | async-done | bytes 73744 | tf_op jit(solution)/shard_map/psum | solution.py:169
  536.9 72.2 %all-reduce.9.cloned.1.call-done = f32[64,384]{1,0:T(8,128)} async-done(((f32[64,384]{1,0:T(8,128)}), f32[64,384]{1,0:T(8,128)}) %all-reduce.9.cloned.1.call-update) | async-done | bytes 98320 | tf_op jit(solution)/shard_map/psum | solution.py:161
  610.1 307.9 %psum.30 = f32[32,64]{1,0:T(8,128)S(1)} all-reduce(f32[32,64]{1,0:T(8,128)S(1)} %convolution_bitcast_fusion.1), channel_id=1, replica_groups=mesh['bin'=64,'diag'=8] {'bin'}, use_global_device_ids=true, to_apply=%region_4.5 | all-reduce | flops 2048 | bytes 16384 | tf_op jit(solution)/shard_map/psum | solution.py:170
  918.6 1.7 convolution_bitcast_fusion
  (114 shorter events, 35.4 us)
Async XLA Ops:
  7.2 0.7 copy-start
  7.2 80.9 %all-reduce.7.cloned.1.call-start = ((), (), s32[]{:S(2)}) async-start(), calls=%async_computation | async-start | bytes 196608 | tf_op jit(solution)/shard_map/psum | solution.py:113
  9.5 525.5 %all-reduce.11.cloned.1.call-start = ((), (), s32[]{:S(2)}) async-start(), calls=%async_computation.2 | async-start | bytes 589824 | tf_op jit(solution)/shard_map/psum | solution.py:169
  88.9 6.0 collective-permute-start
  101.9 7.6 copy-start.4
  103.5 28.0 %copy-start.9 = (s32[2]{0:T(128)S(1)}, s32[2]{0:T(128)}, u32[]{:S(2)}) copy-start(s32[2]{0:T(128)} %param.13) | copy-start | bytes 28
  104.7 15.3 %collective-permute-start.1 = (bf16[32,32,4]{2,0,1:T(8,128)(2,1)S(1)}, bf16[32,32,4]{2,0,1:T(8,128)(2,1)S(1)}, u32[]{:S(2)}, u32[]{:S(2)}) collective-permute-start(bf16[32,32,4]{2,0,1:T(8,128)(2,1)S(1)} %get-tuple-element.22), channel_id=1, source_target_pairs={{0,8},{8,16},{16,24},{24,32},{32,40},{40,48},{48,56},{56,64},{64,7... | collective-permute-start | bytes 24584 | tf_op jit(solution)/shard_map/ppermute | solution.py:19
  108.3 15.9 %collective-permute-start.2 = (bf16[32,32,4]{2,0,1:T(8,128)(2,1)S(1)}, bf16[32,32,4]{2,0,1:T(8,128)(2,1)S(1)}, u32[]{:S(2)}, u32[]{:S(2)}) collective-permute-start(bf16[32,32,4]{2,0,1:T(8,128)(2,1)S(1)} %get-tuple-element.23), channel_id=1, source_target_pairs={{8,0},{16,8},{24,16},{32,24},{40,32},{48,40},{56,48},{64,56},{72,6... | collective-permute-start | bytes 24584 | tf_op jit(solution)/shard_map/ppermute | solution.py:22
  125.0 10.4 %collective-permute-start.3 = (bf16[32,4,392]{2,0,1:T(8,128)(2,1)}, bf16[32,4,392]{2,0,1:T(8,128)(2,1)S(1)}, u32[]{:S(2)}, u32[]{:S(2)}) collective-permute-start(bf16[32,4,392]{2,0,1:T(8,128)(2,1)} %get-tuple-element.14), channel_id=1, source_target_pairs={{0,1},{1,2},{2,3},{3,4},{4,5},{5,6},{6,7},{8,9},{9,10},{10,11},{11... | collective-permute-start | bytes 301064 | tf_op jit(solution)/shard_map/ppermute | solution.py:19
  126.9 8.5 collective-permute-start.4
  140.1 1.2 copy-start.3
  141.3 3.4 copy-start.1
  144.8 6.1 collective-permute-start.5
  146.3 15.0 %collective-permute-start.6 = (bf16[32,32,4]{2,0,1:T(8,128)(2,1)S(1)}, bf16[32,32,4]{2,0,1:T(8,128)(2,1)S(1)}, u32[]{:S(2)}, u32[]{:S(2)}) collective-permute-start(bf16[32,32,4]{2,0,1:T(8,128)(2,1)S(1)} %get-tuple-element.21), channel_id=1, source_target_pairs={{8,0},{16,8},{24,16},{32,24},{40,32},{48,40},{56,48},{64,56},{72,6... | collective-permute-start | bytes 24584 | tf_op jit(solution)/shard_map/ppermute | solution.py:22
  162.1 19.0 %collective-permute-start.7 = (bf16[32,4,392]{2,0,1:T(8,128)(2,1)}, bf16[32,4,392]{2,0,1:T(8,128)(2,1)S(1)}, u32[]{:S(2)}, u32[]{:S(2)}) collective-permute-start(bf16[32,4,392]{2,0,1:T(8,128)(2,1)} %get-tuple-element.12), channel_id=1, source_target_pairs={{0,1},{1,2},{2,3},{3,4},{4,5},{5,6},{6,7},{8,9},{9,10},{10,11},{11... | collective-permute-start | bytes 301064 | tf_op jit(solution)/shard_map/ppermute | solution.py:19
  165.5 15.6 %collective-permute-start.8 = (bf16[32,4,392]{2,0,1:T(8,128)(2,1)}, bf16[32,4,392]{2,0,1:T(8,128)(2,1)}, u32[]{:S(2)}, u32[]{:S(2)}) collective-permute-start(bf16[32,4,392]{2,0,1:T(8,128)(2,1)} %get-tuple-element.13), channel_id=1, source_target_pairs={{1,0},{2,1},{3,2},{4,3},{5,4},{6,5},{7,6},{9,8},{10,9},{11,10},{12... | collective-permute-start | bytes 301064 | tf_op jit(solution)/shard_map/ppermute | solution.py:22
  185.9 1.5 copy-start.7
  185.9 2.4 copy-start.5
  185.9 2.4 copy-start.8
  189.6 13.2 %collective-permute-start.9 = (bf16[32,32,4]{2,0,1:T(8,128)(2,1)S(1)}, bf16[32,32,4]{2,0,1:T(8,128)(2,1)S(1)}, u32[]{:S(2)}, u32[]{:S(2)}) collective-permute-start(bf16[32,32,4]{2,0,1:T(8,128)(2,1)S(1)} %get-tuple-element.18), channel_id=1, source_target_pairs={{0,8},{8,16},{16,24},{24,32},{32,40},{40,48},{48,56},{56,64},{64,7... | collective-permute-start | bytes 24584 | tf_op jit(solution)/shard_map/ppermute | solution.py:19
  191.0 15.8 %collective-permute-start.10 = (bf16[32,32,4]{2,0,1:T(8,128)(2,1)S(1)}, bf16[32,32,4]{2,0,1:T(8,128)(2,1)S(1)}, u32[]{:S(2)}, u32[]{:S(2)}) collective-permute-start(bf16[32,32,4]{2,0,1:T(8,128)(2,1)S(1)} %get-tuple-element.19), channel_id=1, source_target_pairs={{8,0},{16,8},{24,16},{32,24},{40,32},{48,40},{56,48},{64,56},{72,6... | collective-permute-start | bytes 24584 | tf_op jit(solution)/shard_map/ppermute | solution.py:22
  207.0 7.2 collective-permute-start.11
  209.0 7.4 collective-permute-start.12
  219.5 1.4 copy-start.2
  220.3 25.9 %slice-start = ((s8[7077888]{0:T(1024)(128)(4,1)}), s8[4194304]{0:T(1024)(128)(4,1)S(1)}, s32[]{:S(2)}) async-start(s8[7077888]{0:T(1024)(128)(4,1)} %bitcast.114), calls=%async_computation.3 | async-start | bytes 8388608
  220.9 25.4 %slice-start.1 = ((s8[7077888]{0:T(1024)(128)(4,1)}), s8[2883584]{0:T(1024)(128)(4,1)S(1)}, s32[]{:S(2)}) async-start(s8[7077888]{0:T(1024)(128)(4,1)} %bitcast.114), calls=%async_computation.4 | async-start | bytes 5767168
  222.6 6.6 collective-permute-start.13
  223.9 15.5 %collective-permute-start.14 = (bf16[32,32,4]{2,0,1:T(8,128)(2,1)S(1)}, bf16[32,32,4]{2,0,1:T(8,128)(2,1)S(1)}, u32[]{:S(2)}, u32[]{:S(2)}) collective-permute-start(bf16[32,32,4]{2,0,1:T(8,128)(2,1)S(1)} %get-tuple-element.17), channel_id=1, source_target_pairs={{8,0},{16,8},{24,16},{32,24},{40,32},{48,40},{56,48},{64,56},{72,6... | collective-permute-start | bytes 24584 | tf_op jit(solution)/shard_map/ppermute | solution.py:22
  239.6 8.6 collective-permute-start.15
  242.5 6.4 collective-permute-start.16
  262.0 656.7 %copy-start.6 = (bf16[32,64]{1,0:T(8,128)(2,1)S(1)}, bf16[32,64]{1,0:T(8,128)(2,1)}, u32[]{:S(2)}) copy-start(bf16[32,64]{1,0:T(8,128)(2,1)} %param.9) | copy-start | bytes 12292
  263.1 2.8 collective-permute-start.17
  265.2 343.9 %all-reduce.9.cloned.1.call-start = ((), (), s32[]{:S(2)}) async-start(), calls=%async_computation.1 | async-start | bytes 196608 | tf_op jit(solution)/shard_map/psum | solution.py:161
Sparse Core Ops, SparseCore 0:
  11.5 76.5 all-reduce.6
  265.3 269.6 all-reduce.10
  537.9 71.1 all-reduce.8
where the time goes:
time: 937 us; the launch traced here: 927 us
  waiting for transfers between devices  482 us (51%)
  blocking collectives  308 us (33%)
  starting transfers between devices  51.5 us (5%)
  local copies, waits for them, and re-layouts  34.3 us (4%)
  between operations  20 us (2%)
  matrix products  17.8 us (2%)
  other arithmetic  13.7 us (1%)
    psum x1, blocking collectives, on_device(): proj_sum = lax.psum(proj_part, 'bin')  308 us
    psum x1, waiting for transfers between devices, on_device(): conv_sum = lax.psum(conv_part, ('bin', 'diag'))  268 us
    psum x1, waiting for transfers between devices, on_device(): lax.psum(jnp.einsum('ek,eb->kb', projection, embeddings, preferred_elemen...  78.5 us
    psum x1, waiting for transfers between devices, on_device(): lax.psum(jnp.concatenate([left_local, grad_right], axis=0), 'diag')  72.2 us
    ppermute x8, waiting for transfers between devices, with_halo(): lax.ppermute(lax.slice_in_dim(block, 0, width, axis=dim), axis, backward)  31.6 us
    ppermute x8, starting transfers between devices, with_halo(): lax.ppermute(lax.slice_in_dim(block, 0, width, axis=dim), axis, backward)  30.8 us
    ppermute x8, waiting for transfers between devices, with_halo(): lax.ppermute(lax.slice_in_dim(block, block.shape[dim] - width, None, axis...  26.9 us
  transfers between devices with their start and end apart: 21, of which 16 were waited for; matrix products, arithmetic and copies ran while one was open for 1% of the time, Pallas kernels for 0%

commit v1 on v0

v1 whole, which is shorter than its diff:
```python
import functools
import math

import jax
import jax.numpy as jnp
from jax import lax
from jax.experimental import pallas as pl
from jax.experimental.pallas import tpu as pltpu
from jax.sharding import PartitionSpec as P

C = 32
M = 16
LN = 512
BF = jnp.bfloat16
F32 = jnp.float32


def _dot(a, b):
    return jnp.dot(a, b, preferred_element_type=F32)


def _dot_nt(a, b):
    return lax.dot_general(a, b, (((1,), (1,)), ((), ())), preferred_element_type=F32)


def _split(x):
    hi = x.astype(BF)
    return hi, (x - hi.astype(F32)).astype(BF)


def band_kernel(dil_ref, w_ref, wt_ref, t_ref):
    rows = lax.broadcasted_iota(jnp.int32, (256, 512), 0) >> 5
    cols = lax.broadcasted_iota(jnp.int32, (256, 512), 1) >> 5
    delta = cols - rows - 4
    spread = (
        (lax.broadcasted_iota(jnp.int32, (C, 512), 1) & 31)
        == lax.broadcasted_iota(jnp.int32, (C, 512), 0)
    ).astype(F32).astype(BF)
    for layer in range(2):
        masks = [delta == b * dil_ref[layer] for b in (-1, 0, 1)]
        for kind, ref in ((0, w_ref), (1, wt_ref)):
            for slot in range(3):
                total = jnp.zeros((256, 512), F32)
                for b in range(3):
                    along = slot if kind == 0 else 2 - slot
                    w = ref[layer, 3 * along + b]
                    wide = _dot(jnp.concatenate([w] * 8, axis=0), spread)
                    total = jnp.where(masks[b if kind == 0 else 2 - b], wide, total)
                t_ref[2 * kind + layer, :, slot * 512 : (slot + 1) * 512] = total.astype(BF)


def band_weights(dilations, conv_weight):
    return pl.pallas_call(
        band_kernel,
        out_shape=jax.ShapeDtypeStruct((4, 256, 1536), BF),
        in_specs=[
            pl.BlockSpec(memory_space=pltpu.SMEM),
            pl.BlockSpec(memory_space=pltpu.VMEM),
            pl.BlockSpec(memory_space=pltpu.VMEM),
        ],
        out_specs=pl.BlockSpec(memory_space=pltpu.VMEM),
        compiler_params=pltpu.CompilerParams(vmem_limit_bytes=32 * 2**20),
        cost_estimate=pl.CostEstimate(flops=10**9, bytes_accessed=4 * 10**6, transcendentals=0),
        name="band_weights",
    )(dilations, conv_weight, jnp.swapaxes(conv_weight, 2, 3))


def pair_kernel(
    total_bins, total_diags,
    sc_ref, own_ref, next_ref, prev_ref, bias_ref, limit_ref, head_ref, t_ref,
    proj_ref, emb_ref, embn_ref,
    pred_ref, embed_ref, sums_ref,
    x0, x1, g2, g1, d0, d1, bk, mk, vbuf, ubuf, left, gwide, acc, lsum, rsum,
):
    first_row = sc_ref[0]
    first_diag = sc_ref[1]
    s1 = sc_ref[2]
    s2 = sc_ref[3]

    lane = lax.broadcasted_iota(jnp.int32, (8, LN), 1)
    low = lax.broadcasted_iota(jnp.int32, (C, 128), 1) < 64
    bin_id = first_row + jnp.where(lane < 448, lane, lane - LN)
    bin_ok = (bin_id >= 0) & (bin_id < total_bins)

    own = own_ref[...]
    nxt = next_ref[...]
    prv = prev_ref[...]
    left[:, :384] = own[:C]
    left[:, 384:] = jnp.where(low, nxt[:C, :128], prv[:C])
    low48 = lax.broadcasted_iota(jnp.int32, (48, 128), 1) < 64
    gwide[:, :384] = own[2 * C :]
    gwide[:, 384:] = jnp.where(low48, nxt[2 * C :, :128], prv[2 * C :])
    line = jnp.concatenate([prv[C : 2 * C], own[C : 2 * C], nxt[C : 2 * C]], axis=1)
    vbuf[...] = pltpu.roll(line, 784 - first_diag, 1)[:, :640]
    ubuf[...] = pltpu.roll(line, lax.rem(912 - first_diag, 896), 1)[:, :256]

    def store3(ref, row, value, shift):
        ref[0, pl.ds(row, C), :] = pltpu.roll(value, shift, 1).astype(BF)
        ref[1, pl.ds(row, C), :] = value.astype(BF)
        ref[2, pl.ds(row, C), :] = pltpu.roll(value, LN - shift, 1).astype(BF)

    def times(value, mask):
        return (value.reshape(4, 8, value.shape[1]) * mask[None]).reshape(value.shape)

    def stage_zero(g, carry):
        vg = pltpu.roll(vbuf[...], 640 - 8 * g, 1)
        ug = pltpu.roll(ubuf[...], 256 - 8 * g, 1)
        bg = pltpu.roll(bias_ref[...], 128 - 8 * g, 1)
        for r in range(8):
            k = 8 * g + r
            diag_id = first_diag - M + k
            ok = bin_ok & (bin_id + diag_id < total_bins) & (diag_id >= 0) & (diag_id < total_diags)
            mask = ok.astype(F32)
            mk[k] = mask
            shifted = jnp.concatenate(
                [vg[:, r : r + 384], jnp.where(low, vg[:, 384 + r : 512 + r], ug[:, r : r + 128])],
                axis=1,
            )
            t = jnp.tanh(left[...] + shifted + bg[:, r : r + 1])
            row = pl.multiple_of(k * C, C)
            store3(x0, row, times(t, mask), s1)

            @pl.when((g >= 2) & (g < 6))
            def _():
                d0[pl.ds(pl.multiple_of((k - M) * C, C), C), :] = times(
                    1.0 - t[:, :384] * t[:, :384], mask[:, :384]
                )
        return carry

    lax.fori_loop(0, 8, stage_zero, 0)

    def window(ref, first, width):
        rows = pl.ds(pl.multiple_of(first * C, 256), 512)
        return jnp.concatenate([ref[a, rows, :width] for a in range(3)], axis=0)

    def stage_one(g, carry):
        t1 = jnp.tanh(_dot(t_ref[0], window(x0, 8 * g, LN)))
        for r in range(8):
            k = 4 + 8 * g + r
            mask = mk[k]
            t = t1[r * C : (r + 1) * C]
            base = x0[1, pl.ds(pl.multiple_of(k * C, C), C), :].astype(F32)
            store3(x1, pl.multiple_of((k - 4) * C, C), times(base + t, mask), s2)
            d1[pl.ds(pl.multiple_of((k - 4) * C, C), C), :] = times(1.0 - t * t, mask)
        return carry

    lax.fori_loop(0, 7, stage_one, 0)

    head = head_ref[...]
    limits = limit_ref[...]
    own_bin = first_row + lax.broadcasted_iota(jnp.int32, (8, 384), 1)
    own_row = lax.broadcasted_iota(jnp.int32, (8, 384), 0)

    def stage_two(g, carry):
        t2 = jnp.tanh(_dot(t_ref[1], window(x1, 8 * g, LN)))
        cots = gwide[pl.ds(pl.multiple_of(8 * g, 8), 8), :]
        lines = []
        for r in range(8):
            k = 8 + 8 * g + r
            t = t2[r * C : (r + 1) * C]
            value = cots[r : r + 1] * (head * (1.0 - t * t))
            store3(g2, pl.multiple_of((k - 8) * C, C), value, s2)
            lines.append(jnp.sum(head[:, :384] * t[:, :384], axis=0, keepdims=True))

        @pl.when((g >= 1) & (g < 5))
        def _():
            diag_id = first_diag + 8 * (g - 1) + own_row
            ok = (own_bin + diag_id < total_bins) & (diag_id < limits)
            pred_ref[pl.ds(pl.multiple_of(8 * (g - 1), 8), 8), :] = jnp.where(
                ok, jnp.concatenate(lines, axis=0), 0.0
            )
        return carry

    lax.fori_loop(0, 6, stage_two, 0)

    def stage_three(g, carry):
        back = _dot(t_ref[3], window(g2, 8 * g, LN))
        for r in range(8):
            k = 12 + 8 * g + r
            value = back[r * C : (r + 1) * C]
            at = pl.multiple_of((k - 12) * C, C)
            store3(g1, at, value * d1[pl.ds(pl.multiple_of((k - 4) * C, C), C), :], s1)
            bk[pl.ds(at, C), :] = times(value, mk[k])[:, :384]
        return carry

    lax.fori_loop(0, 5, stage_three, 0)

    lsum[...] = jnp.zeros_like(lsum)
    rsum[...] = jnp.zeros_like(rsum)
    acc[...] = jnp.zeros_like(acc)

    def stage_four(g, carry):
        back = _dot(t_ref[2], window(g1, 8 * g, 384))
        part = jnp.zeros((C, 384), F32)
        skew = jnp.zeros((C, LN), F32)
        for r in range(8):
            kk = 8 * g + r
            value = back[r * C : (r + 1) * C] + bk[pl.ds(pl.multiple_of((kk + 4) * C, C), C), :]
            value = value * d0[pl.ds(pl.multiple_of(kk * C, C), C), :]
            part = part + value
            wide = jnp.concatenate([value, jnp.zeros((C, 128), F32)], axis=1)
            skew = skew + (pltpu.roll(wide, r, 1) if r else wide)
        lsum[...] += part
        rsum[...] += pltpu.roll(skew, 8 * g, 1)
        grad_two = g2[1, pl.ds(pl.multiple_of((8 * g + 8) * C, C), 256), :384]
        grad_one = g1[1, pl.ds(pl.multiple_of((8 * g + 4) * C, C), 256), :384]
        for a in range(3):
            near = x0[a, pl.ds(pl.multiple_of((8 * g + 12) * C, C), 512), :384]
            acc[a] += _dot_nt(grad_one, near)
            near = x1[a, pl.ds(pl.multiple_of((8 * g + 8) * C, C), 512), :384]
            acc[3 + a] += _dot_nt(grad_two, near)
        return carry

    lax.fori_loop(0, 4, stage_four, 0)

    rows = lax.broadcasted_iota(jnp.int32, (256, 512), 0) >> 5
    cols = lax.broadcasted_iota(jnp.int32, (256, 512), 1) >> 5
    delta = cols - rows - 4
    taps = []
    for layer in range(2):
        step = (s1, s2)[layer]
        for a in range(3):
            full = acc[3 * layer + a]
            for b in range(3):
                kept = jnp.where(delta == (b - 1) * step, full, 0.0)
                kept = jnp.sum(kept.reshape(8, C, 512), axis=0)
                kept = kept[:, :128] + kept[:, 128:256] + kept[:, 256:384] + kept[:, 384:]
                kept = kept + pltpu.roll(kept, 64, 1)
                taps.append(kept + pltpu.roll(kept, 32, 1))

    right = jnp.concatenate([rsum[...], jnp.zeros((C, 128), F32)], axis=1)
    right = pltpu.roll(right, first_diag, 1)
    both = jnp.concatenate(
        [jnp.concatenate([lsum[...], jnp.zeros((C, 256), F32)], axis=1), right], axis=0
    )
    high, rest = _split(both)
    proj = proj_ref[...]
    embed_ref[:, :640] = (_dot(proj, high) + _dot(proj, rest)).astype(BF)
    embed_ref[:, 640:] = jnp.zeros((256, 128), BF)
    emb = jnp.concatenate([emb_ref[...], embn_ref[...]], axis=1)
    none = jnp.zeros((2 * C, 640), BF)
    part = _dot_nt(emb, jnp.concatenate([none, high], axis=0)) + _dot_nt(
        emb, jnp.concatenate([none, rest], axis=0)
    )
    at = lax.broadcasted_iota(jnp.int32, (64, 128), 1)
    for t in range(8):
        value = jnp.where(at < 32, jnp.concatenate(taps[2 * t : 2 * t + 2], axis=0), 0.0)
        if t == 0:
            value = jnp.where(at < 32, value, jnp.concatenate(taps[16:], axis=0))
        if t < 4:
            value = jnp.where(at < 64, value, part[64 * t : 64 * t + 64])
        sums_ref[pl.ds(t, 64, stride=8), :] = value


def pair_field(total_bins, total_diags, scalars, own, nxt, prv, bias, limits, head, bands, proj, emb, embn):
    vmem = pl.BlockSpec(memory_space=pltpu.VMEM)
    return pl.pallas_call(
        functools.partial(pair_kernel, total_bins, total_diags),
        out_shape=(
            jax.ShapeDtypeStruct((32, 384), F32),
            jax.ShapeDtypeStruct((256, 768), BF),
            jax.ShapeDtypeStruct((512, 128), F32),
        ),
        in_specs=[pl.BlockSpec(memory_space=pltpu.SMEM)] + [vmem] * 10,
        out_specs=(vmem, vmem, vmem),
        scratch_shapes=[
            pltpu.VMEM((3, 64 * C, LN), BF),
            pltpu.VMEM((3, 56 * C, LN), BF),
            pltpu.VMEM((3, 48 * C, LN), BF),
            pltpu.VMEM((3, 40 * C, LN), BF),
            pltpu.VMEM((32 * C, 384), F32),
            pltpu.VMEM((56 * C, LN), F32),
            pltpu.VMEM((40 * C, 384), F32),
            pltpu.VMEM((64, 8, LN), F32),
            pltpu.VMEM((C, 640), F32),
            pltpu.VMEM((C, 256), F32),
            pltpu.VMEM((C, LN), F32),
            pltpu.VMEM((48, LN), F32),
            pltpu.VMEM((6, 256, 512), F32),
            pltpu.VMEM((C, 384), F32),
            pltpu.VMEM((C, LN), F32),
        ],
        compiler_params=pltpu.CompilerParams(vmem_limit_bytes=56 * 2**20),
        cost_estimate=pl.CostEstimate(
            flops=12 * 10**9, bytes_accessed=5 * 10**6, transcendentals=3 * 10**6
        ),
        name="pair_field",
    )(scalars, own, nxt, prv, bias, limits, head, bands, proj, emb, embn)


def on_device(
    embeddings, projection, dist_bias, conv_weight, head_weight, dilations, band_limit, cotangent
):
    bins = lax.axis_size("bin")
    diags = lax.axis_size("diag")
    diag_dev, rows_dev = cotangent.shape
    total_bins = rows_dev * bins
    total_diags = diag_dev * diags
    bin_at = lax.axis_index("bin")
    diag_at = lax.axis_index("diag")
    first_row = bin_at * rows_dev
    first_diag = diag_at * diag_dev

    bands = band_weights(dilations, conv_weight)
    bias = lax.dynamic_slice_in_dim(jnp.pad(dist_bias, ((0, 0), (M, M + 64))), first_diag, 128, 1)
    head = jnp.broadcast_to(head_weight[:, None], (C, LN))
    limits = jnp.broadcast_to(band_limit[None, :], (8, rows_dev))
    scalars = jnp.stack([first_row, first_diag, dilations[0], dilations[1]]).astype(jnp.int32)

    row_ids = first_row + jnp.arange(rows_dev, dtype=jnp.int32)[None, :]
    diag_ids = first_diag + jnp.arange(diag_dev, dtype=jnp.int32)[:, None]
    counted = (row_ids + diag_ids < total_bins) & (diag_ids < band_limit[None, :])
    cots = jnp.where(counted, cotangent, 0.0)
    cots_bf = cots.astype(BF)
    peer = jnp.arange(diags, dtype=jnp.int32)[:, None, None]
    edge = jnp.where(
        peer > diag_at, cots_bf[None, diag_dev - 8 :], cots_bf[None, :8]
    )
    own_rows = jnp.concatenate([embeddings, projection], axis=1)
    pack = jnp.concatenate(
        [
            jnp.broadcast_to(own_rows[None], (diags,) + own_rows.shape),
            jnp.pad(edge, ((0, 0), (0, 0), (0, projection.shape[1]))),
        ],
        axis=1,
    )
    got = lax.all_to_all(pack, "diag", 0, 0)
    features = diag_dev * diags
    emb_all = got[:, :diag_dev, :rows_dev].reshape(features, rows_dev)
    proj_all = got[:, :diag_dev, rows_dev:].reshape(features, -1)
    edges = got[:, diag_dev:, :rows_dev]
    before = lax.dynamic_index_in_dim(edges, jnp.maximum(diag_at - 1, 0), 0, False)
    after = lax.dynamic_index_in_dim(edges, jnp.minimum(diag_at + 1, diags - 1), 0, False)
    before = jnp.where(diag_at > 0, before.astype(F32), 0.0)
    after = jnp.where(diag_at < diags - 1, after.astype(F32), 0.0)
    projected = lax.dot_general(
        proj_all, emb_all, (((0,), (0,)), ((), ())), preferred_element_type=F32
    )
    own = jnp.concatenate([projected, before, cots, after], axis=0)

    up = [(i, i + 1) for i in range(bins - 1)]
    down = [(i + 1, i) for i in range(bins - 1)]
    nxt = lax.ppermute(own, "bin", down)
    prv = lax.ppermute(own[:, rows_dev - 128 :], "bin", up)
    embn = lax.ppermute(emb_all[:, :256], "bin", down)

    predicted, embed_parts, sums = pair_field(
        total_bins, total_diags, scalars, own, nxt, prv, bias, limits, head, bands,
        proj_all, emb_all, embn,
    )

    shares = lax.all_to_all(sums.reshape(bins, 512 // bins, 128), "bin", 0, 0)
    share = jnp.sum(shares, axis=0)
    high = share.astype(BF)
    rest = (share - high.astype(F32)).astype(BF)
    tail = jnp.pad(jnp.concatenate([high, rest], axis=0), ((0, diag_dev - 2 * share.shape[0]), (0, 0)))
    parts = embed_parts.reshape(diags, diag_dev, 768)
    parts = jnp.concatenate(
        [parts[:, :, :640], jnp.broadcast_to(tail[None], (diags,) + tail.shape)], axis=2
    )
    parts = lax.all_to_all(parts, "diag", 0, 0)
    total = jnp.sum(parts.astype(F32), axis=0)
    incoming = lax.ppermute(total[:, rows_dev:640].astype(BF), "bin", up)
    count = share.shape[0]
    whole = total[:count, 640:] + total[count : 2 * count, 640:]
    every = lax.all_to_all(
        jnp.broadcast_to(whole[None], (bins,) + whole.shape), "bin", 0, 0
    )
    grad_embed = total[:, :rows_dev] + jnp.pad(
        incoming.astype(F32), ((0, 0), (0, rows_dev - incoming.shape[1]))
    )
    scaling = 1.0 / math.sqrt(total_bins * total_diags)
    first16 = jnp.swapaxes(every[:, :, :C], 0, 1).reshape(16, C, C)
    last2 = every[:, 0, C : 2 * C].reshape(2, C, C)
    grad_conv = scaling * jnp.concatenate([first16, last2], axis=0).reshape(2, 9, C, C)
    proj_sum = jnp.swapaxes(every[:, :4, 2 * C :], 0, 1).reshape(features, 2 * C)
    grad_proj = scaling * lax.dynamic_slice_in_dim(proj_sum, first_diag, diag_dev, 0)
    return (predicted, grad_embed, grad_proj, grad_conv)


def solution(mesh):
    return jax.shard_map(
        on_device,
        mesh=mesh,
        in_specs=(
            P("diag", "bin"),
            P("diag", None),
            P(),
            P(),
            P(),
            P(),
            P("bin"),
            P("diag", "bin"),
        ),
        out_specs=(P("diag", "bin"), P("diag", "bin"), P("diag", None), P()),
        check_vma=False,
    )
```

time: 937 us -> 145 us (0.15)
  the two profiles are of different devices: /device:TPU:128 before, /device:TPU:8 now
where the time goes in v1:
time: 145 us; the launch traced here: 144 us
  Pallas kernels  41.8 us (29%)
  starting transfers between devices  40.5 us (28%)
  waiting for transfers between devices  29.5 us (20%)
  blocking collectives  17.8 us (12%)
  local copies, waits for them, and re-layouts  8.3 us (6%)
  other arithmetic  4.79 us (3%)
    pallas_call x1, Pallas kernels, pair_field(): pl.pallas_call(functools.partial(pair_kernel, total_bins, total_diags), o...  38.5 us
    all_to_all x1, blocking collectives, on_device(): parts = lax.all_to_all(parts, 'diag', 0, 0)  17.8 us
    all_to_all x1, waiting for transfers between devices, on_device(): got = lax.all_to_all(pack, 'diag', 0, 0)  12.7 us
    all_to_all x1, starting transfers between devices, on_device(): shares = lax.all_to_all(sums.reshape(bins, 512 // bins, 128), 'bin', 0, 0)  12.4 us
    all_to_all x1, starting transfers between devices, on_device(): got = lax.all_to_all(pack, 'diag', 0, 0)  10.4 us
    all_to_all x1, waiting for transfers between devices, on_device(): shares = lax.all_to_all(sums.reshape(bins, 512 // bins, 128), 'bin', 0, 0)  9.68 us
    all_to_all x1, starting transfers between devices, on_device(): lax.all_to_all(jnp.broadcast_to(whole[None], (bins,) + whole.shape), 'bin...  6.05 us
    all_to_all x1, waiting for transfers between devices, on_device(): lax.all_to_all(jnp.broadcast_to(whole[None], (bins,) + whole.shape), 'bin...  3.82 us
  transfers between devices with their start and end apart: 7, of which 4 were waited for; matrix products, arithmetic and copies ran while one was open for 3% of the time, Pallas kernels for 2%

profile of v1, /device:TPU:8, one launch (start us, length us, event | category | flops | bytes accessed | tf_op | source)
XLA Modules:
  0.0 144.0 jit_solution(158279684745497498)
XLA Ops:
  0.6 0.0 copy-start.1
  0.6 0.0 copy-start
  0.7 0.9 fusion.9
  1.6 0.8 pad_maximum_fusion.2
  2.4 0.1 broadcast_select_fusion
  2.5 0.8 fusion.1
  3.3 10.4 %all-to-all-start = ((bf16[8,40,448]{2,1,0:T(8,128)(2,1)}), bf16[8,40,448]{2,1,0:T(8,128)(2,1)S(1)}, u32[]{:S(2)}, u32[]{:S(2)}) async-start(bf16[8,40,448]{2,1,0:T(8,128)(2,1)} %fusion.1), calls=%async_computation | async-start | bytes 655360 | tf_op jit(solution)/shard_map/all_to_all | solution.py:327
  13.7 1.4 pad_dynamic-slice_fusion.bias_ref
  15.1 12.7 %all-to-all-done = bf16[8,40,448]{2,1,0:T(8,128)(2,1)S(1)} async-done(((bf16[8,40,448]{2,1,0:T(8,128)(2,1)}), bf16[8,40,448]{2,1,0:T(8,128)(2,1)S(1)}, u32[]{:S(2)}, u32[]{:S(2)}) %all-to-all-start) | async-done | bytes 286752 | tf_op jit(solution)/shard_map/all_to_all | solution.py:327
  27.9 0.0 copy-start.3
  27.9 2.5 %collective-permute-start.2 = (bf16[256,256]{1,0:T(8,128)(2,1)S(1)}, bf16[256,256]{1,0:T(8,128)(2,1)S(1)}, u32[]{:S(2)}, u32[]{:S(2)}) collective-permute-start(bf16[256,256]{1,0:T(8,128)(2,1)S(1)} %slice.70), channel_id=1, source_target_pairs={{8,0},{16,8},{24,16},{32,24},{40,32},{48,40},{56,48},{64,56},{72,6... | collective-permute-start | bytes 393224 | tf_op jit(solution)/shard_map/ppermute | solution.py:345
  30.4 0.2 convolution_bitcast_fusion
  30.6 0.0 copy-start.4
  30.6 3.3 %collective-permute-start = (f32[112,384]{1,0:T(8,128)S(1)}, f32[112,384]{1,0:T(8,128)S(1)}, u32[]{:S(2)}, u32[]{:S(2)}) collective-permute-start(f32[112,384]{1,0:T(8,128)S(1)} %pad_maximum_fusion.1.own_ref), channel_id=1, source_target_pairs={{8,0},{16,8},{24,16},{32,24},{40,32},{48,40},{56,48},{64,56},{72,6... | collective-permute-start | bytes 516104 | tf_op jit(solution)/shard_map/ppermute | solution.py:343
  33.9 0.6 pad_add_fusion.sc_ref
  34.5 0.1 copy.26
  34.7 2.6 %collective-permute-start.1 = (f32[112,128]{1,0:T(8,128)S(1)}, f32[112,128]{1,0:T(8,128)S(1)}, u32[]{:S(2)}, u32[]{:S(2)}) collective-permute-start(f32[112,128]{1,0:T(8,128)S(1)} %slice.69), channel_id=1, source_target_pairs={{0,8},{8,16},{16,24},{24,32},{32,40},{40,48},{48,56},{56,64},{64,7... | collective-permute-start | bytes 172040 | tf_op jit(solution)/shard_map/ppermute | solution.py:344
  37.3 3.4 %band_weights.1.t_ref = bf16[4,256,1536]{2,1,0:T(8,128)(2,1)S(1)} custom-call(s32[2]{0:T(128)S(1)} %copy-done.1, bf16[2,9,32,32]{3,2,1,0:T(8,128)(2,1)S(1)} %copy-done, bf16[2,9,32,32]{3,2,1,0:T(8,128)(2,1)S(1)} %bitcast.22), custom_call_target="tpu_custom_call" | custom-call | flops 1000000000 | bytes 4000000 | tf_op jit(solution)/shard_map/band_weights/pallas_call | solution.py:53
  40.6 1.6 %copy-done.2 = bf16[4,256,1536]{2,1,0:T(8,128)(2,1)} copy-done((bf16[4,256,1536]{2,1,0:T(8,128)(2,1)}, bf16[4,256,1536]{2,1,0:T(8,128)(2,1)S(1)}, u32[]{:S(2)}) %copy-start.2) | copy-done | bytes 3145752
  42.3 0.6 slice.66
  42.9 0.0 collective-permute-done.1.prev_ref
  42.9 0.0 collective-permute-done.2.embn_ref
  42.9 0.0 collective-permute-done.next_ref
  42.9 0.0 copy-done.5
  42.9 0.0 copy-start.7
  42.9 0.7 broadcast_in_dim.75.limit_ref
  43.6 0.7 broadcast_in_dim.76.head_ref
  44.3 38.5 %pair_field.1 = (f32[32,384]{1,0:T(8,128)}, bf16[256,768]{1,0:T(8,128)(2,1)}, f32[512,128]{1,0:T(8,128)}) custom-call(s32[4]{0:T(128)} %pad_add_fusion.sc_ref, f32[112,384]{1,0:T(8,128)} %copy-done.4, f32[112,384]{1,0:T(8,128)} %copy-done.7, f32[112,128]{1,0:T(8,128)} %copy-done.9, f32[32,128]{1,0:T(8,128)} %pad_dynamic-slice_fusion.bias_ref, ...), custom_call_target="tpu_custom_call" | custom-call | flops 12000000000 | bytes 5000000 | tf_op jit(solution)/shard_map/pair_field/pallas_call | solution.py:257
  82.8 12.4 %all-to-all-start.1 = ((f32[64,8,128]{2,1,0:T(8,128)}), f32[64,8,128]{2,1,0:T(8,128)S(1)}, u32[]{:S(2)}, u32[]{:S(2)}) async-start(f32[64,8,128]{2,1,0:T(8,128)} %bitcast.28), calls=%async_computation.1 | async-start | bytes 524288 | tf_op jit(solution)/shard_map/all_to_all | solution.py:352
  95.2 1.0 slice.71
  96.2 9.7 %all-to-all-done.1 = f32[64,8,128]{2,1,0:T(8,128)S(1)} async-done(((f32[64,8,128]{2,1,0:T(8,128)}), f32[64,8,128]{2,1,0:T(8,128)S(1)}, u32[]{:S(2)}, u32[]{:S(2)}) %all-to-all-start.1) | async-done | bytes 262176 | tf_op jit(solution)/shard_map/all_to_all | solution.py:352
  105.9 0.1 reduce_sum.18
  106.0 17.8 %all_to_all.20 = bf16[8,32,768]{2,1,0:T(8,128)(2,1)S(1)} all-to-all(bf16[8,32,768]{2,1,0:T(8,128)(2,1)S(1)} %pad_maximum_fusion), channel_id=1, replica_groups=mesh['bin'=64,'diag'=8] {'diag'}, dimensions={0} | all-to-all | bytes 786432 | tf_op jit(solution)/shard_map/all_to_all | solution.py:361
  123.8 0.1 convert_reduce_fusion
  123.9 0.7 broadcast_in_dim.78
  124.6 6.1 %all-to-all-start.3 = ((f32[64,8,128]{2,1,0:T(8,128)}), f32[64,8,128]{2,1,0:T(8,128)S(1)}, u32[]{:S(2)}, u32[]{:S(2)}) async-start(f32[64,8,128]{2,1,0:T(8,128)} %broadcast_in_dim.78), calls=%async_computation.3 | async-start | bytes 524288 | tf_op jit(solution)/shard_map/all_to_all | solution.py:366
  130.7 3.4 %collective-permute-start.3 = (bf16[32,256]{1,0:T(8,128)(2,1)S(1)}, bf16[32,256]{1,0:T(8,128)(2,1)S(1)}, u32[]{:S(2)}, u32[]{:S(2)}) collective-permute-start(bf16[32,256]{1,0:T(8,128)(2,1)S(1)} %slice.89), channel_id=1, source_target_pairs={{0,8},{8,16},{16,24},{24,32},{32,40},{40,48},{48,56},{56,64},{64,7... | collective-permute-start | bytes 49160 | tf_op jit(solution)/shard_map/ppermute | solution.py:363
  134.0 3.3 %collective-permute-done.3 = bf16[32,256]{1,0:T(8,128)(2,1)S(1)} collective-permute-done((bf16[32,256]{1,0:T(8,128)(2,1)S(1)}, bf16[32,256]{1,0:T(8,128)(2,1)S(1)}, u32[]{:S(2)}, u32[]{:S(2)}) %collective-permute-start.3) | collective-permute-done | bytes 16416 | tf_op jit(solution)/shard_map/ppermute | solution.py:363
  137.4 0.6 slice_add_fusion
  138.0 3.8 %all-to-all-done.3 = f32[64,8,128]{2,1,0:T(8,128)S(1)} async-done(((f32[64,8,128]{2,1,0:T(8,128)}), f32[64,8,128]{2,1,0:T(8,128)S(1)}, u32[]{:S(2)}, u32[]{:S(2)}) %all-to-all-start.3) | async-done | bytes 262176 | tf_op jit(solution)/shard_map/all_to_all | solution.py:366
  141.8 0.1 copy.31
  141.9 0.1 slice_bitcast_fusion.1
  142.0 0.1 copy.27
  142.2 0.1 reshape.63
  142.3 0.1 dynamic-slice_multiply_fusion
  142.4 0.7 copy.30
  143.1 0.1 slice.78
  143.2 0.8 maximum_multiply_fusion
  (31 shorter events, 0.2 us)
Async XLA Ops:
  0.6 33.3 %copy-start.1 = (s32[2]{0:T(128)S(1)}, s32[2]{0:T(128)}, u32[]{:S(2)}) copy-start(s32[2]{0:T(128)} %dil_ref.1) | copy-start | bytes 28
  0.6 33.9 %copy-start = (bf16[2,9,32,32]{3,2,1,0:T(8,128)(2,1)S(1)}, bf16[2,9,32,32]{3,2,1,0:T(8,128)(2,1)}, u32[]{:S(2)}) copy-start(bf16[2,9,32,32]{3,2,1,0:T(8,128)(2,1)} %w_ref.1) | copy-start | bytes 110596
  3.3 39.7 %copy-start.5 = (s32[384]{0:T(512)S(1)}, s32[384]{0:T(512)}, u32[]{:S(2)}) copy-start(s32[384]{0:T(512)} %param.14) | copy-start | bytes 4612
  3.3 40.3 %copy-start.6 = (f32[32]{0:T(128)S(1)}, f32[32]{0:T(128)}, u32[]{:S(2)}) copy-start(f32[32]{0:T(128)} %param.12) | copy-start | bytes 388
  3.3 24.6 %all-to-all-start = ((bf16[8,40,448]{2,1,0:T(8,128)(2,1)}), bf16[8,40,448]{2,1,0:T(8,128)(2,1)S(1)}, u32[]{:S(2)}, u32[]{:S(2)}) async-start(bf16[8,40,448]{2,1,0:T(8,128)(2,1)} %fusion.1), calls=%async_computation | async-start | bytes 655360 | tf_op jit(solution)/shard_map/all_to_all | solution.py:327
  27.9 16.4 %copy-start.3 = (bf16[8,32,384]{2,1,0:T(8,128)(2,1)}, bf16[8,32,384]{2,1,0:T(8,128)(2,1)S(1)}, u32[]{:S(2)}) copy-start(bf16[8,32,384]{2,1,0:T(8,128)(2,1)S(1)} %slice.67) | copy-start | bytes 589828
  27.9 15.0 %collective-permute-start.2 = (bf16[256,256]{1,0:T(8,128)(2,1)S(1)}, bf16[256,256]{1,0:T(8,128)(2,1)S(1)}, u32[]{:S(2)}, u32[]{:S(2)}) collective-permute-start(bf16[256,256]{1,0:T(8,128)(2,1)S(1)} %slice.70), channel_id=1, source_target_pairs={{8,0},{16,8},{24,16},{32,24},{40,32},{48,40},{56,48},{64,56},{72,6... | collective-permute-start | bytes 393224 | tf_op jit(solution)/shard_map/ppermute | solution.py:345
  30.6 13.7 %copy-start.4 = (f32[112,384]{1,0:T(8,128)}, f32[112,384]{1,0:T(8,128)S(1)}, u32[]{:S(2)}) copy-start(f32[112,384]{1,0:T(8,128)S(1)} %pad_maximum_fusion.1.own_ref) | copy-start | bytes 516100
  30.6 12.3 %collective-permute-start = (f32[112,384]{1,0:T(8,128)S(1)}, f32[112,384]{1,0:T(8,128)S(1)}, u32[]{:S(2)}, u32[]{:S(2)}) collective-permute-start(f32[112,384]{1,0:T(8,128)S(1)} %pad_maximum_fusion.1.own_ref), channel_id=1, source_target_pairs={{8,0},{16,8},{24,16},{32,24},{40,32},{48,40},{56,48},{64,56},{72,6... | collective-permute-start | bytes 516104 | tf_op jit(solution)/shard_map/ppermute | solution.py:343
  34.7 8.2 %collective-permute-start.1 = (f32[112,128]{1,0:T(8,128)S(1)}, f32[112,128]{1,0:T(8,128)S(1)}, u32[]{:S(2)}, u32[]{:S(2)}) collective-permute-start(f32[112,128]{1,0:T(8,128)S(1)} %slice.69), channel_id=1, source_target_pairs={{0,8},{8,16},{16,24},{24,32},{32,40},{40,48},{48,56},{56,64},{64,7... | collective-permute-start | bytes 172040 | tf_op jit(solution)/shard_map/ppermute | solution.py:344
  40.6 1.6 %copy-start.2 = (bf16[4,256,1536]{2,1,0:T(8,128)(2,1)}, bf16[4,256,1536]{2,1,0:T(8,128)(2,1)S(1)}, u32[]{:S(2)}) copy-start(bf16[4,256,1536]{2,1,0:T(8,128)(2,1)S(1)} %band_weights.1.t_ref) | copy-start | bytes 9437188
  42.9 1.4 copy-start.9
  42.9 1.4 copy-start.8
  42.9 1.4 copy-start.7
  82.8 23.1 %all-to-all-start.1 = ((f32[64,8,128]{2,1,0:T(8,128)}), f32[64,8,128]{2,1,0:T(8,128)S(1)}, u32[]{:S(2)}, u32[]{:S(2)}) async-start(f32[64,8,128]{2,1,0:T(8,128)} %bitcast.28), calls=%async_computation.1 | async-start | bytes 524288 | tf_op jit(solution)/shard_map/all_to_all | solution.py:352
  124.6 17.2 %all-to-all-start.3 = ((f32[64,8,128]{2,1,0:T(8,128)}), f32[64,8,128]{2,1,0:T(8,128)S(1)}, u32[]{:S(2)}, u32[]{:S(2)}) async-start(f32[64,8,128]{2,1,0:T(8,128)} %broadcast_in_dim.78), calls=%async_computation.3 | async-start | bytes 524288 | tf_op jit(solution)/shard_map/all_to_all | solution.py:366
  130.7 6.7 %collective-permute-start.3 = (bf16[32,256]{1,0:T(8,128)(2,1)S(1)}, bf16[32,256]{1,0:T(8,128)(2,1)S(1)}, u32[]{:S(2)}, u32[]{:S(2)}) collective-permute-start(bf16[32,256]{1,0:T(8,128)(2,1)S(1)} %slice.89), channel_id=1, source_target_pairs={{0,8},{8,16},{16,24},{24,32},{32,40},{40,48},{48,56},{56,64},{64,7... | collective-permute-start | bytes 49160 | tf_op jit(solution)/shard_map/ppermute | solution.py:363

commit v2 on v1

v2 whole, which is shorter than its diff:
```python
import functools
import math

import jax
import jax.numpy as jnp
from jax import lax
from jax.experimental import pallas as pl
from jax.experimental.pallas import tpu as pltpu
from jax.sharding import PartitionSpec as P

C = 32
M = 16
LN = 512
BF = jnp.bfloat16
F32 = jnp.float32


def _dot(a, b):
    return jnp.dot(a, b, preferred_element_type=F32)


def _dot_nt(a, b):
    return lax.dot_general(a, b, (((1,), (1,)), ((), ())), preferred_element_type=F32)


def _split(x):
    hi = x.astype(BF)
    return hi, (x - hi.astype(F32)).astype(BF)


def band_kernel(dil_ref, w_ref, wt_ref, t_ref):
    rows = lax.broadcasted_iota(jnp.int32, (256, 512), 0) >> 5
    cols = lax.broadcasted_iota(jnp.int32, (256, 512), 1) >> 5
    delta = cols - rows - 4
    spread = (
        (lax.broadcasted_iota(jnp.int32, (C, 512), 1) & 31)
        == lax.broadcasted_iota(jnp.int32, (C, 512), 0)
    ).astype(F32).astype(BF)
    for layer in range(2):
        masks = [delta == b * dil_ref[layer] for b in (-1, 0, 1)]
        for kind, ref in ((0, w_ref), (1, wt_ref)):
            for slot in range(3):
                total = jnp.zeros((256, 512), F32)
                for b in range(3):
                    along = slot if kind == 0 else 2 - slot
                    w = ref[layer, 3 * along + b]
                    wide = _dot(jnp.concatenate([w] * 8, axis=0), spread)
                    total = jnp.where(masks[b if kind == 0 else 2 - b], wide, total)
                t_ref[2 * kind + layer, :, slot * 512 : (slot + 1) * 512] = total.astype(BF)


def band_weights(dilations, conv_weight):
    return pl.pallas_call(
        band_kernel,
        out_shape=jax.ShapeDtypeStruct((4, 256, 1536), BF),
        in_specs=[
            pl.BlockSpec(memory_space=pltpu.SMEM),
            pl.BlockSpec(memory_space=pltpu.VMEM),
            pl.BlockSpec(memory_space=pltpu.VMEM),
        ],
        out_specs=pl.BlockSpec(memory_space=pltpu.VMEM),
        compiler_params=pltpu.CompilerParams(vmem_limit_bytes=32 * 2**20),
        cost_estimate=pl.CostEstimate(flops=10**9, bytes_accessed=4 * 10**6, transcendentals=0),
        name="band_weights",
    )(dilations, conv_weight, jnp.swapaxes(conv_weight, 2, 3))


def pair_kernel(
    total_bins, total_diags,
    sc_ref, own_ref, next_ref, prev_ref, bias_ref, limit_ref, head_ref, t_ref, emb_ref,
    pred_ref, both_ref, spill_ref, sums_ref,
    x0, x1, g2, g1, d0, d1, bk, mk, vbuf, ubuf, left, gwide, acc, lsum, rsum,
):
    first_row = sc_ref[0]
    first_diag = sc_ref[1]
    s1 = sc_ref[2]
    s2 = sc_ref[3]

    lane = lax.broadcasted_iota(jnp.int32, (8, LN), 1)
    low = lax.broadcasted_iota(jnp.int32, (C, 128), 1) < 64
    bin_id = first_row + jnp.where(lane < 448, lane, lane - LN)
    bin_ok = (bin_id >= 0) & (bin_id < total_bins)

    own = own_ref[...]
    prv = prev_ref[...]

    def rows_of(first, count, lanes):
        return next_ref[first : first + count, lanes].astype(F32)

    every, head_half, tail_half = slice(None), slice(0, 128), slice(128, 256)
    next_right = jnp.concatenate(
        [
            rows_of(0, C, every) + rows_of(C, C, every),
            rows_of(2 * C, C, head_half) + rows_of(2 * C, C, tail_half),
        ],
        axis=1,
    )
    next_left = rows_of(3 * C, C, head_half) + rows_of(3 * C, C, tail_half)
    next_cots = rows_of(4 * C, 48, head_half)
    left[:, :384] = own[:C]
    left[:, 384:] = jnp.where(low, next_left, prv[:C])
    low48 = lax.broadcasted_iota(jnp.int32, (48, 128), 1) < 64
    gwide[:, :384] = own[2 * C :]
    gwide[:, 384:] = jnp.where(low48, next_cots, prv[2 * C :])
    line = jnp.concatenate([prv[C : 2 * C], own[C : 2 * C], next_right], axis=1)
    vbuf[...] = pltpu.roll(line, 784 - first_diag, 1)[:, :512]
    ubuf[...] = pltpu.roll(line, lax.rem(912 - first_diag, 896), 1)[:, :256]

    at = lax.broadcasted_iota(jnp.int32, (C, 128), 1)

    def columns(value):
        return [value[:, 128 * i : 128 * i + 128] for i in range(value.shape[1] // 128)]

    def store3(ref, row, value, shift):
        cols = columns(value.astype(BF))
        later = [pltpu.roll(v, shift, 1) for v in cols]
        sooner = [pltpu.roll(v, 128 - shift, 1) for v in cols]
        ref[1, pl.ds(row, C), :] = value.astype(BF)
        for i in range(4):
            here = pl.ds(128 * i, 128)
            ref[0, pl.ds(row, C), here] = jnp.where(at < shift, later[i - 1], later[i])
            ref[2, pl.ds(row, C), here] = jnp.where(
                at < 128 - shift, sooner[i], sooner[(i + 1) % 4]
            )

    def times(value, mask):
        return (value.reshape(4, 8, value.shape[1]) * mask[None]).reshape(value.shape)

    def stage_zero(g):
        for r in range(8):
            k = 8 * g + r
            diag_id = first_diag - M + k
            ok = bin_ok & (bin_id + diag_id < total_bins) & (diag_id >= 0) & (diag_id < total_diags)
            mask = ok.astype(F32)
            mk[k] = mask
            by = (128 - k) % 128
            v = [pltpu.roll(vbuf[:, 128 * i : 128 * i + 128], by, 1) for i in range(4)]
            u = [pltpu.roll(ubuf[:, 128 * i : 128 * i + 128], by, 1) for i in range(2)]
            here = at < 128 - k
            shifted = jnp.concatenate(
                [jnp.where(here, v[i], v[i + 1]) for i in range(3)]
                + [jnp.where(low, v[3], jnp.where(here, u[0], u[1]))],
                axis=1,
            )
            t = jnp.tanh(left[...] + shifted + bias_ref[:, k : k + 1])
            row = k * C
            store3(x0, row, times(t, mask), s1)
            d0[pl.ds(row, C), :] = times(1.0 - t[:, :384] * t[:, :384], mask[:, :384])


    def window(ref, first, width):
        rows = pl.ds(first * C, 512)
        return jnp.concatenate([ref[a, rows, :width] for a in range(3)], axis=0)

    def stage_one(g):
        t1 = jnp.tanh(_dot(t_ref[0], window(x0, 8 * g, LN)))
        for r in range(8):
            k = 4 + 8 * g + r
            mask = mk[k]
            t = t1[r * C : (r + 1) * C]
            base = x0[1, pl.ds(k * C, C), :].astype(F32)
            store3(x1, (k - 4) * C, times(base + t, mask), s2)
            d1[pl.ds((k - 4) * C, C), :] = times(1.0 - t * t, mask)


    head = jnp.broadcast_to(head_ref[...], (C, LN))
    limits = limit_ref[...]
    own_bin = first_row + lax.broadcasted_iota(jnp.int32, (8, 384), 1)
    own_row = lax.broadcasted_iota(jnp.int32, (8, 384), 0)

    def stage_two(g):
        t2 = jnp.tanh(_dot(t_ref[1], window(x1, 8 * g, LN)))
        cots = gwide[pl.ds(8 * g, 8), :]
        lines = []
        for r in range(8):
            k = 8 + 8 * g + r
            t = t2[r * C : (r + 1) * C]
            value = cots[r : r + 1] * (head * (1.0 - t * t))
            store3(g2, (k - 8) * C, value, s2)
            lines.append(jnp.sum(head[:, :384] * t[:, :384], axis=0, keepdims=True))

        if 1 <= g < 5:
            diag_id = first_diag + 8 * (g - 1) + own_row
            ok = (own_bin + diag_id < total_bins) & (diag_id < limits)
            pred_ref[pl.ds(8 * (g - 1), 8), :] = jnp.where(
                ok, jnp.concatenate(lines, axis=0), 0.0
            )


    def stage_three(g):
        back = _dot(t_ref[3], window(g2, 8 * g, LN))
        for r in range(8):
            k = 12 + 8 * g + r
            value = back[r * C : (r + 1) * C]
            at = (k - 12) * C
            store3(g1, at, value * d1[pl.ds((k - 4) * C, C), :], s1)
            bk[pl.ds(at, C), :] = times(value, mk[k])[:, :384]


    lsum[...] = jnp.zeros_like(lsum)
    rsum[...] = jnp.zeros_like(rsum)
    acc[...] = jnp.zeros_like(acc)

    def stage_four(g):
        back = _dot(t_ref[2], window(g1, 8 * g, 384))
        part = jnp.zeros((C, 384), F32)
        skew = jnp.zeros((C, LN), F32)
        for r in range(8):
            kk = 8 * g + r
            value = back[r * C : (r + 1) * C] + bk[pl.ds((kk + 4) * C, C), :]
            value = value * d0[pl.ds((kk + M) * C, C), :]
            part = part + value
            wide = jnp.concatenate([value, jnp.zeros((C, 128), F32)], axis=1)
            skew = skew + (pltpu.roll(wide, r, 1) if r else wide)
        lsum[...] += part
        rsum[...] += pltpu.roll(skew, 8 * g, 1)
        grad_two = g2[1, pl.ds((8 * g + 8) * C, 256), :384]
        grad_one = g1[1, pl.ds((8 * g + 4) * C, 256), :384]
        for a in range(3):
            near = x0[a, pl.ds((8 * g + 12) * C, 512), :384]
            acc[a] += _dot_nt(grad_one, near)
            near = x1[a, pl.ds((8 * g + 8) * C, 512), :384]
            acc[3 + a] += _dot_nt(grad_two, near)


    stages = ((stage_zero, 8), (stage_one, 7), (stage_two, 6), (stage_three, 5), (stage_four, 4))
    for stage, groups in stages:
        for g in range(groups):
            stage(g)

    rows = lax.broadcasted_iota(jnp.int32, (256, 512), 0) >> 5
    cols = lax.broadcasted_iota(jnp.int32, (256, 512), 1) >> 5
    delta = cols - rows - 4
    taps = []
    for layer in range(2):
        step = (s1, s2)[layer]
        for a in range(3):
            full = acc[3 * layer + a]
            for b in range(3):
                kept = jnp.where(delta == (b - 1) * step, full, 0.0)
                kept = jnp.sum(kept.reshape(8, C, 512), axis=0)
                kept = kept[:, :128] + kept[:, 128:256] + kept[:, 256:384] + kept[:, 384:]
                kept = kept + pltpu.roll(kept, 64, 1)
                taps.append(kept + pltpu.roll(kept, 32, 1))

    right = jnp.concatenate([rsum[...], jnp.zeros((C, 128), F32)], axis=1)
    right = pltpu.roll(right, first_diag, 1)
    both_ref[:C] = lsum[...]
    both_ref[C:] = right[:, :384]
    spill_ref[...] = right[:, 384:].astype(BF)
    both = jnp.concatenate(
        [jnp.concatenate([lsum[...], jnp.zeros((C, 256), F32)], axis=1), right], axis=0
    )
    none = jnp.zeros((2 * C, 640), BF)
    high, rest = _split(both)
    emb = jnp.concatenate([emb_ref[...], next_ref[4 * C + 48 :]], axis=1)
    part = _dot_nt(emb, jnp.concatenate([none, high], axis=0)) + _dot_nt(
        emb, jnp.concatenate([none, rest], axis=0)
    )
    for t in range(16):
        value = jnp.where(at < 32, taps[t], 0.0)
        if t < 2:
            value = jnp.where(at < 32, value, taps[16 + t])
        if t < 8:
            value = jnp.where(at < 64, value, part[C * t : C * t + C])
        sums_ref[C * t : C * t + C] = value


def pair_field(total_bins, total_diags, *operands):
    vmem = pl.BlockSpec(memory_space=pltpu.VMEM)
    return pl.pallas_call(
        functools.partial(pair_kernel, total_bins, total_diags),
        out_shape=(
            jax.ShapeDtypeStruct((32, 384), F32),
            jax.ShapeDtypeStruct((2 * C, 384), F32),
            jax.ShapeDtypeStruct((C, 256), BF),
            jax.ShapeDtypeStruct((512, 128), F32),
        ),
        in_specs=[pl.BlockSpec(memory_space=pltpu.SMEM)] + [vmem] * 8,
        out_specs=(vmem,) * 4,
        scratch_shapes=[
            pltpu.VMEM((3, 64 * C, LN), BF),
            pltpu.VMEM((3, 56 * C, LN), BF),
            pltpu.VMEM((3, 48 * C, LN), BF),
            pltpu.VMEM((3, 40 * C, LN), BF),
            pltpu.VMEM((64 * C, 384), F32),
            pltpu.VMEM((56 * C, LN), F32),
            pltpu.VMEM((40 * C, 384), F32),
            pltpu.VMEM((64, 8, LN), F32),
            pltpu.VMEM((C, 512), F32),
            pltpu.VMEM((C, 256), F32),
            pltpu.VMEM((C, LN), F32),
            pltpu.VMEM((48, LN), F32),
            pltpu.VMEM((6, 256, 512), F32),
            pltpu.VMEM((C, 384), F32),
            pltpu.VMEM((C, LN), F32),
        ],
        compiler_params=pltpu.CompilerParams(vmem_limit_bytes=56 * 2**20),
        cost_estimate=pl.CostEstimate(
            flops=12 * 10**9, bytes_accessed=5 * 10**6, transcendentals=3 * 10**6
        ),
        name="pair_field",
    )(*operands)


def on_device(
    embeddings, projection, dist_bias, conv_weight, head_weight, dilations, band_limit, cotangent
):
    bins = lax.axis_size("bin")
    diags = lax.axis_size("diag")
    diag_dev, rows_dev = cotangent.shape
    total_bins = rows_dev * bins
    total_diags = diag_dev * diags
    bin_at = lax.axis_index("bin")
    diag_at = lax.axis_index("diag")
    first_row = bin_at * rows_dev
    first_diag = diag_at * diag_dev

    bands = band_weights(dilations, conv_weight)
    bias = lax.dynamic_slice_in_dim(jnp.pad(dist_bias, ((0, 0), (M, M + 64))), first_diag, 128, 1)
    scalars = jnp.stack([first_row, first_diag, dilations[0], dilations[1]]).astype(jnp.int32)

    row_ids = first_row + jnp.arange(rows_dev, dtype=jnp.int32)[None, :]
    diag_ids = first_diag + jnp.arange(diag_dev, dtype=jnp.int32)[:, None]
    counted = (row_ids + diag_ids < total_bins) & (diag_ids < band_limit[None, :])
    cots = jnp.where(counted, cotangent, 0.0)
    cots_bf = cots.astype(BF)
    peer = jnp.arange(diags, dtype=jnp.int32)[:, None, None]
    edge = jnp.where(
        peer > diag_at, cots_bf[None, diag_dev - 8 :], cots_bf[None, :8]
    )
    columns = projection.shape[1]
    quarter = diag_dev // 4
    flat = jnp.concatenate([projection[quarter * i : quarter * (i + 1)] for i in range(4)], axis=1)
    flat = jnp.pad(flat, ((0, 0), (0, rows_dev - 4 * columns)))
    pack = jnp.concatenate(
        [
            jnp.broadcast_to(embeddings[None], (diags,) + embeddings.shape),
            edge,
            jnp.broadcast_to(flat[None], (diags,) + flat.shape),
        ],
        axis=1,
    )
    got = lax.all_to_all(pack, "diag", 0, 0)
    got, bands, bias = lax.optimization_barrier((got, bands, bias))
    features = diag_dev * diags
    emb_all = got[:, :diag_dev].reshape(features, rows_dev)
    flat = got[:, diag_dev + 8 :]
    proj_all = jnp.concatenate(
        [flat[:, :, columns * i : columns * (i + 1)] for i in range(4)], axis=1
    ).reshape(features, columns)
    edges = got[:, diag_dev : diag_dev + 8]
    before = lax.dynamic_index_in_dim(edges, jnp.maximum(diag_at - 1, 0), 0, False)
    after = lax.dynamic_index_in_dim(edges, jnp.minimum(diag_at + 1, diags - 1), 0, False)
    before = jnp.where(diag_at > 0, before.astype(F32), 0.0)
    after = jnp.where(diag_at < diags - 1, after.astype(F32), 0.0)
    projected = lax.dot_general(
        proj_all, emb_all, (((0,), (0,)), ((), ())), preferred_element_type=F32
    )
    own = jnp.concatenate([projected, before, cots, after], axis=0)

    up = [(i, i + 1) for i in range(bins - 1)]
    down = [(i + 1, i) for i in range(bins - 1)]
    high, rest = _split(projected)
    first = jnp.concatenate(
        [
            high[C:, :256],
            rest[C:, :256],
            jnp.concatenate([high[C:, 256:], rest[C:, 256:]], axis=1),
            jnp.concatenate([high[:C, :128], rest[:C, :128]], axis=1),
            own[2 * C :, :256].astype(BF),
            emb_all[:, :256],
        ],
        axis=0,
    )
    nxt = lax.ppermute(first, "bin", down)
    prv = lax.ppermute(own[:, rows_dev - 128 :], "bin", up)

    predicted, both, spill, sums = pair_field(
        total_bins, total_diags, scalars, own, nxt, prv, bias, band_limit[None, :],
        head_weight[:, None], bands, emb_all,
    )

    spill = lax.ppermute(spill, "bin", up)
    shares = lax.all_to_all(sums.reshape(bins, 512 // bins, 128), "bin", 0, 0)
    both = both + jnp.pad(spill.astype(F32), ((C, 0), (0, rows_dev - spill.shape[1])))
    high, rest = _split(both)
    parts = _dot(
        jnp.concatenate([proj_all, proj_all], axis=1), jnp.concatenate([high, rest], axis=0)
    ).astype(BF).reshape(diags, diag_dev, rows_dev)
    share = jnp.sum(shares, axis=0)
    high, rest = _split(share)
    count = share.shape[0]
    tail = jnp.pad(jnp.concatenate([high, rest], axis=0), ((0, diag_dev - 2 * count), (0, 0)))
    parts = jnp.concatenate(
        [parts, jnp.broadcast_to(tail[None], (diags,) + tail.shape)], axis=2
    )
    total = jnp.sum(lax.all_to_all(parts, "diag", 0, 0).astype(F32), axis=0)
    grad_embed = total[:, :rows_dev]
    whole = total[:count, rows_dev:] + total[count : 2 * count, rows_dev:]
    every = lax.all_to_all(
        jnp.broadcast_to(whole[None], (bins,) + whole.shape), "bin", 0, 0
    ).reshape(bins * count, 128)
    scaling = 1.0 / math.sqrt(total_bins * total_diags)
    grad_conv = scaling * jnp.concatenate(
        [every[:, :C].reshape(16, C, C), every[: 2 * C, C : 2 * C].reshape(2, C, C)], axis=0
    ).reshape(2, 9, C, C)
    grad_proj = scaling * lax.dynamic_slice(
        every, (first_diag, 2 * C), (diag_dev, 2 * C)
    )
    return (predicted, grad_embed, grad_proj, grad_conv)


def solution(mesh):
    return jax.shard_map(
        on_device,
        mesh=mesh,
        in_specs=(
            P("diag", "bin"),
            P("diag", None),
            P(),
            P(),
            P(),
            P(),
            P("bin"),
            P("diag", "bin"),
        ),
        out_specs=(P("diag", "bin"), P("diag", "bin"), P("diag", None), P()),
        check_vma=False,
    )
```

time: 145 us -> 121 us (0.83)
  Pallas kernels: 41.8 us -> 21.2 us
  waiting for transfers between devices: 29.5 us -> 24.3 us
  local copies, waits for them, and re-layouts: 8.3 us -> 11.9 us
  starting transfers between devices: 40.5 us -> 38.5 us
    pallas_call x1, Pallas kernels: 38.5 us -> 17.8 us  [pair_field(): pl.pallas_call(functools.partial(pair_kernel, total_bins, total_diags), o...]
    all_to_all x1, waiting for transfers between devices: 12.7 us -> 2.54 us  [on_device(): got = lax.all_to_all(pack, 'diag', 0, 0)]
    all_to_all x1, waiting for transfers between devices: 3.82 us -> 11.3 us  [on_device(): lax.all_to_all(jnp.broadcast_to(whole[None], (bins,) + whole.shape), 'bin...]
    all_to_all x1, waiting for transfers between devices: 9.68 us -> 3.92 us  [on_device(): shares = lax.all_to_all(sums.reshape(bins, 512 // bins, 128), 'bin', 0, 0)]
    ppermute x3 -> x2, starting transfers between devices: 9.1 us -> 5.83 us  [the longest x1 3.37 us: on_device(): spill = lax.ppermute(spill, 'bin', up)]
    unnamed x22 -> x21, local copies, waits for them, and re-layouts: 2.49 us -> 5.56 us
    ppermute x1, waiting for transfers between devices: 0.01 us -> 2.79 us  [on_device(): prv = lax.ppermute(own[:, rows_dev - 128:], 'bin', up)]
    broadcast_in_dim x3 -> x4, local copies, waits for them, and re-layouts: 1.38 us -> 3.37 us  [the longest x1 1.34 us: on_device(): head_weight[:, None]]
  transfers between devices with their start and end apart: 7 -> 6, of which waited for: 4 -> 5; matrix products, arithmetic and copies ran while one was open for 3% -> 6% of each run, Pallas kernels for 2% -> 3%
where the time goes in v2:
time: 121 us; the launch traced here: 120 us
  starting transfers between devices  38.5 us (32%)
  waiting for transfers between devices  24.3 us (20%)
  Pallas kernels  21.2 us (18%)
  blocking collectives  18.1 us (15%)
  local copies, waits for them, and re-layouts  11.9 us (10%)
  other arithmetic  4.96 us (4%)
    all_to_all x1, blocking collectives, on_device(): total = jnp.sum(lax.all_to_all(parts, 'diag', 0, 0).astype(F32), axis=0)  18.1 us
    pallas_call x1, Pallas kernels, pair_field(): pl.pallas_call(functools.partial(pair_kernel, total_bins, total_diags), o...  17.8 us
    all_to_all x1, starting transfers between devices, on_device(): shares = lax.all_to_all(sums.reshape(bins, 512 // bins, 128), 'bin', 0, 0)  12.2 us
    all_to_all x1, waiting for transfers between devices, on_device(): lax.all_to_all(jnp.broadcast_to(whole[None], (bins,) + whole.shape), 'bin...  11.3 us
    all_to_all x1, starting transfers between devices, on_device(): got = lax.all_to_all(pack, 'diag', 0, 0)  10.3 us
    all_to_all x1, starting transfers between devices, on_device(): lax.all_to_all(jnp.broadcast_to(whole[None], (bins,) + whole.shape), 'bin...  6.58 us
    unnamed x21, local copies, waits for them, and re-layouts  5.56 us
    all_to_all x1, waiting for transfers between devices, on_device(): shares = lax.all_to_all(sums.reshape(bins, 512 // bins, 128), 'bin', 0, 0)  3.92 us
  transfers between devices with their start and end apart: 6, of which 5 were waited for; matrix products, arithmetic and copies ran while one was open for 6% of the time, Pallas kernels for 3%

profile of v2, /device:TPU:8, one launch (start us, length us, event | category | flops | bytes accessed | tf_op | source)
XLA Modules:
  0.0 120.3 jit_solution(6930438226158427700)
XLA Ops:
  0.6 0.0 copy-start.6
  0.7 0.7 fusion.30
  1.4 0.9 fusion.24
  2.3 0.1 broadcast_select_fusion
  2.4 0.1 fusion.19
  2.5 0.8 broadcast_in_dim.45
  3.3 0.7 pad_maximum_fusion
  4.0 10.3 %all-to-all-start = ((bf16[8,48,384]{2,1,0:T(8,128)(2,1)}), bf16[8,48,384]{2,1,0:T(8,128)(2,1)S(1)}, u32[]{:S(2)}, u32[]{:S(2)}) async-start(bf16[8,48,384]{2,1,0:T(8,128)(2,1)} %pad_maximum_fusion), calls=%async_computation | async-start | bytes 589824 | tf_op jit(solution)/shard_map/all_to_all | solution.py:344
  14.3 1.3 %broadcast_in_dim.76.limit_ref = s32[1,384]{1,0:T(1,128)} reshape(s32[384]{0:T(512)} %param.14) | data formatting | bytes 3072 | tf_op jit(solution)/shard_map/broadcast_in_dim | solution.py:325
  15.6 1.3 %copy.13.head_ref = f32[32,1]{1,0:T(8,128)} copy(f32[32,1]{0,1:T(1,128)} %bitcast.34) | data formatting | bytes 256 | tf_op jit(solution)/shard_map/broadcast_in_dim | solution.py:381
  16.9 1.0 copy.12
  18.0 0.0 copy-start
  18.0 0.9 copy-done
  18.9 0.7 copy-done.1
  19.5 3.3 %band_weights.1.t_ref = bf16[4,256,1536]{2,1,0:T(8,128)(2,1)S(1)} custom-call(s32[2]{0:T(128)S(1)} %copy-done.1, bf16[2,9,32,32]{3,2,1,0:T(8,128)(2,1)S(1)} %copy-done, bf16[2,9,32,32]{3,2,1,0:T(8,128)(2,1)S(1)} %bitcast.23), custom_call_target="tpu_custom_call" | custom-call | flops 1000000000 | bytes 4000000 | tf_op jit(solution)/shard_map/band_weights/pallas_call | solution.py:53
  22.9 0.0 copy-start.3
  22.9 1.6 %copy-done.3 = bf16[4,256,1536]{2,1,0:T(8,128)(2,1)} copy-done((bf16[4,256,1536]{2,1,0:T(8,128)(2,1)}, bf16[4,256,1536]{2,1,0:T(8,128)(2,1)S(1)}, u32[]{:S(2)}) %copy-start.3) | copy-done | bytes 3145752
  24.5 0.0 copy-done.6
  24.5 0.7 pad_dynamic-slice_fusion.bias_ref
  25.2 2.5 %all-to-all-done = bf16[8,48,384]{2,1,0:T(8,128)(2,1)S(1)} async-done(((bf16[8,48,384]{2,1,0:T(8,128)(2,1)}), bf16[8,48,384]{2,1,0:T(8,128)(2,1)S(1)}, u32[]{:S(2)}, u32[]{:S(2)}) %all-to-all-start) | async-done | bytes 294944 | tf_op jit(solution)/shard_map/all_to_all | solution.py:344
  27.8 0.1 fusion.26
  27.9 0.0 copy-start.4
  27.9 0.2 subtract_convert_fusion.1
  28.2 2.5 %collective-permute-start = (bf16[432,256]{1,0:T(8,128)(2,1)S(1)}, bf16[432,256]{1,0:T(8,128)(2,1)S(1)}, u32[]{:S(2)}, u32[]{:S(2)}) collective-permute-start(bf16[432,256]{1,0:T(8,128)(2,1)S(1)} %slice_dynamic-update-slice_fusion), channel_id=1, source_target_pairs={{8,0},{16,8},{24,16},{32,24},{40,32},{48,40},{56,48},{64,56},{72,6... | collective-permute-start | bytes 663560 | tf_op jit(solution)/shard_map/ppermute | solution.py:376
  30.7 0.0 copy-start.5
  30.7 3.6 %collective-permute-start.1 = (f32[112,128]{1,0:T(8,128)S(1)}, f32[112,128]{1,0:T(8,128)S(1)}, u32[]{:S(2)}, u32[]{:S(2)}) collective-permute-start(f32[112,128]{1,0:T(8,128)S(1)} %slice.123), channel_id=1, source_target_pairs={{0,8},{8,16},{16,24},{24,32},{32,40},{40,48},{48,56},{56,64},{64,7... | collective-permute-start | bytes 172040 | tf_op jit(solution)/shard_map/ppermute | solution.py:377
  34.3 0.6 pad_add_fusion.sc_ref
  34.9 2.8 %collective-permute-done.1.prev_ref = f32[112,128]{1,0:T(8,128)S(1)} collective-permute-done((f32[112,128]{1,0:T(8,128)S(1)}, f32[112,128]{1,0:T(8,128)S(1)}, u32[]{:S(2)}, u32[]{:S(2)}) %collective-permute-start.1) | collective-permute-done | bytes 57376 | tf_op jit(solution)/shard_map/ppermute | solution.py:377
  37.7 0.0 collective-permute-done.next_ref
  37.7 0.0 copy-done.4
  37.7 0.6 copy-done.8
  38.3 0.7 copy-done.7
  39.0 17.8 %pair_field.1 = (f32[32,384]{1,0:T(8,128)}, f32[64,384]{1,0:T(8,128)}, bf16[32,256]{1,0:T(8,128)(2,1)}, f32[512,128]{1,0:T(8,128)}) custom-call(s32[4]{0:T(128)} %pad_add_fusion.sc_ref, f32[112,384]{1,0:T(8,128)} %copy-done.5, bf16[432,256]{1,0:T(8,128)(2,1)} %copy-done.7, f32[112,128]{1,0:T(8,128)} %copy-done.8, f32[32,128]{1,0:T(8,128)} %pad_dynamic-slice_fusion.bias_ref, ...), custom_call_target="tpu_custom_call" | custom-call | flops 12000000000 | bytes 5000000 | tf_op jit(solution)/shard_map/pair_field/pallas_call | solution.py:271
  56.8 12.2 %all-to-all-start.1 = ((f32[64,8,128]{2,1,0:T(8,128)}), f32[64,8,128]{2,1,0:T(8,128)S(1)}, u32[]{:S(2)}, u32[]{:S(2)}) async-start(f32[64,8,128]{2,1,0:T(8,128)} %bitcast.31), calls=%async_computation.1 | async-start | bytes 524288 | tf_op jit(solution)/shard_map/all_to_all | solution.py:385
  69.0 3.4 %collective-permute-start.2 = (bf16[32,256]{1,0:T(8,128)(2,1)}, bf16[32,256]{1,0:T(8,128)(2,1)S(1)}, u32[]{:S(2)}, u32[]{:S(2)}) collective-permute-start(bf16[32,256]{1,0:T(8,128)(2,1)} %get-tuple-element.16), channel_id=1, source_target_pairs={{0,8},{8,16},{16,24},{24,32},{32,40},{40,48},{48,56},{56,64},{64,7... | collective-permute-start | bytes 49160 | tf_op jit(solution)/shard_map/ppermute | solution.py:384
  72.4 3.7 %collective-permute-done.2 = bf16[32,256]{1,0:T(8,128)(2,1)S(1)} collective-permute-done((bf16[32,256]{1,0:T(8,128)(2,1)}, bf16[32,256]{1,0:T(8,128)(2,1)S(1)}, u32[]{:S(2)}, u32[]{:S(2)}) %collective-permute-start.2) | collective-permute-done | bytes 16416 | tf_op jit(solution)/shard_map/ppermute | solution.py:384
  76.2 0.9 fusion.3
  77.1 0.3 convolution_convert_fusion
  77.3 3.9 %all-to-all-done.1 = f32[64,8,128]{2,1,0:T(8,128)S(1)} async-done(((f32[64,8,128]{2,1,0:T(8,128)}), f32[64,8,128]{2,1,0:T(8,128)S(1)}, u32[]{:S(2)}, u32[]{:S(2)}) %all-to-all-start.1) | async-done | bytes 262176 | tf_op jit(solution)/shard_map/all_to_all | solution.py:385
  81.3 0.1 reduce_sum.18
  81.4 18.1 %all_to_all.20 = bf16[8,32,512]{2,1,0:T(8,128)(2,1)S(1)} all-to-all(bf16[8,32,512]{2,1,0:T(8,128)(2,1)S(1)} %pad_maximum_fusion.1), channel_id=1, replica_groups=mesh['bin'=64,'diag'=8] {'diag'}, dimensions={0} | all-to-all | bytes 524288 | tf_op jit(solution)/shard_map/all_to_all | solution.py:398
  99.5 0.7 broadcast_in_dim.79
  100.3 6.6 %all-to-all-start.3 = ((f32[64,8,128]{2,1,0:T(8,128)}), f32[64,8,128]{2,1,0:T(8,128)S(1)}, u32[]{:S(2)}, u32[]{:S(2)}) async-start(f32[64,8,128]{2,1,0:T(8,128)} %broadcast_in_dim.79), calls=%async_computation.3 | async-start | bytes 524288 | tf_op jit(solution)/shard_map/all_to_all | solution.py:401
  106.8 0.6 slice.124
  107.5 11.3 %all-to-all-done.3 = f32[64,8,128]{2,1,0:T(8,128)S(1)} async-done(((f32[64,8,128]{2,1,0:T(8,128)}), f32[64,8,128]{2,1,0:T(8,128)S(1)}, u32[]{:S(2)}, u32[]{:S(2)}) %all-to-all-start.3) | async-done | bytes 262176 | tf_op jit(solution)/shard_map/all_to_all | solution.py:401
  118.8 0.1 slice.128
  118.9 0.7 dynamic-slice_multiply_fusion
  119.6 0.8 maximum_multiply_fusion
  (30 shorter events, 0.3 us)
Async XLA Ops:
  0.6 23.9 %copy-start.6 = (f32[32,256]{1,0:T(8,128)S(1)}, f32[32,256]{1,0:T(8,128)}, u32[]{:S(2)}) copy-start(f32[32,256]{1,0:T(8,128)} %param.10) | copy-start | bytes 98308
  4.0 23.8 %all-to-all-start = ((bf16[8,48,384]{2,1,0:T(8,128)(2,1)}), bf16[8,48,384]{2,1,0:T(8,128)(2,1)S(1)}, u32[]{:S(2)}, u32[]{:S(2)}) async-start(bf16[8,48,384]{2,1,0:T(8,128)(2,1)} %pad_maximum_fusion), calls=%async_computation | async-start | bytes 589824 | tf_op jit(solution)/shard_map/all_to_all | solution.py:344
  14.3 20.0 %copy-start.2 = (s32[2]{0:T(128)S(1)}, s32[2]{0:T(128)}, u32[]{:S(2)}) copy-start(s32[2]{0:T(128)} %dil_ref.1) | copy-start | bytes 28
  18.0 0.9 copy-start
  18.9 0.7 copy-start.1
  22.9 1.6 %copy-start.3 = (bf16[4,256,1536]{2,1,0:T(8,128)(2,1)}, bf16[4,256,1536]{2,1,0:T(8,128)(2,1)S(1)}, u32[]{:S(2)}) copy-start(bf16[4,256,1536]{2,1,0:T(8,128)(2,1)S(1)} %band_weights.1.t_ref) | copy-start | bytes 9437188
  27.9 9.8 %copy-start.4 = (bf16[8,32,384]{2,1,0:T(8,128)(2,1)}, bf16[8,32,384]{2,1,0:T(8,128)(2,1)S(1)}, u32[]{:S(2)}) copy-start(bf16[8,32,384]{2,1,0:T(8,128)(2,1)S(1)} %slice.98) | copy-start | bytes 589828
  28.2 9.5 %collective-permute-start = (bf16[432,256]{1,0:T(8,128)(2,1)S(1)}, bf16[432,256]{1,0:T(8,128)(2,1)S(1)}, u32[]{:S(2)}, u32[]{:S(2)}) collective-permute-start(bf16[432,256]{1,0:T(8,128)(2,1)S(1)} %slice_dynamic-update-slice_fusion), channel_id=1, source_target_pairs={{8,0},{16,8},{24,16},{32,24},{40,32},{48,40},{56,48},{64,56},{72,6... | collective-permute-start | bytes 663560 | tf_op jit(solution)/shard_map/ppermute | solution.py:376
  30.7 7.0 %copy-start.5 = (f32[112,384]{1,0:T(8,128)}, f32[112,384]{1,0:T(8,128)S(1)}, u32[]{:S(2)}) copy-start(f32[112,384]{1,0:T(8,128)S(1)} %pad_maximum_fusion.2.own_ref) | copy-start | bytes 516100
  30.7 7.0 %collective-permute-start.1 = (f32[112,128]{1,0:T(8,128)S(1)}, f32[112,128]{1,0:T(8,128)S(1)}, u32[]{:S(2)}, u32[]{:S(2)}) collective-permute-start(f32[112,128]{1,0:T(8,128)S(1)} %slice.123), channel_id=1, source_target_pairs={{0,8},{8,16},{16,24},{24,32},{32,40},{40,48},{48,56},{56,64},{64,7... | collective-permute-start | bytes 172040 | tf_op jit(solution)/shard_map/ppermute | solution.py:377
  37.7 0.6 copy-start.8
  38.3 0.7 copy-start.7
  56.8 24.4 %all-to-all-start.1 = ((f32[64,8,128]{2,1,0:T(8,128)}), f32[64,8,128]{2,1,0:T(8,128)S(1)}, u32[]{:S(2)}, u32[]{:S(2)}) async-start(f32[64,8,128]{2,1,0:T(8,128)} %bitcast.31), calls=%async_computation.1 | async-start | bytes 524288 | tf_op jit(solution)/shard_map/all_to_all | solution.py:385
  69.0 7.1 %collective-permute-start.2 = (bf16[32,256]{1,0:T(8,128)(2,1)}, bf16[32,256]{1,0:T(8,128)(2,1)S(1)}, u32[]{:S(2)}, u32[]{:S(2)}) collective-permute-start(bf16[32,256]{1,0:T(8,128)(2,1)} %get-tuple-element.16), channel_id=1, source_target_pairs={{0,8},{8,16},{16,24},{24,32},{32,40},{40,48},{48,56},{56,64},{64,7... | collective-permute-start | bytes 49160 | tf_op jit(solution)/shard_map/ppermute | solution.py:384
  100.3 18.5 %all-to-all-start.3 = ((f32[64,8,128]{2,1,0:T(8,128)}), f32[64,8,128]{2,1,0:T(8,128)S(1)}, u32[]{:S(2)}, u32[]{:S(2)}) async-start(f32[64,8,128]{2,1,0:T(8,128)} %broadcast_in_dim.79), calls=%async_computation.3 | async-start | bytes 524288 | tf_op jit(solution)/shard_map/all_to_all | solution.py:401

commit v3 on v2

--- a/solution.py
+++ b/solution.py
@@ -28,25 +28,34 @@
     return hi, (x - hi.astype(F32)).astype(BF)
 
 
-def band_kernel(dil_ref, w_ref, wt_ref, t_ref):
-    rows = lax.broadcasted_iota(jnp.int32, (256, 512), 0) >> 5
-    cols = lax.broadcasted_iota(jnp.int32, (256, 512), 1) >> 5
-    delta = cols - rows - 4
+def band_kernel(dil_ref, w_ref, t_ref):
     spread = (
         (lax.broadcasted_iota(jnp.int32, (C, 512), 1) & 31)
         == lax.broadcasted_iota(jnp.int32, (C, 512), 0)
     ).astype(F32).astype(BF)
+    offset = (lax.broadcasted_iota(jnp.int32, (C, 512), 1) >> 5) - 4
     for layer in range(2):
-        masks = [delta == b * dil_ref[layer] for b in (-1, 0, 1)]
-        for kind, ref in ((0, w_ref), (1, wt_ref)):
+        step = dil_ref[layer]
+        for kind in range(2):
             for slot in range(3):
-                total = jnp.zeros((256, 512), F32)
+                wide = []
                 for b in range(3):
-                    along = slot if kind == 0 else 2 - slot
-                    w = ref[layer, 3 * along + b]
-                    wide = _dot(jnp.concatenate([w] * 8, axis=0), spread)
-                    total = jnp.where(masks[b if kind == 0 else 2 - b], wide, total)
-                t_ref[2 * kind + layer, :, slot * 512 : (slot + 1) * 512] = total.astype(BF)
+                    if kind == 0:
+                        wide.append(_dot(w_ref[layer, 3 * slot + b], spread))
+                    else:
+                        w = w_ref[layer, 3 * (2 - slot) + 2 - b]
+                        wide.append(
+                            lax.dot_general(
+                                w, spread, (((0,), (0,)), ((), ())), preferred_element_type=F32
+                            )
+                        )
+                for j in range(8):
+                    value = jnp.zeros((C, 512), F32)
+                    for b in range(3):
+                        value = jnp.where(offset == j + (b - 1) * step, wide[b], value)
+                    t_ref[2 * kind + layer, C * j : C * j + C, 512 * slot : 512 * slot + 512] = (
+                        value.astype(BF)
+                    )
 
 
 def band_weights(dilations, conv_weight):
@@ -56,25 +65,65 @@
         in_specs=[
             pl.BlockSpec(memory_space=pltpu.SMEM),
             pl.BlockSpec(memory_space=pltpu.VMEM),
-            pl.BlockSpec(memory_space=pltpu.VMEM),
         ],
         out_specs=pl.BlockSpec(memory_space=pltpu.VMEM),
         compiler_params=pltpu.CompilerParams(vmem_limit_bytes=32 * 2**20),
         cost_estimate=pl.CostEstimate(flops=10**9, bytes_accessed=4 * 10**6, transcendentals=0),
         name="band_weights",
-    )(dilations, conv_weight, jnp.swapaxes(conv_weight, 2, 3))
+    )(dilations, conv_weight)
+
+
+def prepare_kernel(total_bins, emb_ref, proj_ref, cot_ref, limit_ref, pack_ref, cots_ref):
+    diag_dev, rows_dev = cot_ref.shape
+    diag_at = lax.axis_index("diag")
+    first_row = lax.axis_index("bin") * rows_dev
+    shape = (diag_dev, rows_dev)
+    bin_id = first_row + lax.broadcasted_iota(jnp.int32, shape, 1)
+    diag_id = diag_at * diag_dev + lax.broadcasted_iota(jnp.int32, shape, 0)
+    counted = (bin_id + diag_id < total_bins) & (diag_id < limit_ref[...][None, :])
+    cots = jnp.where(counted, cot_ref[...], 0.0)
+    cots_ref[...] = cots
+    columns = proj_ref.shape[1]
+    quarter = diag_dev // 4
+    proj = proj_ref[...].astype(F32)
+    flat = jnp.concatenate(
+        [proj[quarter * i : quarter * (i + 1)] for i in range(4)]
+        + [jnp.zeros((quarter, rows_dev - 4 * columns), F32)],
+        axis=1,
+    )
+    last = jnp.concatenate([cots[diag_dev - 8 :], flat], axis=0)
+    first = jnp.concatenate([cots[:8], flat], axis=0)
+    for peer in range(pack_ref.shape[0]):
+        pack_ref[peer, :diag_dev] = emb_ref[...]
+        pack_ref[peer, diag_dev:] = jnp.where(peer > diag_at, last, first).astype(BF)
+
+
+def prepare(total_bins, diags, *operands):
+    diag_dev, rows_dev = operands[0].shape
+    vmem = pl.BlockSpec(memory_space=pltpu.VMEM)
+    return pl.pallas_call(
+        functools.partial(prepare_kernel, total_bins),
+        out_shape=(
+            jax.ShapeDtypeStruct((diags, diag_dev + 16, rows_dev), BF),
+            jax.ShapeDtypeStruct((diag_dev, rows_dev), F32),
+        ),
+        in_specs=[vmem] * 4,
+        out_specs=(vmem, vmem),
+        compiler_params=pltpu.CompilerParams(vmem_limit_bytes=16 * 2**20),
+        name="prepare",
+    )(*operands)
 
 
 def pair_kernel(
     total_bins, total_diags,
-    sc_ref, own_ref, next_ref, prev_ref, bias_ref, limit_ref, head_ref, t_ref, emb_ref,
+    dil_ref, head_ref, own_ref, next_ref, prev_ref, bias_ref, limit_ref, t_ref, emb_ref,
     pred_ref, both_ref, spill_ref, sums_ref,
     x0, x1, g2, g1, d0, d1, bk, mk, vbuf, ubuf, left, gwide, acc, lsum, rsum,
 ):
-    first_row = sc_ref[0]
-    first_diag = sc_ref[1]
-    s1 = sc_ref[2]
-    s2 = sc_ref[3]
+    first_row = lax.axis_index("bin") * 384
+    first_diag = lax.axis_index("diag") * 32
+    s1 = dil_ref[0]
+    s2 = dil_ref[1]
 
     lane = lax.broadcasted_iota(jnp.int32, (8, LN), 1)
     low = lax.broadcasted_iota(jnp.int32, (C, 128), 1) < 64
@@ -103,25 +152,23 @@
     gwide[:, :384] = own[2 * C :]
     gwide[:, 384:] = jnp.where(low48, next_cots, prv[2 * C :])
     line = jnp.concatenate([prv[C : 2 * C], own[C : 2 * C], next_right], axis=1)
+    bias = pltpu.roll(bias_ref[...], lax.rem(256 + M - first_diag, 256), 1)
     vbuf[...] = pltpu.roll(line, 784 - first_diag, 1)[:, :512]
     ubuf[...] = pltpu.roll(line, lax.rem(912 - first_diag, 896), 1)[:, :256]
 
     at = lax.broadcasted_iota(jnp.int32, (C, 128), 1)
 
-    def columns(value):
-        return [value[:, 128 * i : 128 * i + 128] for i in range(value.shape[1] // 128)]
-
-    def store3(ref, row, value, shift):
-        cols = columns(value.astype(BF))
-        later = [pltpu.roll(v, shift, 1) for v in cols]
-        sooner = [pltpu.roll(v, 128 - shift, 1) for v in cols]
-        ref[1, pl.ds(row, C), :] = value.astype(BF)
-        for i in range(4):
-            here = pl.ds(128 * i, 128)
-            ref[0, pl.ds(row, C), here] = jnp.where(at < shift, later[i - 1], later[i])
-            ref[2, pl.ds(row, C), here] = jnp.where(
-                at < 128 - shift, sooner[i], sooner[(i + 1) % 4]
-            )
+    def spread(ref, rows, shift):
+        for row in rows:
+            cols = [ref[1, row : row + C, 128 * i : 128 * i + 128] for i in range(4)]
+            later = [pltpu.roll(v, shift, 1) for v in cols]
+            sooner = [pltpu.roll(v, 128 - shift, 1) for v in cols]
+            for i in range(4):
+                here = slice(128 * i, 128 * i + 128)
+                ref[0, row : row + C, here] = jnp.where(at < shift, later[i - 1], later[i])
+                ref[2, row : row + C, here] = jnp.where(
+                    at < 128 - shift, sooner[i], sooner[(i + 1) % 4]
+                )
 
     def times(value, mask):
         return (value.reshape(4, 8, value.shape[1]) * mask[None]).reshape(value.shape)
@@ -142,10 +189,11 @@
                 + [jnp.where(low, v[3], jnp.where(here, u[0], u[1]))],
                 axis=1,
             )
-            t = jnp.tanh(left[...] + shifted + bias_ref[:, k : k + 1])
+            t = jnp.tanh(left[...] + shifted + bias[:, k : k + 1])
             row = k * C
-            store3(x0, row, times(t, mask), s1)
+            x0[1, row : row + C] = times(t, mask).astype(BF)
             d0[pl.ds(row, C), :] = times(1.0 - t[:, :384] * t[:, :384], mask[:, :384])
+        spread(x0, range(8 * g * C, (8 * g + 8) * C, C), s1)
 
 
     def window(ref, first, width):
@@ -159,12 +207,13 @@
             mask = mk[k]
             t = t1[r * C : (r + 1) * C]
             base = x0[1, pl.ds(k * C, C), :].astype(F32)
-            store3(x1, (k - 4) * C, times(base + t, mask), s2)
+            x1[1, pl.ds((k - 4) * C, C), :] = times(base + t, mask).astype(BF)
             d1[pl.ds((k - 4) * C, C), :] = times(1.0 - t * t, mask)
-
-
-    head = jnp.broadcast_to(head_ref[...], (C, LN))
-    limits = limit_ref[...]
+        spread(x1, range(8 * g * C, (8 * g + 8) * C, C), s2)
+
+
+    head = jnp.concatenate([jnp.full((1, LN), head_ref[c], F32) for c in range(C)], axis=0)
+    limits = limit_ref[...][None, :]
     own_bin = first_row + lax.broadcasted_iota(jnp.int32, (8, 384), 1)
     own_row = lax.broadcasted_iota(jnp.int32, (8, 384), 0)
 
@@ -176,8 +225,9 @@
             k = 8 + 8 * g + r
             t = t2[r * C : (r + 1) * C]
             value = cots[r : r + 1] * (head * (1.0 - t * t))
-            store3(g2, (k - 8) * C, value, s2)
+            g2[1, pl.ds((k - 8) * C, C), :] = value.astype(BF)
             lines.append(jnp.sum(head[:, :384] * t[:, :384], axis=0, keepdims=True))
+        spread(g2, range(8 * g * C, (8 * g + 8) * C, C), s2)
 
         if 1 <= g < 5:
             diag_id = first_diag + 8 * (g - 1) + own_row
@@ -193,13 +243,13 @@
             k = 12 + 8 * g + r
             value = back[r * C : (r + 1) * C]
             at = (k - 12) * C
-            store3(g1, at, value * d1[pl.ds((k - 4) * C, C), :], s1)
+            g1[1, pl.ds(at, C), :] = (value * d1[pl.ds((k - 4) * C, C), :]).astype(BF)
             bk[pl.ds(at, C), :] = times(value, mk[k])[:, :384]
+        spread(g1, range(8 * g * C, (8 * g + 8) * C, C), s1)
 
 
     lsum[...] = jnp.zeros_like(lsum)
     rsum[...] = jnp.zeros_like(rsum)
-    acc[...] = jnp.zeros_like(acc)
 
     def stage_four(g):
         back = _dot(t_ref[2], window(g1, 8 * g, 384))
@@ -214,19 +264,20 @@
             skew = skew + (pltpu.roll(wide, r, 1) if r else wide)
         lsum[...] += part
         rsum[...] += pltpu.roll(skew, 8 * g, 1)
-        grad_two = g2[1, pl.ds((8 * g + 8) * C, 256), :384]
-        grad_one = g1[1, pl.ds((8 * g + 4) * C, 256), :384]
+
+    def wgrad(layer):
+        grads, fields, shift, near_at = ((g1, x0, 4, 12), (g2, x1, 8, 8))[layer]
+        lhs = jnp.concatenate([grads[1, (8 * g + shift) * C : (8 * g + shift + 8) * C, :384] for g in range(4)], axis=1)
         for a in range(3):
-            near = x0[a, pl.ds((8 * g + 12) * C, 512), :384]
-            acc[a] += _dot_nt(grad_one, near)
-            near = x1[a, pl.ds((8 * g + 8) * C, 512), :384]
-            acc[3 + a] += _dot_nt(grad_two, near)
-
+            rhs = jnp.concatenate([fields[a, (8 * g + near_at) * C : (8 * g + near_at + 16) * C, :384] for g in range(4)], axis=1)
+            acc[3 * layer + a] = _dot_nt(lhs, rhs)
 
     stages = ((stage_zero, 8), (stage_one, 7), (stage_two, 6), (stage_three, 5), (stage_four, 4))
     for stage, groups in stages:
         for g in range(groups):
             stage(g)
+    wgrad(1)
+    wgrad(0)
 
     rows = lax.broadcasted_iota(jnp.int32, (256, 512), 0) >> 5
     cols = lax.broadcasted_iota(jnp.int32, (256, 512), 1) >> 5
@@ -276,7 +327,7 @@
             jax.ShapeDtypeStruct((C, 256), BF),
             jax.ShapeDtypeStruct((512, 128), F32),
         ),
-        in_specs=[pl.BlockSpec(memory_space=pltpu.SMEM)] + [vmem] * 8,
+        in_specs=[pl.BlockSpec(memory_space=pltpu.SMEM)] * 2 + [vmem] * 7,
         out_specs=(vmem,) * 4,
         scratch_shapes=[
             pltpu.VMEM((3, 64 * C, LN), BF),
@@ -311,38 +362,14 @@
     diag_dev, rows_dev = cotangent.shape
     total_bins = rows_dev * bins
     total_diags = diag_dev * diags
-    bin_at = lax.axis_index("bin")
     diag_at = lax.axis_index("diag")
-    first_row = bin_at * rows_dev
     first_diag = diag_at * diag_dev
 
+    pack, cots = prepare(total_bins, diags, embeddings, projection, cotangent, band_limit)
     bands = band_weights(dilations, conv_weight)
-    bias = lax.dynamic_slice_in_dim(jnp.pad(dist_bias, ((0, 0), (M, M + 64))), first_diag, 128, 1)
-    scalars = jnp.stack([first_row, first_diag, dilations[0], dilations[1]]).astype(jnp.int32)
-
-    row_ids = first_row + jnp.arange(rows_dev, dtype=jnp.int32)[None, :]
-    diag_ids = first_diag + jnp.arange(diag_dev, dtype=jnp.int32)[:, None]
-    counted = (row_ids + diag_ids < total_bins) & (diag_ids < band_limit[None, :])
-    cots = jnp.where(counted, cotangent, 0.0)
-    cots_bf = cots.astype(BF)
-    peer = jnp.arange(diags, dtype=jnp.int32)[:, None, None]
-    edge = jnp.where(
-        peer > diag_at, cots_bf[None, diag_dev - 8 :], cots_bf[None, :8]
-    )
+    got = lax.all_to_all(pack, "diag", 0, 0)
+    got, bands = lax.optimization_barrier((got, bands))
     columns = projection.shape[1]
-    quarter = diag_dev // 4
-    flat = jnp.concatenate([projection[quarter * i : quarter * (i + 1)] for i in range(4)], axis=1)
-    flat = jnp.pad(flat, ((0, 0), (0, rows_dev - 4 * columns)))
-    pack = jnp.concatenate(
-        [
-            jnp.broadcast_to(embeddings[None], (diags,) + embeddings.shape),
-            edge,
-            jnp.broadcast_to(flat[None], (diags,) + flat.shape),
-        ],
-        axis=1,
-    )
-    got = lax.all_to_all(pack, "diag", 0, 0)
-    got, bands, bias = lax.optimization_barrier((got, bands, bias))
     features = diag_dev * diags
     emb_all = got[:, :diag_dev].reshape(features, rows_dev)
     flat = got[:, diag_dev + 8 :]
@@ -377,8 +404,8 @@
     prv = lax.ppermute(own[:, rows_dev - 128 :], "bin", up)
 
     predicted, both, spill, sums = pair_field(
-        total_bins, total_diags, scalars, own, nxt, prv, bias, band_limit[None, :],
-        head_weight[:, None], bands, emb_all,
+        total_bins, total_diags, dilations, head_weight, own, nxt, prv, dist_bias, band_limit,
+        bands, emb_all,
     )
 
     spill = lax.ppermute(spill, "bin", up)

time: 121 us -> 117 us (0.967)
  waiting for transfers between devices: 24.3 us -> 30.6 us
  blocking collectives: 18.1 us -> 14.8 us
  local copies, waits for them, and re-layouts: 11.9 us -> 8.97 us
  other arithmetic: 4.96 us -> 2.57 us
  Pallas kernels: 21.2 us -> 19.9 us
    all_to_all x1, waiting for transfers between devices: 2.54 us -> 8.12 us  [on_device(): got = lax.all_to_all(pack, 'diag', 0, 0)]
    broadcast_in_dim x4 -> x0, local copies, waits for them, and re-layouts: 3.37 us -> none  [the longest x1 1.34 us: on_device(): head_weight[:, None]]
    all_to_all x1, blocking collectives: 18.1 us -> 14.8 us  [on_device(): total = jnp.sum(lax.all_to_all(parts, 'diag', 0, 0).astype(F32), axis=0)]
    unnamed x21 -> x24, local copies, waits for them, and re-layouts: 5.56 us -> 7.41 us
    pallas_call x1, Pallas kernels: 3.34 us -> 2.1 us  [band_weights(): pl.pallas_call(band_kernel, out_shape=jax.ShapeDtypeStruct((4, 256, 1536)...]
  transfers between devices with their start and end apart: 6 -> 6, of which waited for: 5 -> 5; matrix products, arithmetic and copies ran while one was open for 6% -> 2% of each run, Pallas kernels for 3% -> 2%
where the time goes in v3:
time: 117 us; the launch traced here: 116 us
  starting transfers between devices  38.3 us (33%)
  waiting for transfers between devices  30.6 us (26%)
  Pallas kernels  19.9 us (17%)
  blocking collectives  14.8 us (13%)
  local copies, waits for them, and re-layouts  8.97 us (8%)
  other arithmetic  2.57 us (2%)
    pallas_call x1, Pallas kernels, pair_field(): pl.pallas_call(functools.partial(pair_kernel, total_bins, total_diags), o...  17 us
    all_to_all x1, blocking collectives, on_device(): total = jnp.sum(lax.all_to_all(parts, 'diag', 0, 0).astype(F32), axis=0)  14.8 us
    all_to_all x1, starting transfers between devices, on_device(): shares = lax.all_to_all(sums.reshape(bins, 512 // bins, 128), 'bin', 0, 0)  12.2 us
    all_to_all x1, waiting for transfers between devices, on_device(): lax.all_to_all(jnp.broadcast_to(whole[None], (bins,) + whole.shape), 'bin...  11.3 us
    all_to_all x1, starting transfers between devices, on_device(): got = lax.all_to_all(pack, 'diag', 0, 0)  10.3 us
    all_to_all x1, waiting for transfers between devices, on_device(): got = lax.all_to_all(pack, 'diag', 0, 0)  8.12 us
    unnamed x24, local copies, waits for them, and re-layouts  7.41 us
    all_to_all x1, starting transfers between devices, on_device(): lax.all_to_all(jnp.broadcast_to(whole[None], (bins,) + whole.shape), 'bin...  6.57 us
  transfers between devices with their start and end apart: 6, of which 5 were waited for; matrix products, arithmetic and copies ran while one was open for 2% of the time, Pallas kernels for 2%

profile of v3, /device:TPU:8, one launch (start us, length us, event | category | flops | bytes accessed | tf_op | source)
XLA Modules:
  0.0 116.4 jit_solution(9483344875340227840)
XLA Ops:
  0.6 0.0 copy-start
  0.6 0.8 copy-done
  1.4 0.0 copy-start.1
  1.4 0.7 copy-done.1
  2.2 0.0 copy-start.2
  2.2 0.7 copy-done.2
  2.9 0.0 copy-start.3
  2.9 0.7 copy-done.3
  3.5 0.8 prepare.1
  4.3 10.3 %all-to-all-start = ((bf16[8,48,384]{2,1,0:T(8,128)(2,1)}), bf16[8,48,384]{2,1,0:T(8,128)(2,1)S(1)}, u32[]{:S(2)}, u32[]{:S(2)}) async-start(bf16[8,48,384]{2,1,0:T(8,128)(2,1)} %get-tuple-element.12), calls=%async_computation | async-start | bytes 589824 | tf_op jit(solution)/shard_map/all_to_all | solution.py:370
  14.7 0.0 copy-start.4
  14.7 0.9 copy-done.4
  15.6 0.0 copy-start.5
  15.6 0.7 copy-done.5
  16.2 2.1 %band_weights.1.t_ref = bf16[4,256,1536]{2,1,0:T(8,128)(2,1)S(1)} custom-call(s32[2]{0:T(128)S(1)} %copy-done.5, bf16[2,9,32,32]{3,2,1,0:T(8,128)(2,1)S(1)} %copy-done.4), custom_call_target="tpu_custom_call" | custom-call | flops 1000000000 | bytes 4000000 | tf_op jit(solution)/shard_map/band_weights/pallas_call | solution.py:62
  18.3 0.0 copy-start.6
  18.3 1.6 %copy-done.6 = bf16[4,256,1536]{2,1,0:T(8,128)(2,1)} copy-done((bf16[4,256,1536]{2,1,0:T(8,128)(2,1)}, bf16[4,256,1536]{2,1,0:T(8,128)(2,1)S(1)}, u32[]{:S(2)}) %copy-start.6) | copy-done | bytes 3145752
  20.0 8.1 %all-to-all-done = bf16[8,48,384]{2,1,0:T(8,128)(2,1)S(1)} async-done(((bf16[8,48,384]{2,1,0:T(8,128)(2,1)}), bf16[8,48,384]{2,1,0:T(8,128)(2,1)S(1)}, u32[]{:S(2)}, u32[]{:S(2)}) %all-to-all-start) | async-done | bytes 294944 | tf_op jit(solution)/shard_map/all_to_all | solution.py:370
  28.1 0.1 fusion.15
  28.2 0.0 copy-start.7
  28.2 0.2 subtract_convert_fusion.1
  28.5 2.5 %collective-permute-start = (bf16[432,256]{1,0:T(8,128)(2,1)S(1)}, bf16[432,256]{1,0:T(8,128)(2,1)S(1)}, u32[]{:S(2)}, u32[]{:S(2)}) collective-permute-start(bf16[432,256]{1,0:T(8,128)(2,1)S(1)} %slice_dynamic-update-slice_fusion), channel_id=1, source_target_pairs={{8,0},{16,8},{24,16},{32,24},{40,32},{48,40},{56,48},{64,56},{72,6... | collective-permute-start | bytes 663560 | tf_op jit(solution)/shard_map/ppermute | solution.py:403
  31.0 0.0 copy-start.8
  31.1 3.4 %collective-permute-start.1 = (f32[112,128]{1,0:T(8,128)S(1)}, f32[112,128]{1,0:T(8,128)S(1)}, u32[]{:S(2)}, u32[]{:S(2)}) collective-permute-start(f32[112,128]{1,0:T(8,128)S(1)} %slice.94), channel_id=1, source_target_pairs={{0,8},{8,16},{16,24},{24,32},{32,40},{40,48},{48,56},{56,64},{64,7... | collective-permute-start | bytes 172040 | tf_op jit(solution)/shard_map/ppermute | solution.py:404
  34.4 3.6 %collective-permute-done.1.prev_ref = f32[112,128]{1,0:T(8,128)S(1)} collective-permute-done((f32[112,128]{1,0:T(8,128)S(1)}, f32[112,128]{1,0:T(8,128)S(1)}, u32[]{:S(2)}, u32[]{:S(2)}) %collective-permute-start.1) | collective-permute-done | bytes 57376 | tf_op jit(solution)/shard_map/ppermute | solution.py:404
  38.0 0.0 copy-start.10
  38.0 0.0 collective-permute-done.next_ref
  38.0 0.0 copy-done.7
  38.0 0.0 copy-done.8
  38.0 0.6 copy-done.10
  38.7 0.0 copy-start.9
  38.7 0.7 copy-done.9
  39.3 17.0 %pair_field.1 = (f32[32,384]{1,0:T(8,128)}, f32[64,384]{1,0:T(8,128)}, bf16[32,256]{1,0:T(8,128)(2,1)}, f32[512,128]{1,0:T(8,128)}) custom-call(s32[2]{0:T(128)} %dil_ref.3, f32[32]{0:T(128)} %head_ref.1, f32[112,384]{1,0:T(8,128)} %copy-done.8, bf16[432,256]{1,0:T(8,128)(2,1)} %copy-done.9, f32[112,128]{1,0:T(8,128)} %copy-done.10, f32[32,256]{1,0:T(8,128)} %bias_ref.1, ...), custom_call_target="tpu_custom_call" | custom-call | flops 12000000000 | bytes 5000000 | tf_op jit(solution)/shard_map/pair_field/pallas_call | solution.py:322
  56.3 12.2 %all-to-all-start.1 = ((f32[64,8,128]{2,1,0:T(8,128)}), f32[64,8,128]{2,1,0:T(8,128)S(1)}, u32[]{:S(2)}, u32[]{:S(2)}) async-start(f32[64,8,128]{2,1,0:T(8,128)} %bitcast.26), calls=%async_computation.1 | async-start | bytes 524288 | tf_op jit(solution)/shard_map/all_to_all | solution.py:412
  68.5 3.4 %collective-permute-start.2 = (bf16[32,256]{1,0:T(8,128)(2,1)}, bf16[32,256]{1,0:T(8,128)(2,1)S(1)}, u32[]{:S(2)}, u32[]{:S(2)}) collective-permute-start(bf16[32,256]{1,0:T(8,128)(2,1)} %get-tuple-element.18), channel_id=1, source_target_pairs={{0,8},{8,16},{16,24},{24,32},{32,40},{40,48},{48,56},{56,64},{64,7... | collective-permute-start | bytes 49160 | tf_op jit(solution)/shard_map/ppermute | solution.py:411
  71.9 3.7 %collective-permute-done.2 = bf16[32,256]{1,0:T(8,128)(2,1)S(1)} collective-permute-done((bf16[32,256]{1,0:T(8,128)(2,1)}, bf16[32,256]{1,0:T(8,128)(2,1)S(1)}, u32[]{:S(2)}, u32[]{:S(2)}) %collective-permute-start.2) | collective-permute-done | bytes 16416 | tf_op jit(solution)/shard_map/ppermute | solution.py:411
  75.6 0.9 fusion.3
  76.5 0.3 convolution_convert_fusion
  76.8 3.9 %all-to-all-done.1 = f32[64,8,128]{2,1,0:T(8,128)S(1)} async-done(((f32[64,8,128]{2,1,0:T(8,128)}), f32[64,8,128]{2,1,0:T(8,128)S(1)}, u32[]{:S(2)}, u32[]{:S(2)}) %all-to-all-start.1) | async-done | bytes 262176 | tf_op jit(solution)/shard_map/all_to_all | solution.py:412
  80.7 0.1 reduce_sum.18
  80.8 14.8 %all_to_all.20 = bf16[8,32,512]{2,1,0:T(8,128)(2,1)S(1)} all-to-all(bf16[8,32,512]{2,1,0:T(8,128)(2,1)S(1)} %pad_maximum_fusion), channel_id=1, replica_groups=mesh['bin'=64,'diag'=8] {'diag'}, dimensions={0} | all-to-all | bytes 524288 | tf_op jit(solution)/shard_map/all_to_all | solution.py:425
  95.7 0.7 broadcast_in_dim.19
  96.4 6.6 %all-to-all-start.3 = ((f32[64,8,128]{2,1,0:T(8,128)}), f32[64,8,128]{2,1,0:T(8,128)S(1)}, u32[]{:S(2)}, u32[]{:S(2)}) async-start(f32[64,8,128]{2,1,0:T(8,128)} %broadcast_in_dim.19), calls=%async_computation.3 | async-start | bytes 524288 | tf_op jit(solution)/shard_map/all_to_all | solution.py:428
  103.0 0.6 slice.95
  103.6 11.3 %all-to-all-done.3 = f32[64,8,128]{2,1,0:T(8,128)S(1)} async-done(((f32[64,8,128]{2,1,0:T(8,128)}), f32[64,8,128]{2,1,0:T(8,128)S(1)}, u32[]{:S(2)}, u32[]{:S(2)}) %all-to-all-start.3) | async-done | bytes 262176 | tf_op jit(solution)/shard_map/all_to_all | solution.py:428
  114.9 0.1 slice.99
  115.0 0.7 dynamic-slice_multiply_fusion
  115.7 0.8 maximum_multiply_fusion
  (20 shorter events, 0.2 us)
Async XLA Ops:
  0.6 0.8 copy-start
  1.4 0.7 copy-start.1
  2.2 0.7 copy-start.2
  2.9 0.7 copy-start.3
  4.3 23.8 %all-to-all-start = ((bf16[8,48,384]{2,1,0:T(8,128)(2,1)}), bf16[8,48,384]{2,1,0:T(8,128)(2,1)S(1)}, u32[]{:S(2)}, u32[]{:S(2)}) async-start(bf16[8,48,384]{2,1,0:T(8,128)(2,1)} %get-tuple-element.12), calls=%async_computation | async-start | bytes 589824 | tf_op jit(solution)/shard_map/all_to_all | solution.py:370
  14.7 0.9 copy-start.4
  15.6 0.7 copy-start.5
  18.3 1.6 %copy-start.6 = (bf16[4,256,1536]{2,1,0:T(8,128)(2,1)}, bf16[4,256,1536]{2,1,0:T(8,128)(2,1)S(1)}, u32[]{:S(2)}) copy-start(bf16[4,256,1536]{2,1,0:T(8,128)(2,1)S(1)} %band_weights.1.t_ref) | copy-start | bytes 9437188
  28.2 9.8 %copy-start.7 = (bf16[8,32,384]{2,1,0:T(8,128)(2,1)}, bf16[8,32,384]{2,1,0:T(8,128)(2,1)S(1)}, u32[]{:S(2)}) copy-start(bf16[8,32,384]{2,1,0:T(8,128)(2,1)S(1)} %slice.71) | copy-start | bytes 589828
  28.5 9.5 %collective-permute-start = (bf16[432,256]{1,0:T(8,128)(2,1)S(1)}, bf16[432,256]{1,0:T(8,128)(2,1)S(1)}, u32[]{:S(2)}, u32[]{:S(2)}) collective-permute-start(bf16[432,256]{1,0:T(8,128)(2,1)S(1)} %slice_dynamic-update-slice_fusion), channel_id=1, source_target_pairs={{8,0},{16,8},{24,16},{32,24},{40,32},{48,40},{56,48},{64,56},{72,6... | collective-permute-start | bytes 663560 | tf_op jit(solution)/shard_map/ppermute | solution.py:403
  31.0 7.0 %copy-start.8 = (f32[112,384]{1,0:T(8,128)}, f32[112,384]{1,0:T(8,128)S(1)}, u32[]{:S(2)}) copy-start(f32[112,384]{1,0:T(8,128)S(1)} %pad_maximum_fusion.1.own_ref) | copy-start | bytes 516100
  31.1 7.0 %collective-permute-start.1 = (f32[112,128]{1,0:T(8,128)S(1)}, f32[112,128]{1,0:T(8,128)S(1)}, u32[]{:S(2)}, u32[]{:S(2)}) collective-permute-start(f32[112,128]{1,0:T(8,128)S(1)} %slice.94), channel_id=1, source_target_pairs={{0,8},{8,16},{16,24},{24,32},{32,40},{40,48},{48,56},{56,64},{64,7... | collective-permute-start | bytes 172040 | tf_op jit(solution)/shard_map/ppermute | solution.py:404
  38.0 0.6 copy-start.10
  38.7 0.7 copy-start.9
  56.3 24.4 %all-to-all-start.1 = ((f32[64,8,128]{2,1,0:T(8,128)}), f32[64,8,128]{2,1,0:T(8,128)S(1)}, u32[]{:S(2)}, u32[]{:S(2)}) async-start(f32[64,8,128]{2,1,0:T(8,128)} %bitcast.26), calls=%async_computation.1 | async-start | bytes 524288 | tf_op jit(solution)/shard_map/all_to_all | solution.py:412
  68.5 7.1 %collective-permute-start.2 = (bf16[32,256]{1,0:T(8,128)(2,1)}, bf16[32,256]{1,0:T(8,128)(2,1)S(1)}, u32[]{:S(2)}, u32[]{:S(2)}) collective-permute-start(bf16[32,256]{1,0:T(8,128)(2,1)} %get-tuple-element.18), channel_id=1, source_target_pairs={{0,8},{8,16},{16,24},{24,32},{32,40},{40,48},{48,56},{56,64},{64,7... | collective-permute-start | bytes 49160 | tf_op jit(solution)/shard_map/ppermute | solution.py:411
  96.4 18.5 %all-to-all-start.3 = ((f32[64,8,128]{2,1,0:T(8,128)}), f32[64,8,128]{2,1,0:T(8,128)S(1)}, u32[]{:S(2)}, u32[]{:S(2)}) async-start(f32[64,8,128]{2,1,0:T(8,128)} %broadcast_in_dim.19), calls=%async_computation.3 | async-start | bytes 524288 | tf_op jit(solution)/shard_map/all_to_all | solution.py:428

commit v4 on v3

--- a/solution.py
+++ b/solution.py
@@ -29,11 +29,9 @@
 
 
 def band_kernel(dil_ref, w_ref, t_ref):
-    spread = (
-        (lax.broadcasted_iota(jnp.int32, (C, 512), 1) & 31)
-        == lax.broadcasted_iota(jnp.int32, (C, 512), 0)
-    ).astype(F32).astype(BF)
-    offset = (lax.broadcasted_iota(jnp.int32, (C, 512), 1) >> 5) - 4
+    lane = lax.broadcasted_iota(jnp.int32, (C, 384), 1)
+    spread = ((lane & 31) == lax.broadcasted_iota(jnp.int32, (C, 384), 0)).astype(F32).astype(BF)
+    offset = (lane >> 5) - 4
     for layer in range(2):
         step = dil_ref[layer]
         for kind in range(2):
@@ -49,31 +47,42 @@
                                 w, spread, (((0,), (0,)), ((), ())), preferred_element_type=F32
                             )
                         )
-                for j in range(8):
-                    value = jnp.zeros((C, 512), F32)
+                for j in range(4):
+                    value = jnp.zeros((C, 384), F32)
                     for b in range(3):
                         value = jnp.where(offset == j + (b - 1) * step, wide[b], value)
-                    t_ref[2 * kind + layer, C * j : C * j + C, 512 * slot : 512 * slot + 512] = (
+                    t_ref[2 * kind + layer, C * j : C * j + C, 384 * slot : 384 * slot + 384] = (
                         value.astype(BF)
                     )
 
 
 def band_weights(dilations, conv_weight):
+    vmem = pl.BlockSpec(memory_space=pltpu.VMEM)
     return pl.pallas_call(
         band_kernel,
-        out_shape=jax.ShapeDtypeStruct((4, 256, 1536), BF),
-        in_specs=[
-            pl.BlockSpec(memory_space=pltpu.SMEM),
-            pl.BlockSpec(memory_space=pltpu.VMEM),
-        ],
-        out_specs=pl.BlockSpec(memory_space=pltpu.VMEM),
-        compiler_params=pltpu.CompilerParams(vmem_limit_bytes=32 * 2**20),
-        cost_estimate=pl.CostEstimate(flops=10**9, bytes_accessed=4 * 10**6, transcendentals=0),
+        out_shape=jax.ShapeDtypeStruct((4, 128, 1152), BF),
+        in_specs=[pl.BlockSpec(memory_space=pltpu.SMEM), vmem],
+        out_specs=vmem,
+        compiler_params=pltpu.CompilerParams(vmem_limit_bytes=16 * 2**20),
+        cost_estimate=pl.CostEstimate(flops=10**8, bytes_accessed=2 * 10**6, transcendentals=0),
         name="band_weights",
     )(dilations, conv_weight)
 
 
-def prepare_kernel(total_bins, emb_ref, proj_ref, cot_ref, limit_ref, pack_ref, cots_ref):
+def prepare_kernel(
+    total_bins, emb_hbm, proj_hbm, cot_hbm, limit_hbm, pack_ref, cots_ref,
+    emb_ref, proj_ref, cot_ref, limit_ref, sems,
+):
+    copies = [
+        pltpu.make_async_copy(source, target, sems.at[i])
+        for i, (source, target) in enumerate(
+            ((emb_hbm, emb_ref), (proj_hbm, proj_ref), (cot_hbm, cot_ref), (limit_hbm, limit_ref))
+        )
+    ]
+    for copy in copies:
+        copy.start()
+    for copy in copies:
+        copy.wait()
     diag_dev, rows_dev = cot_ref.shape
     diag_at = lax.axis_index("diag")
     first_row = lax.axis_index("bin") * rows_dev
@@ -107,19 +116,27 @@
             jax.ShapeDtypeStruct((diags, diag_dev + 16, rows_dev), BF),
             jax.ShapeDtypeStruct((diag_dev, rows_dev), F32),
         ),
-        in_specs=[vmem] * 4,
+        in_specs=[pl.BlockSpec(memory_space=pl.ANY)] * 4,
         out_specs=(vmem, vmem),
-        compiler_params=pltpu.CompilerParams(vmem_limit_bytes=16 * 2**20),
+        scratch_shapes=[pltpu.VMEM(x.shape, x.dtype) for x in operands]
+        + [pltpu.SemaphoreType.DMA((4,))],
+        compiler_params=pltpu.CompilerParams(vmem_limit_bytes=56 * 2**20),
         name="prepare",
     )(*operands)
 
 
 def pair_kernel(
     total_bins, total_diags,
-    dil_ref, head_ref, own_ref, next_ref, prev_ref, bias_ref, limit_ref, t_ref, emb_ref,
+    dil_ref, head_ref, next_hbm, prev_hbm, own_ref, bias_ref, limit_ref, t_ref, emb_ref,
     pred_ref, both_ref, spill_ref, sums_ref,
-    x0, x1, g2, g1, d0, d1, bk, mk, vbuf, ubuf, left, gwide, acc, lsum, rsum,
+    x0, x1, g2, g1, d0, d1, bk, mk, vbuf, ubuf, left, gwide, acc, lsum, rsum, next_ref, prev_ref, sems,
 ):
+    arrivals = [
+        pltpu.make_async_copy(next_hbm, next_ref, sems.at[0]),
+        pltpu.make_async_copy(prev_hbm, prev_ref, sems.at[1]),
+    ]
+    for copy in arrivals:
+        copy.start()
     first_row = lax.axis_index("bin") * 384
     first_diag = lax.axis_index("diag") * 32
     s1 = dil_ref[0]
@@ -131,6 +148,8 @@
     bin_ok = (bin_id >= 0) & (bin_id < total_bins)
 
     own = own_ref[...]
+    for copy in arrivals:
+        copy.wait()
     prv = prev_ref[...]
 
     def rows_of(first, count, lanes):
@@ -173,7 +192,7 @@
     def times(value, mask):
         return (value.reshape(4, 8, value.shape[1]) * mask[None]).reshape(value.shape)
 
-    def stage_zero(g):
+    def stage_zero(g, back):
         for r in range(8):
             k = 8 * g + r
             diag_id = first_diag - M + k
@@ -197,11 +216,19 @@
 
 
     def window(ref, first, width):
-        rows = pl.ds(first * C, 512)
-        return jnp.concatenate([ref[a, rows, :width] for a in range(3)], axis=0)
-
-    def stage_one(g):
-        t1 = jnp.tanh(_dot(t_ref[0], window(x0, 8 * g, LN)))
+        return [ref[a, first * C : (first + 12) * C, :width] for a in range(3)]
+
+    def conv(kind, ref, first, width):
+        return jnp.concatenate(
+            [
+                _dot(t_ref[kind], jnp.concatenate(window(ref, at_offset, width), axis=0))
+                for at_offset in (first, first + 4)
+            ],
+            axis=0,
+        )
+
+    def stage_one(g, back):
+        t1 = jnp.tanh(back)
         for r in range(8):
             k = 4 + 8 * g + r
             mask = mk[k]
@@ -217,8 +244,8 @@
     own_bin = first_row + lax.broadcasted_iota(jnp.int32, (8, 384), 1)
     own_row = lax.broadcasted_iota(jnp.int32, (8, 384), 0)
 
-    def stage_two(g):
-        t2 = jnp.tanh(_dot(t_ref[1], window(x1, 8 * g, LN)))
+    def stage_two(g, back):
+        t2 = jnp.tanh(back)
         cots = gwide[pl.ds(8 * g, 8), :]
         lines = []
         for r in range(8):
@@ -237,8 +264,7 @@
             )
 
 
-    def stage_three(g):
-        back = _dot(t_ref[3], window(g2, 8 * g, LN))
+    def stage_three(g, back):
         for r in range(8):
             k = 12 + 8 * g + r
             value = back[r * C : (r + 1) * C]
@@ -251,8 +277,7 @@
     lsum[...] = jnp.zeros_like(lsum)
     rsum[...] = jnp.zeros_like(rsum)
 
-    def stage_four(g):
-        back = _dot(t_ref[2], window(g1, 8 * g, 384))
+    def stage_four(g, back):
         part = jnp.zeros((C, 384), F32)
         skew = jnp.zeros((C, LN), F32)
         for r in range(8):
@@ -272,13 +297,18 @@
             rhs = jnp.concatenate([fields[a, (8 * g + near_at) * C : (8 * g + near_at + 16) * C, :384] for g in range(4)], axis=1)
             acc[3 * layer + a] = _dot_nt(lhs, rhs)
 
-    stages = ((stage_zero, 8), (stage_one, 7), (stage_two, 6), (stage_three, 5), (stage_four, 4))
-    for stage, groups in stages:
+    stages = (
+        (stage_zero, 8, None),
+        (stage_one, 7, lambda g: conv(0, x0, 8 * g, LN)),
+        (stage_two, 6, lambda g: conv(1, x1, 8 * g, LN)),
+        (stage_three, 5, lambda g: conv(3, g2, 8 * g, LN)),
+        (stage_four, 4, lambda g: conv(2, g1, 8 * g, 384)),
+    )
+    for stage, groups, dot in stages:
         for g in range(groups):
-            stage(g)
+            stage(g, dot(g) if dot else None)
     wgrad(1)
     wgrad(0)
-
     rows = lax.broadcasted_iota(jnp.int32, (256, 512), 0) >> 5
     cols = lax.broadcasted_iota(jnp.int32, (256, 512), 1) >> 5
     delta = cols - rows - 4
@@ -294,6 +324,7 @@
                 kept = kept + pltpu.roll(kept, 64, 1)
                 taps.append(kept + pltpu.roll(kept, 32, 1))
 
+
     right = jnp.concatenate([rsum[...], jnp.zeros((C, 128), F32)], axis=1)
     right = pltpu.roll(right, first_diag, 1)
     both_ref[:C] = lsum[...]
@@ -327,7 +358,9 @@
             jax.ShapeDtypeStruct((C, 256), BF),
             jax.ShapeDtypeStruct((512, 128), F32),
         ),
-        in_specs=[pl.BlockSpec(memory_space=pltpu.SMEM)] * 2 + [vmem] * 7,
+        in_specs=[pl.BlockSpec(memory_space=pltpu.SMEM)] * 2
+        + [pl.BlockSpec(memory_space=pl.ANY)] * 2
+        + [vmem] * 5,
         out_specs=(vmem,) * 4,
         scratch_shapes=[
             pltpu.VMEM((3, 64 * C, LN), BF),
@@ -345,6 +378,9 @@
             pltpu.VMEM((6, 256, 512), F32),
             pltpu.VMEM((C, 384), F32),
             pltpu.VMEM((C, LN), F32),
+            pltpu.VMEM((432, 256), BF),
+            pltpu.VMEM((112, 128), F32),
+            pltpu.SemaphoreType.DMA((2,)),
         ],
         compiler_params=pltpu.CompilerParams(vmem_limit_bytes=56 * 2**20),
         cost_estimate=pl.CostEstimate(
@@ -352,6 +388,32 @@
         ),
         name="pair_field",
     )(*operands)
+
+
+def finish_kernel(scaling, every_ref, proj_ref, conv_ref):
+    first_diag = pl.multiple_of(lax.axis_index("diag") * C, C)
+    proj_ref[...] = scaling * every_ref[pl.ds(first_diag, C), 2 * C :]
+    for tap in range(18):
+        if tap < 16:
+            value = every_ref[C * tap : C * tap + C, :C]
+        else:
+            value = every_ref[C * (tap - 16) : C * (tap - 15), C : 2 * C]
+        conv_ref[tap // 9, tap % 9] = scaling * value
+
+
+def finish(scaling, every):
+    vmem = pl.BlockSpec(memory_space=pltpu.VMEM)
+    return pl.pallas_call(
+        functools.partial(finish_kernel, scaling),
+        out_shape=(
+            jax.ShapeDtypeStruct((C, 2 * C), F32),
+            jax.ShapeDtypeStruct((2, 9, C, C), F32),
+        ),
+        in_specs=[vmem],
+        out_specs=(vmem, vmem),
+        compiler_params=pltpu.CompilerParams(vmem_limit_bytes=16 * 2**20),
+        name="finish",
+    )(every)
 
 
 def on_device(
@@ -404,7 +466,7 @@
     prv = lax.ppermute(own[:, rows_dev - 128 :], "bin", up)
 
     predicted, both, spill, sums = pair_field(
-        total_bins, total_diags, dilations, head_weight, own, nxt, prv, dist_bias, band_limit,
+        total_bins, total_diags, dilations, head_weight, nxt, prv, own, dist_bias, band_limit,
         bands, emb_all,
     )
 
@@ -429,12 +491,7 @@
         jnp.broadcast_to(whole[None], (bins,) + whole.shape), "bin", 0, 0
     ).reshape(bins * count, 128)
     scaling = 1.0 / math.sqrt(total_bins * total_diags)
-    grad_conv = scaling * jnp.concatenate(
-        [every[:, :C].reshape(16, C, C), every[: 2 * C, C : 2 * C].reshape(2, C, C)], axis=0
-    ).reshape(2, 9, C, C)
-    grad_proj = scaling * lax.dynamic_slice(
-        every, (first_diag, 2 * C), (diag_dev, 2 * C)
-    )
+    grad_proj, grad_conv = finish(scaling, every)
     return (predicted, grad_embed, grad_proj, grad_conv)
 
 

time: 117 us -> 114 us (0.974)
  local copies, waits for them, and re-layouts: 8.97 us -> 5.38 us
    unnamed x24 -> x18, local copies, waits for them, and re-layouts: 7.41 us -> 3.89 us
    mul x2 -> x0, other arithmetic: 1.44 us -> none  [the longest x1 0.75 us: on_device(): scaling * jnp.concatenate([every[:, :C].reshape(16, C, C), every[:2 * C,...]
  transfers between devices with their start and end apart: 6 -> 6, of which waited for: 5 -> 5; matrix products, arithmetic and copies ran while one was open for 2% -> 2% of each run, Pallas kernels for 2% -> 1%
where the time goes in v4:
time: 114 us
  starting transfers between devices  38.3 us (34%)
  waiting for transfers between devices  31.4 us (28%)
  Pallas kernels  20.8 us (18%)
  blocking collectives  14.7 us (13%)
  local copies, waits for them, and re-layouts  5.38 us (5%)
  other arithmetic  1.93 us (2%)
    pallas_call x1, Pallas kernels, pair_field(): pl.pallas_call(functools.partial(pair_kernel, total_bins, total_diags), o...  17.2 us
    all_to_all x1, blocking collectives, on_device(): total = jnp.sum(lax.all_to_all(parts, 'diag', 0, 0).astype(F32), axis=0)  14.7 us
    all_to_all x1, starting transfers between devices, on_device(): shares = lax.all_to_all(sums.reshape(bins, 512 // bins, 128), 'bin', 0, 0)  12.2 us
    all_to_all x1, waiting for transfers between devices, on_device(): lax.all_to_all(jnp.broadcast_to(whole[None], (bins,) + whole.shape), 'bin...  11.3 us
    all_to_all x1, starting transfers between devices, on_device(): got = lax.all_to_all(pack, 'diag', 0, 0)  10.3 us
    all_to_all x1, waiting for transfers between devices, on_device(): got = lax.all_to_all(pack, 'diag', 0, 0)  8.9 us
    all_to_all x1, starting transfers between devices, on_device(): lax.all_to_all(jnp.broadcast_to(whole[None], (bins,) + whole.shape), 'bin...  6.56 us
    all_to_all x1, waiting for transfers between devices, on_device(): shares = lax.all_to_all(sums.reshape(bins, 512 // bins, 128), 'bin', 0, 0)  3.93 us
  transfers between devices with their start and end apart: 6, of which 5 were waited for; matrix products, arithmetic and copies ran while one was open for 2% of the time, Pallas kernels for 1%

profile of v4, /device:TPU:8, one launch (start us, length us, event | category | flops | bytes accessed | tf_op | source)
XLA Modules:
  0.0 113.8 jit_solution(2130997128465708351)
XLA Ops:
  0.6 1.7 %prepare.1 = (bf16[8,48,384]{2,1,0:T(8,128)(2,1)}, f32[32,384]{1,0:T(8,128)}) custom-call(bf16[32,384]{1,0:T(8,128)(2,1)} %emb_hbm.1, bf16[32,64]{1,0:T(8,128)(2,1)} %proj_hbm.1, f32[32,384]{1,0:T(8,128)} %cot_hbm.1, s32[384]{0:T(512)} %limit_ref.1), custom_call_target="tpu_custom_call" | custom-call | tf_op jit(solution)/shard_map/prepare/pallas_call | solution.py:113
  2.3 10.3 %all-to-all-start = ((bf16[8,48,384]{2,1,0:T(8,128)(2,1)}), bf16[8,48,384]{2,1,0:T(8,128)(2,1)S(1)}, u32[]{:S(2)}, u32[]{:S(2)}) async-start(bf16[8,48,384]{2,1,0:T(8,128)(2,1)} %get-tuple-element.14), calls=%async_computation | async-start | bytes 589824 | tf_op jit(solution)/shard_map/all_to_all | solution.py:432
  12.6 0.8 convert.13
  13.4 0.0 copy-start.1
  13.4 0.9 copy-done.1
  14.3 0.0 copy-start.2
  14.3 0.7 copy-done.2
  15.0 0.0 copy-start.5
  15.0 1.1 band_weights.1.t_ref
  16.1 0.0 copy-start
  16.1 1.0 copy-done
  17.2 8.9 %all-to-all-done = bf16[8,48,384]{2,1,0:T(8,128)(2,1)S(1)} async-done(((bf16[8,48,384]{2,1,0:T(8,128)(2,1)}), bf16[8,48,384]{2,1,0:T(8,128)(2,1)S(1)}, u32[]{:S(2)}, u32[]{:S(2)}) %all-to-all-start) | async-done | bytes 294944 | tf_op jit(solution)/shard_map/all_to_all | solution.py:432
  26.1 0.1 fusion.15
  26.2 0.0 copy-start.3
  26.2 0.2 subtract_convert_fusion.1
  26.5 2.5 %collective-permute-start = (bf16[432,256]{1,0:T(8,128)(2,1)S(1)}, bf16[432,256]{1,0:T(8,128)(2,1)S(1)}, u32[]{:S(2)}, u32[]{:S(2)}) collective-permute-start(bf16[432,256]{1,0:T(8,128)(2,1)S(1)} %slice_dynamic-update-slice_fusion), channel_id=1, source_target_pairs={{8,0},{16,8},{24,16},{32,24},{40,32},{48,40},{56,48},{64,56},{72,6... | collective-permute-start | bytes 663560 | tf_op jit(solution)/shard_map/ppermute | solution.py:465
  29.0 0.0 copy-done.5
  29.0 0.0 copy-start.4
  29.0 3.4 %collective-permute-start.1 = (f32[112,128]{1,0:T(8,128)S(1)}, f32[112,128]{1,0:T(8,128)S(1)}, u32[]{:S(2)}, u32[]{:S(2)}) collective-permute-start(f32[112,128]{1,0:T(8,128)S(1)} %slice.86), channel_id=1, source_target_pairs={{0,8},{8,16},{16,24},{24,32},{32,40},{40,48},{48,56},{56,64},{64,7... | collective-permute-start | bytes 172040 | tf_op jit(solution)/shard_map/ppermute | solution.py:466
  32.4 3.6 %collective-permute-done.1.prev_hbm = f32[112,128]{1,0:T(8,128)S(1)} collective-permute-done((f32[112,128]{1,0:T(8,128)S(1)}, f32[112,128]{1,0:T(8,128)S(1)}, u32[]{:S(2)}, u32[]{:S(2)}) %collective-permute-start.1) | collective-permute-done | bytes 57376 | tf_op jit(solution)/shard_map/ppermute | solution.py:466
  36.0 0.0 copy-start.7
  36.0 0.0 collective-permute-done.next_hbm
  36.0 0.0 copy-done.3
  36.0 0.0 copy-done.4
  36.0 0.6 copy-done.7
  36.6 0.0 copy-start.6
  36.6 0.7 copy-done.6
  37.3 17.2 %pair_field.1 = (f32[32,384]{1,0:T(8,128)}, f32[64,384]{1,0:T(8,128)}, bf16[32,256]{1,0:T(8,128)(2,1)}, f32[512,128]{1,0:T(8,128)}) custom-call(s32[2]{0:T(128)} %dil_ref.3, f32[32]{0:T(128)} %head_ref.1, bf16[432,256]{1,0:T(8,128)(2,1)} %copy-done.6, f32[112,128]{1,0:T(8,128)} %copy-done.7, f32[112,384]{1,0:T(8,128)} %copy-done.4, f32[32,256]{1,0:T(8,128)} %bias_ref.1, ...), custom_call_target="tpu_custom_call" | custom-call | flops 12000000000 | bytes 5000000 | tf_op jit(solution)/shard_map/pair_field/pallas_call | solution.py:353
  54.5 12.2 %all-to-all-start.1 = ((f32[64,8,128]{2,1,0:T(8,128)}), f32[64,8,128]{2,1,0:T(8,128)S(1)}, u32[]{:S(2)}, u32[]{:S(2)}) async-start(f32[64,8,128]{2,1,0:T(8,128)} %bitcast.19), calls=%async_computation.1 | async-start | bytes 524288 | tf_op jit(solution)/shard_map/all_to_all | solution.py:474
  66.7 3.4 %collective-permute-start.2 = (bf16[32,256]{1,0:T(8,128)(2,1)}, bf16[32,256]{1,0:T(8,128)(2,1)S(1)}, u32[]{:S(2)}, u32[]{:S(2)}) collective-permute-start(bf16[32,256]{1,0:T(8,128)(2,1)} %get-tuple-element.20), channel_id=1, source_target_pairs={{0,8},{8,16},{16,24},{24,32},{32,40},{40,48},{48,56},{56,64},{64,7... | collective-permute-start | bytes 49160 | tf_op jit(solution)/shard_map/ppermute | solution.py:473
  70.1 3.7 %collective-permute-done.2 = bf16[32,256]{1,0:T(8,128)(2,1)S(1)} collective-permute-done((bf16[32,256]{1,0:T(8,128)(2,1)}, bf16[32,256]{1,0:T(8,128)(2,1)S(1)}, u32[]{:S(2)}, u32[]{:S(2)}) %collective-permute-start.2) | collective-permute-done | bytes 16416 | tf_op jit(solution)/shard_map/ppermute | solution.py:473
  73.8 0.9 fusion.3
  74.7 0.3 convolution_convert_fusion
  75.0 3.9 %all-to-all-done.1 = f32[64,8,128]{2,1,0:T(8,128)S(1)} async-done(((f32[64,8,128]{2,1,0:T(8,128)}), f32[64,8,128]{2,1,0:T(8,128)S(1)}, u32[]{:S(2)}, u32[]{:S(2)}) %all-to-all-start.1) | async-done | bytes 262176 | tf_op jit(solution)/shard_map/all_to_all | solution.py:474
  78.9 0.1 reduce_sum.18
  79.0 14.7 %all_to_all.20 = bf16[8,32,512]{2,1,0:T(8,128)(2,1)S(1)} all-to-all(bf16[8,32,512]{2,1,0:T(8,128)(2,1)S(1)} %pad_maximum_fusion), channel_id=1, replica_groups=mesh['bin'=64,'diag'=8] {'diag'}, dimensions={0} | all-to-all | bytes 524288 | tf_op jit(solution)/shard_map/all_to_all | solution.py:487
  93.8 0.7 broadcast_in_dim.19
  94.5 6.6 %all-to-all-start.3 = ((f32[64,8,128]{2,1,0:T(8,128)}), f32[64,8,128]{2,1,0:T(8,128)S(1)}, u32[]{:S(2)}, u32[]{:S(2)}) async-start(f32[64,8,128]{2,1,0:T(8,128)} %broadcast_in_dim.19), calls=%async_computation.3 | async-start | bytes 524288 | tf_op jit(solution)/shard_map/all_to_all | solution.py:490
  101.1 0.6 slice.87
  101.7 11.3 %all-to-all-done.3 = f32[64,8,128]{2,1,0:T(8,128)S(1)} async-done(((f32[64,8,128]{2,1,0:T(8,128)}), f32[64,8,128]{2,1,0:T(8,128)S(1)}, u32[]{:S(2)}, u32[]{:S(2)}) %all-to-all-start.3) | async-done | bytes 262176 | tf_op jit(solution)/shard_map/all_to_all | solution.py:490
  113.0 0.8 finish.1
  (19 shorter events, 0.2 us)
Async XLA Ops:
  2.3 23.8 %all-to-all-start = ((bf16[8,48,384]{2,1,0:T(8,128)(2,1)}), bf16[8,48,384]{2,1,0:T(8,128)(2,1)S(1)}, u32[]{:S(2)}, u32[]{:S(2)}) async-start(bf16[8,48,384]{2,1,0:T(8,128)(2,1)} %get-tuple-element.14), calls=%async_computation | async-start | bytes 589824 | tf_op jit(solution)/shard_map/all_to_all | solution.py:432
  13.4 0.9 copy-start.1
  14.3 0.7 copy-start.2
  15.0 14.0 %copy-start.5 = (f32[32,384]{1,0:T(8,128)S(1)}, f32[32,384]{1,0:T(8,128)}, u32[]{:S(2)}) copy-start(f32[32,384]{1,0:T(8,128)} %get-tuple-element.16) | copy-start | bytes 147460
  16.1 1.0 copy-start
  26.2 9.8 %copy-start.3 = (bf16[8,32,384]{2,1,0:T(8,128)(2,1)}, bf16[8,32,384]{2,1,0:T(8,128)(2,1)S(1)}, u32[]{:S(2)}) copy-start(bf16[8,32,384]{2,1,0:T(8,128)(2,1)S(1)} %slice.65) | copy-start | bytes 589828
  26.5 9.5 %collective-permute-start = (bf16[432,256]{1,0:T(8,128)(2,1)S(1)}, bf16[432,256]{1,0:T(8,128)(2,1)S(1)}, u32[]{:S(2)}, u32[]{:S(2)}) collective-permute-start(bf16[432,256]{1,0:T(8,128)(2,1)S(1)} %slice_dynamic-update-slice_fusion), channel_id=1, source_target_pairs={{8,0},{16,8},{24,16},{32,24},{40,32},{48,40},{56,48},{64,56},{72,6... | collective-permute-start | bytes 663560 | tf_op jit(solution)/shard_map/ppermute | solution.py:465
  29.0 7.0 %copy-start.4 = (f32[112,384]{1,0:T(8,128)}, f32[112,384]{1,0:T(8,128)S(1)}, u32[]{:S(2)}) copy-start(f32[112,384]{1,0:T(8,128)S(1)} %pad_maximum_fusion.1.own_ref) | copy-start | bytes 516100
  29.0 7.0 %collective-permute-start.1 = (f32[112,128]{1,0:T(8,128)S(1)}, f32[112,128]{1,0:T(8,128)S(1)}, u32[]{:S(2)}, u32[]{:S(2)}) collective-permute-start(f32[112,128]{1,0:T(8,128)S(1)} %slice.86), channel_id=1, source_target_pairs={{0,8},{8,16},{16,24},{24,32},{32,40},{40,48},{48,56},{56,64},{64,7... | collective-permute-start | bytes 172040 | tf_op jit(solution)/shard_map/ppermute | solution.py:466
  36.0 0.6 copy-start.7
  36.6 0.7 copy-start.6
  54.5 24.4 %all-to-all-start.1 = ((f32[64,8,128]{2,1,0:T(8,128)}), f32[64,8,128]{2,1,0:T(8,128)S(1)}, u32[]{:S(2)}, u32[]{:S(2)}) async-start(f32[64,8,128]{2,1,0:T(8,128)} %bitcast.19), calls=%async_computation.1 | async-start | bytes 524288 | tf_op jit(solution)/shard_map/all_to_all | solution.py:474
  66.7 7.1 %collective-permute-start.2 = (bf16[32,256]{1,0:T(8,128)(2,1)}, bf16[32,256]{1,0:T(8,128)(2,1)S(1)}, u32[]{:S(2)}, u32[]{:S(2)}) collective-permute-start(bf16[32,256]{1,0:T(8,128)(2,1)} %get-tuple-element.20), channel_id=1, source_target_pairs={{0,8},{8,16},{16,24},{24,32},{32,40},{40,48},{48,56},{56,64},{64,7... | collective-permute-start | bytes 49160 | tf_op jit(solution)/shard_map/ppermute | solution.py:473
  94.5 18.5 %all-to-all-start.3 = ((f32[64,8,128]{2,1,0:T(8,128)}), f32[64,8,128]{2,1,0:T(8,128)S(1)}, u32[]{:S(2)}, u32[]{:S(2)}) async-start(f32[64,8,128]{2,1,0:T(8,128)} %broadcast_in_dim.19), calls=%async_computation.3 | async-start | bytes 524288 | tf_op jit(solution)/shard_map/all_to_all | solution.py:490

commit v5 on v4

--- a/solution.py
+++ b/solution.py
@@ -116,27 +116,21 @@
             jax.ShapeDtypeStruct((diags, diag_dev + 16, rows_dev), BF),
             jax.ShapeDtypeStruct((diag_dev, rows_dev), F32),
         ),
-        in_specs=[pl.BlockSpec(memory_space=pl.ANY)] * 4,
+        in_specs=[pl.BlockSpec(memory_space=pltpu.HBM)] * 4,
         out_specs=(vmem, vmem),
         scratch_shapes=[pltpu.VMEM(x.shape, x.dtype) for x in operands]
         + [pltpu.SemaphoreType.DMA((4,))],
-        compiler_params=pltpu.CompilerParams(vmem_limit_bytes=56 * 2**20),
+        compiler_params=pltpu.CompilerParams(vmem_limit_bytes=16 * 2**20),
         name="prepare",
     )(*operands)
 
 
 def pair_kernel(
     total_bins, total_diags,
-    dil_ref, head_ref, next_hbm, prev_hbm, own_ref, bias_ref, limit_ref, t_ref, emb_ref,
+    dil_ref, head_ref, next_ref, prev_ref, own_ref, bias_ref, limit_ref, t_ref, emb_ref,
     pred_ref, both_ref, spill_ref, sums_ref,
-    x0, x1, g2, g1, d0, d1, bk, mk, vbuf, ubuf, left, gwide, acc, lsum, rsum, next_ref, prev_ref, sems,
+    x0, x1, g2, g1, d0, d1, bk, mk, vbuf, ubuf, left, gwide, acc, lsum, rsum,
 ):
-    arrivals = [
-        pltpu.make_async_copy(next_hbm, next_ref, sems.at[0]),
-        pltpu.make_async_copy(prev_hbm, prev_ref, sems.at[1]),
-    ]
-    for copy in arrivals:
-        copy.start()
     first_row = lax.axis_index("bin") * 384
     first_diag = lax.axis_index("diag") * 32
     s1 = dil_ref[0]
@@ -148,8 +142,6 @@
     bin_ok = (bin_id >= 0) & (bin_id < total_bins)
 
     own = own_ref[...]
-    for copy in arrivals:
-        copy.wait()
     prv = prev_ref[...]
 
     def rows_of(first, count, lanes):
@@ -339,13 +331,13 @@
     part = _dot_nt(emb, jnp.concatenate([none, high], axis=0)) + _dot_nt(
         emb, jnp.concatenate([none, rest], axis=0)
     )
-    for t in range(16):
-        value = jnp.where(at < 32, taps[t], 0.0)
-        if t < 2:
-            value = jnp.where(at < 32, value, taps[16 + t])
-        if t < 8:
-            value = jnp.where(at < 64, value, part[C * t : C * t + C])
-        sums_ref[C * t : C * t + C] = value
+    for i in range(4):
+        value = jnp.where(at < 64, taps[4 * i + 1], taps[4 * i + 3])
+        value = jnp.where((at & 63) < 32, jnp.where(at < 64, taps[4 * i], taps[4 * i + 2]), value)
+        sums_ref[C * i : C * i + C] = value
+    sums_ref[4 * C : 5 * C] = jnp.where(at < 32, taps[16], taps[17])
+    sums_ref[5 * C : 9 * C] = pltpu.roll(part[: 4 * C], 64, 1) + part[4 * C :]
+    sums_ref[9 * C :] = jnp.zeros((C, 128), F32)
 
 
 def pair_field(total_bins, total_diags, *operands):
@@ -356,11 +348,9 @@
             jax.ShapeDtypeStruct((32, 384), F32),
             jax.ShapeDtypeStruct((2 * C, 384), F32),
             jax.ShapeDtypeStruct((C, 256), BF),
-            jax.ShapeDtypeStruct((512, 128), F32),
+            jax.ShapeDtypeStruct((10 * C, 128), F32),
         ),
-        in_specs=[pl.BlockSpec(memory_space=pltpu.SMEM)] * 2
-        + [pl.BlockSpec(memory_space=pl.ANY)] * 2
-        + [vmem] * 5,
+        in_specs=[pl.BlockSpec(memory_space=pltpu.SMEM)] * 2 + [vmem] * 7,
         out_specs=(vmem,) * 4,
         scratch_shapes=[
             pltpu.VMEM((3, 64 * C, LN), BF),
@@ -378,11 +368,8 @@
             pltpu.VMEM((6, 256, 512), F32),
             pltpu.VMEM((C, 384), F32),
             pltpu.VMEM((C, LN), F32),
-            pltpu.VMEM((432, 256), BF),
-            pltpu.VMEM((112, 128), F32),
-            pltpu.SemaphoreType.DMA((2,)),
         ],
-        compiler_params=pltpu.CompilerParams(vmem_limit_bytes=56 * 2**20),
+        compiler_params=pltpu.CompilerParams(vmem_limit_bytes=42 * 2**20),
         cost_estimate=pl.CostEstimate(
             flops=12 * 10**9, bytes_accessed=5 * 10**6, transcendentals=3 * 10**6
         ),
@@ -391,13 +378,13 @@
 
 
 def finish_kernel(scaling, every_ref, proj_ref, conv_ref):
-    first_diag = pl.multiple_of(lax.axis_index("diag") * C, C)
-    proj_ref[...] = scaling * every_ref[pl.ds(first_diag, C), 2 * C :]
+    diag_at = lax.axis_index("diag")
+    row = pl.multiple_of((5 + (diag_at & 3)) * C, C)
+    value = every_ref[pl.ds(row, C), :]
+    proj_ref[...] = scaling * jnp.where(diag_at < 4, value[:, : 2 * C], value[:, 2 * C :])
     for tap in range(18):
-        if tap < 16:
-            value = every_ref[C * tap : C * tap + C, :C]
-        else:
-            value = every_ref[C * (tap - 16) : C * (tap - 15), C : 2 * C]
+        lanes = C * (tap % 4)
+        value = every_ref[C * (tap // 4) : C * (tap // 4) + C, lanes : lanes + C]
         conv_ref[tap // 9, tap % 9] = scaling * value
 
 
@@ -471,13 +458,13 @@
     )
 
     spill = lax.ppermute(spill, "bin", up)
-    shares = lax.all_to_all(sums.reshape(bins, 512 // bins, 128), "bin", 0, 0)
+    shares = lax.all_to_all(sums.reshape(bins, 10 * C // bins, 1, 128), "bin", 0, 0)
     both = both + jnp.pad(spill.astype(F32), ((C, 0), (0, rows_dev - spill.shape[1])))
     high, rest = _split(both)
     parts = _dot(
         jnp.concatenate([proj_all, proj_all], axis=1), jnp.concatenate([high, rest], axis=0)
     ).astype(BF).reshape(diags, diag_dev, rows_dev)
-    share = jnp.sum(shares, axis=0)
+    share = jnp.sum(shares, axis=0)[:, 0]
     high, rest = _split(share)
     count = share.shape[0]
     tail = jnp.pad(jnp.concatenate([high, rest], axis=0), ((0, diag_dev - 2 * count), (0, 0)))
@@ -488,7 +475,7 @@
     grad_embed = total[:, :rows_dev]
     whole = total[:count, rows_dev:] + total[count : 2 * count, rows_dev:]
     every = lax.all_to_all(
-        jnp.broadcast_to(whole[None], (bins,) + whole.shape), "bin", 0, 0
+        jnp.broadcast_to(whole[None, :, None], (bins, count, 1, 128)), "bin", 0, 0
     ).reshape(bins * count, 128)
     scaling = 1.0 / math.sqrt(total_bins * total_diags)
     grad_proj, grad_conv = finish(scaling, every)

time: 114 us -> 113 us (level)
  Pallas kernels: 20.8 us -> 17.8 us
  waiting for transfers between devices: 31.4 us -> 33.7 us
  other arithmetic: 1.93 us -> 0.31 us
    all_to_all x2, waiting for transfers between devices: 15.2 us -> 19.5 us  [the longest x1 9.89 us: on_device(): lax.all_to_all(sums.reshape(bins, 10 * C // bins, 1, 128), 'bin', 0, 0)]
    ppermute x1, waiting for transfers between devices: 3.72 us -> 0.01 us  [on_device(): spill = lax.ppermute(spill, 'bin', up)]
    pallas_call x1, Pallas kernels: 17.2 us -> 15 us  [pair_field(): pl.pallas_call(functools.partial(pair_kernel, total_bins, total_diags), o...]
    all_to_all x1, waiting for transfers between devices: 8.9 us -> 10.7 us  [on_device(): got = lax.all_to_all(pack, 'diag', 0, 0)]
    unnamed x18 -> x22, local copies, waits for them, and re-layouts: 3.89 us -> 4.5 us
  transfers between devices with their start and end apart: 6 -> 6, of which waited for: 5 -> 4; matrix products, arithmetic and copies ran while one was open for 2% -> 1% of each run, Pallas kernels for 1% -> 1%
where the time goes in v5:
time: 113 us
  starting transfers between devices  38.9 us (34%)
  waiting for transfers between devices  33.7 us (30%)
  Pallas kernels  17.8 us (16%)
  blocking collectives  14.6 us (13%)
  local copies, waits for them, and re-layouts  6.02 us (5%)
    pallas_call x1, Pallas kernels, pair_field(): pl.pallas_call(functools.partial(pair_kernel, total_bins, total_diags), o...  15 us
    all_to_all x1, blocking collectives, on_device(): total = jnp.sum(lax.all_to_all(parts, 'diag', 0, 0).astype(F32), axis=0)  14.6 us
    all_to_all x1, starting transfers between devices, on_device(): lax.all_to_all(sums.reshape(bins, 10 * C // bins, 1, 128), 'bin', 0, 0)  12.7 us
    all_to_all x1, waiting for transfers between devices, on_device(): got = lax.all_to_all(pack, 'diag', 0, 0)  10.7 us
    all_to_all x1, starting transfers between devices, on_device(): got = lax.all_to_all(pack, 'diag', 0, 0)  10.3 us
    all_to_all x1, waiting for transfers between devices, on_device(): lax.all_to_all(sums.reshape(bins, 10 * C // bins, 1, 128), 'bin', 0, 0)  9.89 us
    all_to_all x1, waiting for transfers between devices, on_device(): lax.all_to_all(jnp.broadcast_to(whole[None, :, None], (bins, count, 1, 12...  9.57 us
    all_to_all x1, starting transfers between devices, on_device(): lax.all_to_all(jnp.broadcast_to(whole[None, :, None], (bins, count, 1, 12...  5.96 us
  transfers between devices with their start and end apart: 6, of which 4 were waited for; matrix products, arithmetic and copies ran while one was open for 1% of the time, Pallas kernels for 1%

profile of v5, /device:TPU:8, one launch (start us, length us, event | category | flops | bytes accessed | tf_op | source)
XLA Modules:
  0.0 112.8 jit_solution(12976529693806898118)
XLA Ops:
  0.6 0.0 copy-start.1
  0.6 0.8 copy-done.1
  1.4 0.0 copy-start.2
  1.4 0.7 copy-done.2
  2.2 0.0 copy-start.3
  2.2 0.7 copy-done.3
  2.9 0.0 copy-start.4
  2.9 0.7 copy-done.4
  3.5 0.9 prepare.1
  4.5 10.3 %all-to-all-start = ((bf16[8,48,384]{2,1,0:T(8,128)(2,1)}), bf16[8,48,384]{2,1,0:T(8,128)(2,1)S(1)}, u32[]{:S(2)}, u32[]{:S(2)}) async-start(bf16[8,48,384]{2,1,0:T(8,128)(2,1)} %get-tuple-element.14), calls=%async_computation | async-start | bytes 589824 | tf_op jit(solution)/shard_map/all_to_all | solution.py:419
  14.8 0.0 copy-start
  14.8 0.9 copy-done
  15.7 0.0 copy-start.6
  15.7 0.7 copy-done.6
  16.4 1.1 band_weights.1.t_ref
  17.5 0.0 copy-start.5
  17.5 0.0 copy-start.7
  17.5 0.0 copy-start.8
  17.5 0.0 copy-start.9
  17.5 10.7 %all-to-all-done = bf16[8,48,384]{2,1,0:T(8,128)(2,1)S(1)} async-done(((bf16[8,48,384]{2,1,0:T(8,128)(2,1)}), bf16[8,48,384]{2,1,0:T(8,128)(2,1)S(1)}, u32[]{:S(2)}, u32[]{:S(2)}) %all-to-all-start) | async-done | bytes 294944 | tf_op jit(solution)/shard_map/all_to_all | solution.py:419
  28.2 0.1 fusion.15
  28.4 0.2 subtract_convert_fusion.1
  28.7 2.5 %collective-permute-start = (bf16[432,256]{1,0:T(8,128)(2,1)S(1)}, bf16[432,256]{1,0:T(8,128)(2,1)S(1)}, u32[]{:S(2)}, u32[]{:S(2)}) collective-permute-start(bf16[432,256]{1,0:T(8,128)(2,1)S(1)} %slice_dynamic-update-slice_fusion), channel_id=1, source_target_pairs={{8,0},{16,8},{24,16},{32,24},{40,32},{48,40},{56,48},{64,56},{72,6... | collective-permute-start | bytes 663560 | tf_op jit(solution)/shard_map/ppermute | solution.py:452
  31.2 3.4 %collective-permute-start.1 = (f32[112,128]{1,0:T(8,128)S(1)}, f32[112,128]{1,0:T(8,128)S(1)}, u32[]{:S(2)}, u32[]{:S(2)}) collective-permute-start(f32[112,128]{1,0:T(8,128)S(1)} %slice.86), channel_id=1, source_target_pairs={{0,8},{8,16},{16,24},{24,32},{32,40},{40,48},{48,56},{56,64},{64,7... | collective-permute-start | bytes 172040 | tf_op jit(solution)/shard_map/ppermute | solution.py:453
  34.6 3.6 %collective-permute-done.1.prev_ref = f32[112,128]{1,0:T(8,128)S(1)} collective-permute-done((f32[112,128]{1,0:T(8,128)S(1)}, f32[112,128]{1,0:T(8,128)S(1)}, u32[]{:S(2)}, u32[]{:S(2)}) %collective-permute-start.1) | collective-permute-done | bytes 57376 | tf_op jit(solution)/shard_map/ppermute | solution.py:453
  38.1 0.0 collective-permute-done.next_ref
  38.1 0.0 copy-done.5
  38.2 0.0 copy-done.7
  38.2 0.0 copy-done.8
  38.2 0.0 copy-done.9
  38.2 15.0 %pair_field.1 = (f32[32,384]{1,0:T(8,128)}, f32[64,384]{1,0:T(8,128)S(1)}, bf16[32,256]{1,0:T(8,128)(2,1)S(1)}, f32[320,128]{1,0:T(8,128)}) custom-call(s32[2]{0:T(128)S(1)} %copy-done.7, f32[32]{0:T(128)S(1)} %copy-done.9, bf16[432,256]{1,0:T(8,128)(2,1)S(1)} %collective-permute-done.next_ref, f32[112,128]{1,0:T(8,128)S(1)} %collective-permute-done.1.prev_ref, ...), custom_call_target="tpu_custom_call" | custom-call | flops 12000000000 | bytes 5000000 | tf_op jit(solution)/shard_map/pair_field/pallas_call | solution.py:345
  53.1 4.1 %collective-permute-start.2 = (bf16[32,256]{1,0:T(8,128)(2,1)S(1)}, bf16[32,256]{1,0:T(8,128)(2,1)S(1)}, u32[]{:S(2)}, u32[]{:S(2)}) collective-permute-start(bf16[32,256]{1,0:T(8,128)(2,1)S(1)} %get-tuple-element.20), channel_id=1, source_target_pairs={{0,8},{8,16},{16,24},{24,32},{32,40},{40,48},{48,56},{56,64},{64,7... | collective-permute-start | bytes 49160 | tf_op jit(solution)/shard_map/ppermute | solution.py:460
  57.3 12.7 %all-to-all-start.1 = ((f32[64,5,1,128]{3,2,1,0:T(1,128)}), f32[64,5,1,128]{3,2,1,0:T(1,128)S(1)}, u32[]{:S(2)}, u32[]{:S(2)}) async-start(f32[64,5,1,128]{3,2,1,0:T(1,128)} %bitcast.6), calls=%async_computation.1 | async-start | bytes 327680 | tf_op jit(solution)/shard_map/all_to_all | solution.py:461
  70.0 0.0 collective-permute-done.2
  70.0 0.3 convolution_convert_fusion
  70.3 9.9 %all-to-all-done.1 = f32[64,5,1,128]{3,2,1,0:T(1,128)S(1)} async-done(((f32[64,5,1,128]{3,2,1,0:T(1,128)}), f32[64,5,1,128]{3,2,1,0:T(1,128)S(1)}, u32[]{:S(2)}, u32[]{:S(2)}) %all-to-all-start.1) | async-done | bytes 163872 | tf_op jit(solution)/shard_map/all_to_all | solution.py:461
  80.2 0.1 reduce_sum.18
  80.4 14.6 %all_to_all.20 = bf16[8,32,512]{2,1,0:T(8,128)(2,1)S(1)} all-to-all(bf16[8,32,512]{2,1,0:T(8,128)(2,1)S(1)} %pad_maximum_fusion), channel_id=1, replica_groups=mesh['bin'=64,'diag'=8] {'diag'}, dimensions={0} | all-to-all | bytes 524288 | tf_op jit(solution)/shard_map/all_to_all | solution.py:474
  95.1 0.8 broadcast_in_dim.19
  95.8 6.0 %all-to-all-start.3 = ((f32[64,5,1,128]{3,2,1,0:T(1,128)}), f32[64,5,1,128]{3,2,1,0:T(1,128)S(1)}, u32[]{:S(2)}, u32[]{:S(2)}) async-start(f32[64,5,1,128]{3,2,1,0:T(1,128)} %broadcast_in_dim.19), calls=%async_computation.3 | async-start | bytes 327680 | tf_op jit(solution)/shard_map/all_to_all | solution.py:477
  101.8 0.6 slice.87
  102.4 9.6 %all-to-all-done.3 = f32[64,5,1,128]{3,2,1,0:T(1,128)S(1)} async-done(((f32[64,5,1,128]{3,2,1,0:T(1,128)}), f32[64,5,1,128]{3,2,1,0:T(1,128)S(1)}, u32[]{:S(2)}, u32[]{:S(2)}) %all-to-all-start.3) | async-done | bytes 163872 | tf_op jit(solution)/shard_map/all_to_all | solution.py:477
  112.0 0.8 finish.1
  (21 shorter events, 0.2 us)
Async XLA Ops:
  0.6 0.8 copy-start.1
  1.4 0.7 copy-start.2
  2.2 0.7 copy-start.3
  2.9 0.7 copy-start.4
  4.5 23.8 %all-to-all-start = ((bf16[8,48,384]{2,1,0:T(8,128)(2,1)}), bf16[8,48,384]{2,1,0:T(8,128)(2,1)S(1)}, u32[]{:S(2)}, u32[]{:S(2)}) async-start(bf16[8,48,384]{2,1,0:T(8,128)(2,1)} %get-tuple-element.14), calls=%async_computation | async-start | bytes 589824 | tf_op jit(solution)/shard_map/all_to_all | solution.py:419
  14.8 0.9 copy-start
  15.7 0.7 copy-start.6
  17.5 20.7 %copy-start.5 = (s32[384]{0:T(512)S(1)}, s32[384]{0:T(512)}, u32[]{:S(2)}) copy-start(s32[384]{0:T(512)} %limit_ref.1) | copy-start | bytes 4612
  17.5 20.7 %copy-start.7 = (s32[2]{0:T(128)S(1)}, s32[2]{0:T(128)}, u32[]{:S(2)}) copy-start(s32[2]{0:T(128)} %dil_ref.3) | copy-start | bytes 28
  17.5 20.7 %copy-start.8 = (f32[32,256]{1,0:T(8,128)S(1)}, f32[32,256]{1,0:T(8,128)}, u32[]{:S(2)}) copy-start(f32[32,256]{1,0:T(8,128)} %bias_ref.1) | copy-start | bytes 98308
  17.5 20.7 %copy-start.9 = (f32[32]{0:T(128)S(1)}, f32[32]{0:T(128)}, u32[]{:S(2)}) copy-start(f32[32]{0:T(128)} %head_ref.1) | copy-start | bytes 388
  28.7 9.5 %collective-permute-start = (bf16[432,256]{1,0:T(8,128)(2,1)S(1)}, bf16[432,256]{1,0:T(8,128)(2,1)S(1)}, u32[]{:S(2)}, u32[]{:S(2)}) collective-permute-start(bf16[432,256]{1,0:T(8,128)(2,1)S(1)} %slice_dynamic-update-slice_fusion), channel_id=1, source_target_pairs={{8,0},{16,8},{24,16},{32,24},{40,32},{48,40},{56,48},{64,56},{72,6... | collective-permute-start | bytes 663560 | tf_op jit(solution)/shard_map/ppermute | solution.py:452
  31.2 7.0 %collective-permute-start.1 = (f32[112,128]{1,0:T(8,128)S(1)}, f32[112,128]{1,0:T(8,128)S(1)}, u32[]{:S(2)}, u32[]{:S(2)}) collective-permute-start(f32[112,128]{1,0:T(8,128)S(1)} %slice.86), channel_id=1, source_target_pairs={{0,8},{8,16},{16,24},{24,32},{32,40},{40,48},{48,56},{56,64},{64,7... | collective-permute-start | bytes 172040 | tf_op jit(solution)/shard_map/ppermute | solution.py:453
  53.1 16.9 %collective-permute-start.2 = (bf16[32,256]{1,0:T(8,128)(2,1)S(1)}, bf16[32,256]{1,0:T(8,128)(2,1)S(1)}, u32[]{:S(2)}, u32[]{:S(2)}) collective-permute-start(bf16[32,256]{1,0:T(8,128)(2,1)S(1)} %get-tuple-element.20), channel_id=1, source_target_pairs={{0,8},{8,16},{16,24},{24,32},{32,40},{40,48},{48,56},{56,64},{64,7... | collective-permute-start | bytes 49160 | tf_op jit(solution)/shard_map/ppermute | solution.py:460
  57.3 22.9 %all-to-all-start.1 = ((f32[64,5,1,128]{3,2,1,0:T(1,128)}), f32[64,5,1,128]{3,2,1,0:T(1,128)S(1)}, u32[]{:S(2)}, u32[]{:S(2)}) async-start(f32[64,5,1,128]{3,2,1,0:T(1,128)} %bitcast.6), calls=%async_computation.1 | async-start | bytes 327680 | tf_op jit(solution)/shard_map/all_to_all | solution.py:461
  95.8 16.2 %all-to-all-start.3 = ((f32[64,5,1,128]{3,2,1,0:T(1,128)}), f32[64,5,1,128]{3,2,1,0:T(1,128)S(1)}, u32[]{:S(2)}, u32[]{:S(2)}) async-start(f32[64,5,1,128]{3,2,1,0:T(1,128)} %broadcast_in_dim.19), calls=%async_computation.3 | async-start | bytes 327680 | tf_op jit(solution)/shard_map/all_to_all | solution.py:477

commit v6 on v5

--- a/solution.py
+++ b/solution.py
@@ -120,7 +120,7 @@
         out_specs=(vmem, vmem),
         scratch_shapes=[pltpu.VMEM(x.shape, x.dtype) for x in operands]
         + [pltpu.SemaphoreType.DMA((4,))],
-        compiler_params=pltpu.CompilerParams(vmem_limit_bytes=16 * 2**20),
+        compiler_params=pltpu.CompilerParams(vmem_limit_bytes=56 * 2**20),
         name="prepare",
     )(*operands)
 
@@ -331,13 +331,18 @@
     part = _dot_nt(emb, jnp.concatenate([none, high], axis=0)) + _dot_nt(
         emb, jnp.concatenate([none, rest], axis=0)
     )
+    blocks = []
     for i in range(4):
         value = jnp.where(at < 64, taps[4 * i + 1], taps[4 * i + 3])
-        value = jnp.where((at & 63) < 32, jnp.where(at < 64, taps[4 * i], taps[4 * i + 2]), value)
-        sums_ref[C * i : C * i + C] = value
-    sums_ref[4 * C : 5 * C] = jnp.where(at < 32, taps[16], taps[17])
-    sums_ref[5 * C : 9 * C] = pltpu.roll(part[: 4 * C], 64, 1) + part[4 * C :]
-    sums_ref[9 * C :] = jnp.zeros((C, 128), F32)
+        blocks.append(
+            jnp.where((at & 63) < 32, jnp.where(at < 64, taps[4 * i], taps[4 * i + 2]), value)
+        )
+    blocks.append(jnp.where(at < 32, taps[16], taps[17]))
+    value = pltpu.roll(part[: 4 * C], 64, 1) + part[4 * C :]
+    blocks += [value[C * i : C * i + C] for i in range(4)] + [jnp.zeros((C, 128), F32)]
+    sums_ref[...] = jnp.zeros_like(sums_ref)
+    for t in range(5):
+        sums_ref[pl.ds(t, 64, stride=8), :] = jnp.concatenate(blocks[2 * t : 2 * t + 2], axis=0)
 
 
 def pair_field(total_bins, total_diags, *operands):
@@ -348,7 +353,7 @@
             jax.ShapeDtypeStruct((32, 384), F32),
             jax.ShapeDtypeStruct((2 * C, 384), F32),
             jax.ShapeDtypeStruct((C, 256), BF),
-            jax.ShapeDtypeStruct((10 * C, 128), F32),
+            jax.ShapeDtypeStruct((512, 128), F32),
         ),
         in_specs=[pl.BlockSpec(memory_space=pltpu.SMEM)] * 2 + [vmem] * 7,
         out_specs=(vmem,) * 4,
@@ -379,13 +384,15 @@
 
 def finish_kernel(scaling, every_ref, proj_ref, conv_ref):
     diag_at = lax.axis_index("diag")
-    row = pl.multiple_of((5 + (diag_at & 3)) * C, C)
-    value = every_ref[pl.ds(row, C), :]
+    rows = [every_ref[pl.ds(t, 64, stride=5), :] for t in range(5)]
+    blocks = [row[C * half : C * half + C] for row in rows for half in range(2)]
+    value = blocks[5]
+    for i in range(1, 4):
+        value = jnp.where((diag_at & 3) == i, blocks[5 + i], value)
     proj_ref[...] = scaling * jnp.where(diag_at < 4, value[:, : 2 * C], value[:, 2 * C :])
     for tap in range(18):
         lanes = C * (tap % 4)
-        value = every_ref[C * (tap // 4) : C * (tap // 4) + C, lanes : lanes + C]
-        conv_ref[tap // 9, tap % 9] = scaling * value
+        conv_ref[tap // 9, tap % 9] = scaling * blocks[tap // 4][:, lanes : lanes + C]
 
 
 def finish(scaling, every):
@@ -458,13 +465,13 @@
     )
 
     spill = lax.ppermute(spill, "bin", up)
-    shares = lax.all_to_all(sums.reshape(bins, 10 * C // bins, 1, 128), "bin", 0, 0)
+    shares = lax.all_to_all(sums.reshape(bins, 512 // bins, 128), "bin", 0, 0)
     both = both + jnp.pad(spill.astype(F32), ((C, 0), (0, rows_dev - spill.shape[1])))
     high, rest = _split(both)
     parts = _dot(
         jnp.concatenate([proj_all, proj_all], axis=1), jnp.concatenate([high, rest], axis=0)
     ).astype(BF).reshape(diags, diag_dev, rows_dev)
-    share = jnp.sum(shares, axis=0)[:, 0]
+    share = jnp.sum(shares, axis=0)[:5]
     high, rest = _split(share)
     count = share.shape[0]
     tail = jnp.pad(jnp.concatenate([high, rest], axis=0), ((0, diag_dev - 2 * count), (0, 0)))

time: 113 us -> 109 us (0.965)
  local copies, waits for them, and re-layouts: 6.02 us -> 3.12 us
  waiting for transfers between devices: 33.7 us -> 31.6 us
    all_to_all x1, waiting for transfers between devices: 9.89 us -> 5.28 us  [on_device(): shares = lax.all_to_all(sums.reshape(bins, 512 // bins, 128), 'bin', 0, 0)]
    ppermute x1, waiting for transfers between devices: 0.01 us -> 3.28 us  [on_device(): spill = lax.ppermute(spill, 'bin', up)]
    unnamed x22 -> x16, local copies, waits for them, and re-layouts: 4.5 us -> 1.6 us
  transfers between devices with their start and end apart: 6 -> 6, of which waited for: 4 -> 5; matrix products, arithmetic and copies ran while one was open for 1% -> 2% of each run, Pallas kernels for 1% -> 1%
where the time goes in v6:
time: 109 us
  starting transfers between devices  38.2 us (35%)
  waiting for transfers between devices  31.6 us (29%)
  Pallas kernels  18.6 us (17%)
  blocking collectives  14.7 us (13%)
  local copies, waits for them, and re-layouts  3.12 us (3%)
    pallas_call x1, Pallas kernels, pair_field(): pl.pallas_call(functools.partial(pair_kernel, total_bins, total_diags), o...  15 us
    all_to_all x1, blocking collectives, on_device(): total = jnp.sum(lax.all_to_all(parts, 'diag', 0, 0).astype(F32), axis=0)  14.7 us
    all_to_all x1, starting transfers between devices, on_device(): shares = lax.all_to_all(sums.reshape(bins, 512 // bins, 128), 'bin', 0, 0)  12.2 us
    all_to_all x1, starting transfers between devices, on_device(): got = lax.all_to_all(pack, 'diag', 0, 0)  10.3 us
    all_to_all x1, waiting for transfers between devices, on_device(): got = lax.all_to_all(pack, 'diag', 0, 0)  9.9 us
    all_to_all x1, waiting for transfers between devices, on_device(): lax.all_to_all(jnp.broadcast_to(whole[None, :, None], (bins, count, 1, 12...  9.57 us
    all_to_all x1, starting transfers between devices, on_device(): lax.all_to_all(jnp.broadcast_to(whole[None, :, None], (bins, count, 1, 12...  6.43 us
    all_to_all x1, waiting for transfers between devices, on_device(): shares = lax.all_to_all(sums.reshape(bins, 512 // bins, 128), 'bin', 0, 0)  5.28 us
  transfers between devices with their start and end apart: 6, of which 5 were waited for; matrix products, arithmetic and copies ran while one was open for 2% of the time, Pallas kernels for 1%

profile of v6, /device:TPU:8, one launch (start us, length us, event | category | flops | bytes accessed | tf_op | source)
XLA Modules:
  0.0 108.6 jit_solution(8182802564367432077)
XLA Ops:
  0.6 1.7 %prepare.1 = (bf16[8,48,384]{2,1,0:T(8,128)(2,1)}, f32[32,384]{1,0:T(8,128)}) custom-call(bf16[32,384]{1,0:T(8,128)(2,1)} %emb_hbm.1, bf16[32,64]{1,0:T(8,128)(2,1)} %proj_hbm.1, f32[32,384]{1,0:T(8,128)} %cot_hbm.1, s32[384]{0:T(512)} %limit_ref.1), custom_call_target="tpu_custom_call" | custom-call | tf_op jit(solution)/shard_map/prepare/pallas_call | solution.py:113
  2.3 10.3 %all-to-all-start = ((bf16[8,48,384]{2,1,0:T(8,128)(2,1)}), bf16[8,48,384]{2,1,0:T(8,128)(2,1)S(1)}, u32[]{:S(2)}, u32[]{:S(2)}) async-start(bf16[8,48,384]{2,1,0:T(8,128)(2,1)} %get-tuple-element.14), calls=%async_computation | async-start | bytes 589824 | tf_op jit(solution)/shard_map/all_to_all | solution.py:426
  12.6 0.8 convert.13
  13.4 0.0 copy-start
  13.4 0.9 copy-done
  14.3 0.0 copy-start.2
  14.3 0.7 copy-done.2
  15.0 0.0 copy-start.6
  15.0 1.1 %band_weights.1.t_ref = bf16[4,128,1152]{2,1,0:T(8,128)(2,1)S(1)} custom-call(s32[2]{0:T(128)S(1)} %copy-done.2, bf16[2,9,32,32]{3,2,1,0:T(8,128)(2,1)S(1)} %copy-done), custom_call_target="tpu_custom_call" | custom-call | flops 100000000 | bytes 2000000 | tf_op jit(solution)/shard_map/band_weights/pallas_call | solution.py:61
  16.1 0.0 copy-start.1
  16.1 0.0 copy-start.3
  16.1 0.0 copy-start.4
  16.2 0.0 copy-start.5
  16.2 9.9 %all-to-all-done = bf16[8,48,384]{2,1,0:T(8,128)(2,1)S(1)} async-done(((bf16[8,48,384]{2,1,0:T(8,128)(2,1)}), bf16[8,48,384]{2,1,0:T(8,128)(2,1)S(1)}, u32[]{:S(2)}, u32[]{:S(2)}) %all-to-all-start) | async-done | bytes 294944 | tf_op jit(solution)/shard_map/all_to_all | solution.py:426
  26.1 0.1 fusion.15
  26.2 0.2 subtract_convert_fusion.1
  26.5 2.5 %collective-permute-start = (bf16[432,256]{1,0:T(8,128)(2,1)S(1)}, bf16[432,256]{1,0:T(8,128)(2,1)S(1)}, u32[]{:S(2)}, u32[]{:S(2)}) collective-permute-start(bf16[432,256]{1,0:T(8,128)(2,1)S(1)} %slice_dynamic-update-slice_fusion), channel_id=1, source_target_pairs={{8,0},{16,8},{24,16},{32,24},{40,32},{48,40},{56,48},{64,56},{72,6... | collective-permute-start | bytes 663560 | tf_op jit(solution)/shard_map/ppermute | solution.py:459
  29.0 0.0 copy-done.6
  29.0 3.4 %collective-permute-start.1 = (f32[112,128]{1,0:T(8,128)S(1)}, f32[112,128]{1,0:T(8,128)S(1)}, u32[]{:S(2)}, u32[]{:S(2)}) collective-permute-start(f32[112,128]{1,0:T(8,128)S(1)} %slice.90), channel_id=1, source_target_pairs={{0,8},{8,16},{16,24},{24,32},{32,40},{40,48},{48,56},{56,64},{64,7... | collective-permute-start | bytes 172040 | tf_op jit(solution)/shard_map/ppermute | solution.py:460
  32.4 3.6 %collective-permute-done.1.prev_ref = f32[112,128]{1,0:T(8,128)S(1)} collective-permute-done((f32[112,128]{1,0:T(8,128)S(1)}, f32[112,128]{1,0:T(8,128)S(1)}, u32[]{:S(2)}, u32[]{:S(2)}) %collective-permute-start.1) | collective-permute-done | bytes 57376 | tf_op jit(solution)/shard_map/ppermute | solution.py:460
  36.0 0.0 collective-permute-done.next_ref
  36.0 0.0 copy-done.1
  36.0 0.0 copy-done.3
  36.0 0.0 copy-done.4
  36.0 0.0 copy-done.5
  36.0 15.0 %pair_field.1 = (f32[32,384]{1,0:T(8,128)}, f32[64,384]{1,0:T(8,128)S(1)}, bf16[32,256]{1,0:T(8,128)(2,1)S(1)}, f32[512,128]{1,0:T(8,128)}) custom-call(s32[2]{0:T(128)S(1)} %copy-done.3, f32[32]{0:T(128)S(1)} %copy-done.5, bf16[432,256]{1,0:T(8,128)(2,1)S(1)} %collective-permute-done.next_ref, f32[112,128]{1,0:T(8,128)S(1)} %collective-permute-done.1.prev_ref, ...), custom_call_target="tpu_custom_call" | custom-call | flops 12000000000 | bytes 5000000 | tf_op jit(solution)/shard_map/pair_field/pallas_call | solution.py:350
  51.0 12.2 %all-to-all-start.1 = ((f32[64,8,128]{2,1,0:T(8,128)}), f32[64,8,128]{2,1,0:T(8,128)S(1)}, u32[]{:S(2)}, u32[]{:S(2)}) async-start(f32[64,8,128]{2,1,0:T(8,128)} %bitcast.6), calls=%async_computation.1 | async-start | bytes 524288 | tf_op jit(solution)/shard_map/all_to_all | solution.py:468
  63.2 3.4 %collective-permute-start.2 = (bf16[32,256]{1,0:T(8,128)(2,1)S(1)}, bf16[32,256]{1,0:T(8,128)(2,1)S(1)}, u32[]{:S(2)}, u32[]{:S(2)}) collective-permute-start(bf16[32,256]{1,0:T(8,128)(2,1)S(1)} %get-tuple-element.20), channel_id=1, source_target_pairs={{0,8},{8,16},{16,24},{24,32},{32,40},{40,48},{48,56},{56,64},{64,7... | collective-permute-start | bytes 49160 | tf_op jit(solution)/shard_map/ppermute | solution.py:467
  66.6 3.3 %collective-permute-done.2 = bf16[32,256]{1,0:T(8,128)(2,1)S(1)} collective-permute-done((bf16[32,256]{1,0:T(8,128)(2,1)S(1)}, bf16[32,256]{1,0:T(8,128)(2,1)S(1)}, u32[]{:S(2)}, u32[]{:S(2)}) %collective-permute-start.2) | collective-permute-done | bytes 16416 | tf_op jit(solution)/shard_map/ppermute | solution.py:467
  69.9 0.3 convolution_convert_fusion
  70.1 5.3 %all-to-all-done.1 = f32[64,8,128]{2,1,0:T(8,128)S(1)} async-done(((f32[64,8,128]{2,1,0:T(8,128)}), f32[64,8,128]{2,1,0:T(8,128)S(1)}, u32[]{:S(2)}, u32[]{:S(2)}) %all-to-all-start.1) | async-done | bytes 262176 | tf_op jit(solution)/shard_map/all_to_all | solution.py:468
  75.4 0.1 reduce_sum.18
  75.6 14.7 %all_to_all.20 = bf16[8,32,512]{2,1,0:T(8,128)(2,1)S(1)} all-to-all(bf16[8,32,512]{2,1,0:T(8,128)(2,1)S(1)} %pad_maximum_fusion), channel_id=1, replica_groups=mesh['bin'=64,'diag'=8] {'diag'}, dimensions={0} | all-to-all | bytes 524288 | tf_op jit(solution)/shard_map/all_to_all | solution.py:481
  90.3 0.8 broadcast_in_dim.19
  91.1 6.4 %all-to-all-start.3 = ((f32[64,5,1,128]{3,2,1,0:T(1,128)}), f32[64,5,1,128]{3,2,1,0:T(1,128)S(1)}, u32[]{:S(2)}, u32[]{:S(2)}) async-start(f32[64,5,1,128]{3,2,1,0:T(1,128)} %broadcast_in_dim.19), calls=%async_computation.3 | async-start | bytes 327680 | tf_op jit(solution)/shard_map/all_to_all | solution.py:484
  97.5 0.6 slice.91
  98.1 9.6 %all-to-all-done.3 = f32[64,5,1,128]{3,2,1,0:T(1,128)S(1)} async-done(((f32[64,5,1,128]{3,2,1,0:T(1,128)}), f32[64,5,1,128]{3,2,1,0:T(1,128)S(1)}, u32[]{:S(2)}, u32[]{:S(2)}) %all-to-all-start.3) | async-done | bytes 163872 | tf_op jit(solution)/shard_map/all_to_all | solution.py:484
  107.7 0.8 finish.1
  (20 shorter events, 0.2 us)
Async XLA Ops:
  2.3 23.8 %all-to-all-start = ((bf16[8,48,384]{2,1,0:T(8,128)(2,1)}), bf16[8,48,384]{2,1,0:T(8,128)(2,1)S(1)}, u32[]{:S(2)}, u32[]{:S(2)}) async-start(bf16[8,48,384]{2,1,0:T(8,128)(2,1)} %get-tuple-element.14), calls=%async_computation | async-start | bytes 589824 | tf_op jit(solution)/shard_map/all_to_all | solution.py:426
  13.4 0.9 copy-start
  14.3 0.7 copy-start.2
  15.0 14.0 %copy-start.6 = (f32[32,384]{1,0:T(8,128)S(1)}, f32[32,384]{1,0:T(8,128)}, u32[]{:S(2)}) copy-start(f32[32,384]{1,0:T(8,128)} %get-tuple-element.16) | copy-start | bytes 147460
  16.1 19.9 %copy-start.1 = (s32[384]{0:T(512)S(1)}, s32[384]{0:T(512)}, u32[]{:S(2)}) copy-start(s32[384]{0:T(512)} %limit_ref.1) | copy-start | bytes 4612
  16.1 19.9 %copy-start.3 = (s32[2]{0:T(128)S(1)}, s32[2]{0:T(128)}, u32[]{:S(2)}) copy-start(s32[2]{0:T(128)} %dil_ref.3) | copy-start | bytes 28
  16.1 19.9 %copy-start.4 = (f32[32,256]{1,0:T(8,128)S(1)}, f32[32,256]{1,0:T(8,128)}, u32[]{:S(2)}) copy-start(f32[32,256]{1,0:T(8,128)} %bias_ref.1) | copy-start | bytes 98308
  16.2 19.9 %copy-start.5 = (f32[32]{0:T(128)S(1)}, f32[32]{0:T(128)}, u32[]{:S(2)}) copy-start(f32[32]{0:T(128)} %head_ref.1) | copy-start | bytes 388
  26.5 9.5 %collective-permute-start = (bf16[432,256]{1,0:T(8,128)(2,1)S(1)}, bf16[432,256]{1,0:T(8,128)(2,1)S(1)}, u32[]{:S(2)}, u32[]{:S(2)}) collective-permute-start(bf16[432,256]{1,0:T(8,128)(2,1)S(1)} %slice_dynamic-update-slice_fusion), channel_id=1, source_target_pairs={{8,0},{16,8},{24,16},{32,24},{40,32},{48,40},{56,48},{64,56},{72,6... | collective-permute-start | bytes 663560 | tf_op jit(solution)/shard_map/ppermute | solution.py:459
  29.0 7.0 %collective-permute-start.1 = (f32[112,128]{1,0:T(8,128)S(1)}, f32[112,128]{1,0:T(8,128)S(1)}, u32[]{:S(2)}, u32[]{:S(2)}) collective-permute-start(f32[112,128]{1,0:T(8,128)S(1)} %slice.90), channel_id=1, source_target_pairs={{0,8},{8,16},{16,24},{24,32},{32,40},{40,48},{48,56},{56,64},{64,7... | collective-permute-start | bytes 172040 | tf_op jit(solution)/shard_map/ppermute | solution.py:460
  51.0 24.4 %all-to-all-start.1 = ((f32[64,8,128]{2,1,0:T(8,128)}), f32[64,8,128]{2,1,0:T(8,128)S(1)}, u32[]{:S(2)}, u32[]{:S(2)}) async-start(f32[64,8,128]{2,1,0:T(8,128)} %bitcast.6), calls=%async_computation.1 | async-start | bytes 524288 | tf_op jit(solution)/shard_map/all_to_all | solution.py:468
  63.2 6.7 %collective-permute-start.2 = (bf16[32,256]{1,0:T(8,128)(2,1)S(1)}, bf16[32,256]{1,0:T(8,128)(2,1)S(1)}, u32[]{:S(2)}, u32[]{:S(2)}) collective-permute-start(bf16[32,256]{1,0:T(8,128)(2,1)S(1)} %get-tuple-element.20), channel_id=1, source_target_pairs={{0,8},{8,16},{16,24},{24,32},{32,40},{40,48},{48,56},{56,64},{64,7... | collective-permute-start | bytes 49160 | tf_op jit(solution)/shard_map/ppermute | solution.py:467
  91.1 16.6 %all-to-all-start.3 = ((f32[64,5,1,128]{3,2,1,0:T(1,128)}), f32[64,5,1,128]{3,2,1,0:T(1,128)S(1)}, u32[]{:S(2)}, u32[]{:S(2)}) async-start(f32[64,5,1,128]{3,2,1,0:T(1,128)} %broadcast_in_dim.19), calls=%async_computation.3 | async-start | bytes 327680 | tf_op jit(solution)/shard_map/all_to_all | solution.py:484

commit v7 on v6

--- a/solution.py
+++ b/solution.py
@@ -382,6 +382,36 @@
     )(*operands)
 
 
+def combine_kernel(parts_ref, embed_ref, copies_ref):
+    total = parts_ref[0].astype(F32)
+    for peer in range(1, parts_ref.shape[0]):
+        total = total + parts_ref[peer].astype(F32)
+    columns = embed_ref.shape[1]
+    embed_ref[...] = total[:, :columns]
+    tail = total[:, columns:]
+    place = lax.rem(lax.broadcasted_iota(jnp.int32, (40, 128), 0), 5)
+    block = jnp.zeros((40, 128), F32)
+    for row in range(5):
+        block = jnp.where(place == row, tail[row : row + 1] + tail[row + 5 : row + 6], block)
+    for i in range(copies_ref.shape[0] // 40):
+        copies_ref[40 * i : 40 * i + 40] = block
+
+
+def combine(bins, columns, parts):
+    vmem = pl.BlockSpec(memory_space=pltpu.VMEM)
+    return pl.pallas_call(
+        combine_kernel,
+        out_shape=(
+            jax.ShapeDtypeStruct((parts.shape[1], columns), F32),
+            jax.ShapeDtypeStruct((5 * bins, 128), F32),
+        ),
+        in_specs=[vmem],
+        out_specs=(vmem, vmem),
+        compiler_params=pltpu.CompilerParams(vmem_limit_bytes=16 * 2**20),
+        name="combine",
+    )(parts)
+
+
 def finish_kernel(scaling, every_ref, proj_ref, conv_ref):
     diag_at = lax.axis_index("diag")
     rows = [every_ref[pl.ds(t, 64, stride=5), :] for t in range(5)]
@@ -478,12 +508,8 @@
     parts = jnp.concatenate(
         [parts, jnp.broadcast_to(tail[None], (diags,) + tail.shape)], axis=2
     )
-    total = jnp.sum(lax.all_to_all(parts, "diag", 0, 0).astype(F32), axis=0)
-    grad_embed = total[:, :rows_dev]
-    whole = total[:count, rows_dev:] + total[count : 2 * count, rows_dev:]
-    every = lax.all_to_all(
-        jnp.broadcast_to(whole[None, :, None], (bins, count, 1, 128)), "bin", 0, 0
-    ).reshape(bins * count, 128)
+    grad_embed, copies = combine(bins, rows_dev, lax.all_to_all(parts, "diag", 0, 0))
+    every = lax.all_to_all(copies.reshape(bins, count, 1, 128), "bin", 0, 0).reshape(bins * count, 128)
     scaling = 1.0 / math.sqrt(total_bins * total_diags)
     grad_proj, grad_conv = finish(scaling, every)
     return (predicted, grad_embed, grad_proj, grad_conv)

time: 109 us -> 109 us (level)
  blocking collectives: 14.7 us -> 31.1 us
  waiting for transfers between devices: 31.6 us -> 22 us
  starting transfers between devices: 38.2 us -> 31.7 us
  local copies, waits for them, and re-layouts: 3.12 us -> 1.74 us
    all_to_all x1 -> x2, blocking collectives: 14.7 us -> 31.1 us  [the longest x1 16.4 us: on_device(): lax.all_to_all(copies.reshape(bins, count, 1, 128), 'bin', 0, 0)]
    all_to_all x1 -> x0, waiting for transfers between devices: 9.57 us -> none  [on_device(): lax.all_to_all(jnp.broadcast_to(whole[None, :, None], (bins, count, 1, 12...]
    all_to_all x1 -> x0, starting transfers between devices: 6.43 us -> none  [on_device(): lax.all_to_all(jnp.broadcast_to(whole[None, :, None], (bins, count, 1, 12...]
  transfers between devices with their start and end apart: 6 -> 5, of which waited for: 5 -> 4; matrix products, arithmetic and copies ran while one was open for 2% -> 1% of each run, Pallas kernels for 1% -> 1%
where the time goes in v7:
time: 109 us; the launch traced here: 108 us
  starting transfers between devices  31.7 us (29%)
  blocking collectives  31.1 us (29%)
  waiting for transfers between devices  22 us (20%)
  Pallas kernels  19.2 us (18%)
  local copies, waits for them, and re-layouts  1.74 us (2%)
    all_to_all x1, blocking collectives, on_device(): lax.all_to_all(copies.reshape(bins, count, 1, 128), 'bin', 0, 0)  16.4 us
    pallas_call x1, Pallas kernels, pair_field(): pl.pallas_call(functools.partial(pair_kernel, total_bins, total_diags), o...  15 us
    all_to_all x1, blocking collectives, on_device(): lax.all_to_all(parts, 'diag', 0, 0)  14.7 us
    all_to_all x1, starting transfers between devices, on_device(): shares = lax.all_to_all(sums.reshape(bins, 512 // bins, 128), 'bin', 0, 0)  12.2 us
    all_to_all x1, starting transfers between devices, on_device(): got = lax.all_to_all(pack, 'diag', 0, 0)  10.3 us
    all_to_all x1, waiting for transfers between devices, on_device(): got = lax.all_to_all(pack, 'diag', 0, 0)  9.9 us
    all_to_all x1, waiting for transfers between devices, on_device(): shares = lax.all_to_all(sums.reshape(bins, 512 // bins, 128), 'bin', 0, 0)  5.28 us
    ppermute x1, waiting for transfers between devices, on_device(): prv = lax.ppermute(own[:, rows_dev - 128:], 'bin', up)  3.58 us
  transfers between devices with their start and end apart: 5, of which 4 were waited for; matrix products, arithmetic and copies ran while one was open for 1% of the time, Pallas kernels for 1%

profile of v7, /device:TPU:8, one launch (start us, length us, event | category | flops | bytes accessed | tf_op | source)
XLA Modules:
  0.0 108.2 jit_solution(14873376493083477130)
XLA Ops:
  0.6 1.7 %prepare.1 = (bf16[8,48,384]{2,1,0:T(8,128)(2,1)}, f32[32,384]{1,0:T(8,128)}) custom-call(bf16[32,384]{1,0:T(8,128)(2,1)} %emb_hbm.1, bf16[32,64]{1,0:T(8,128)(2,1)} %proj_hbm.1, f32[32,384]{1,0:T(8,128)} %cot_hbm.1, s32[384]{0:T(512)} %limit_ref.1), custom_call_target="tpu_custom_call" | custom-call | tf_op jit(solution)/shard_map/prepare/pallas_call | solution.py:113
  2.3 10.3 %all-to-all-start = ((bf16[8,48,384]{2,1,0:T(8,128)(2,1)}), bf16[8,48,384]{2,1,0:T(8,128)(2,1)S(1)}, u32[]{:S(2)}, u32[]{:S(2)}) async-start(bf16[8,48,384]{2,1,0:T(8,128)(2,1)} %get-tuple-element.16), calls=%async_computation | async-start | bytes 589824 | tf_op jit(solution)/shard_map/all_to_all | solution.py:456
  12.6 0.8 convert.13
  13.4 0.0 copy-start
  13.4 0.9 copy-done
  14.3 0.0 copy-start.2
  14.3 0.7 copy-done.2
  15.0 0.0 copy-start.6
  15.0 1.1 %band_weights.1.t_ref = bf16[4,128,1152]{2,1,0:T(8,128)(2,1)S(1)} custom-call(s32[2]{0:T(128)S(1)} %copy-done.2, bf16[2,9,32,32]{3,2,1,0:T(8,128)(2,1)S(1)} %copy-done), custom_call_target="tpu_custom_call" | custom-call | flops 100000000 | bytes 2000000 | tf_op jit(solution)/shard_map/band_weights/pallas_call | solution.py:61
  16.1 0.0 copy-start.1
  16.1 0.0 copy-start.3
  16.1 0.0 copy-start.4
  16.2 0.0 copy-start.5
  16.2 9.9 %all-to-all-done = bf16[8,48,384]{2,1,0:T(8,128)(2,1)S(1)} async-done(((bf16[8,48,384]{2,1,0:T(8,128)(2,1)}), bf16[8,48,384]{2,1,0:T(8,128)(2,1)S(1)}, u32[]{:S(2)}, u32[]{:S(2)}) %all-to-all-start) | async-done | bytes 294944 | tf_op jit(solution)/shard_map/all_to_all | solution.py:456
  26.1 0.1 fusion.15
  26.2 0.2 subtract_convert_fusion.1
  26.5 2.5 %collective-permute-start = (bf16[432,256]{1,0:T(8,128)(2,1)S(1)}, bf16[432,256]{1,0:T(8,128)(2,1)S(1)}, u32[]{:S(2)}, u32[]{:S(2)}) collective-permute-start(bf16[432,256]{1,0:T(8,128)(2,1)S(1)} %slice_dynamic-update-slice_fusion), channel_id=1, source_target_pairs={{8,0},{16,8},{24,16},{32,24},{40,32},{48,40},{56,48},{64,56},{72,6... | collective-permute-start | bytes 663560 | tf_op jit(solution)/shard_map/ppermute | solution.py:489
  29.0 0.0 copy-done.6
  29.0 3.4 %collective-permute-start.1 = (f32[112,128]{1,0:T(8,128)S(1)}, f32[112,128]{1,0:T(8,128)S(1)}, u32[]{:S(2)}, u32[]{:S(2)}) collective-permute-start(f32[112,128]{1,0:T(8,128)S(1)} %slice.78), channel_id=1, source_target_pairs={{0,8},{8,16},{16,24},{24,32},{32,40},{40,48},{48,56},{56,64},{64,7... | collective-permute-start | bytes 172040 | tf_op jit(solution)/shard_map/ppermute | solution.py:490
  32.4 3.6 %collective-permute-done.1.prev_ref = f32[112,128]{1,0:T(8,128)S(1)} collective-permute-done((f32[112,128]{1,0:T(8,128)S(1)}, f32[112,128]{1,0:T(8,128)S(1)}, u32[]{:S(2)}, u32[]{:S(2)}) %collective-permute-start.1) | collective-permute-done | bytes 57376 | tf_op jit(solution)/shard_map/ppermute | solution.py:490
  36.0 0.0 collective-permute-done.next_ref
  36.0 0.0 copy-done.1
  36.0 0.0 copy-done.3
  36.0 0.0 copy-done.4
  36.0 0.0 copy-done.5
  36.0 15.0 %pair_field.1 = (f32[32,384]{1,0:T(8,128)}, f32[64,384]{1,0:T(8,128)S(1)}, bf16[32,256]{1,0:T(8,128)(2,1)S(1)}, f32[512,128]{1,0:T(8,128)}) custom-call(s32[2]{0:T(128)S(1)} %copy-done.3, f32[32]{0:T(128)S(1)} %copy-done.5, bf16[432,256]{1,0:T(8,128)(2,1)S(1)} %collective-permute-done.next_ref, f32[112,128]{1,0:T(8,128)S(1)} %collective-permute-done.1.prev_ref, ...), custom_call_target="tpu_custom_call" | custom-call | flops 12000000000 | bytes 5000000 | tf_op jit(solution)/shard_map/pair_field/pallas_call | solution.py:350
  51.0 12.2 %all-to-all-start.1 = ((f32[64,8,128]{2,1,0:T(8,128)}), f32[64,8,128]{2,1,0:T(8,128)S(1)}, u32[]{:S(2)}, u32[]{:S(2)}) async-start(f32[64,8,128]{2,1,0:T(8,128)} %bitcast.6), calls=%async_computation.1 | async-start | bytes 524288 | tf_op jit(solution)/shard_map/all_to_all | solution.py:498
  63.2 3.4 %collective-permute-start.2 = (bf16[32,256]{1,0:T(8,128)(2,1)S(1)}, bf16[32,256]{1,0:T(8,128)(2,1)S(1)}, u32[]{:S(2)}, u32[]{:S(2)}) collective-permute-start(bf16[32,256]{1,0:T(8,128)(2,1)S(1)} %get-tuple-element.22), channel_id=1, source_target_pairs={{0,8},{8,16},{16,24},{24,32},{32,40},{40,48},{48,56},{56,64},{64,7... | collective-permute-start | bytes 49160 | tf_op jit(solution)/shard_map/ppermute | solution.py:497
  66.6 3.3 %collective-permute-done.2 = bf16[32,256]{1,0:T(8,128)(2,1)S(1)} collective-permute-done((bf16[32,256]{1,0:T(8,128)(2,1)S(1)}, bf16[32,256]{1,0:T(8,128)(2,1)S(1)}, u32[]{:S(2)}, u32[]{:S(2)}) %collective-permute-start.2) | collective-permute-done | bytes 16416 | tf_op jit(solution)/shard_map/ppermute | solution.py:497
  69.9 0.3 convolution_convert_fusion
  70.1 5.3 %all-to-all-done.1 = f32[64,8,128]{2,1,0:T(8,128)S(1)} async-done(((f32[64,8,128]{2,1,0:T(8,128)}), f32[64,8,128]{2,1,0:T(8,128)S(1)}, u32[]{:S(2)}, u32[]{:S(2)}) %all-to-all-start.1) | async-done | bytes 262176 | tf_op jit(solution)/shard_map/all_to_all | solution.py:498
  75.4 0.1 reduce_sum.9
  75.6 14.7 %all_to_all.20.parts_ref = bf16[8,32,512]{2,1,0:T(8,128)(2,1)S(1)} all-to-all(bf16[8,32,512]{2,1,0:T(8,128)(2,1)S(1)} %pad_maximum_fusion), channel_id=1, replica_groups=mesh['bin'=64,'diag'=8] {'diag'}, dimensions={0} | all-to-all | bytes 524288 | tf_op jit(solution)/shard_map/all_to_all | solution.py:511
  90.3 0.7 combine.1
  90.9 16.4 %all_to_all.21 = f32[64,5,1,128]{3,2,1,0:T(1,128)S(1)} all-to-all(f32[64,5,1,128]{3,2,1,0:T(1,128)S(1)} %bitcast.19), channel_id=1, replica_groups=mesh['bin'=64,'diag'=8] {'bin'}, dimensions={0} | all-to-all | bytes 327680 | tf_op jit(solution)/shard_map/all_to_all | solution.py:512
  107.3 0.8 finish.1
  (18 shorter events, 0.2 us)
Async XLA Ops:
  2.3 23.8 %all-to-all-start = ((bf16[8,48,384]{2,1,0:T(8,128)(2,1)}), bf16[8,48,384]{2,1,0:T(8,128)(2,1)S(1)}, u32[]{:S(2)}, u32[]{:S(2)}) async-start(bf16[8,48,384]{2,1,0:T(8,128)(2,1)} %get-tuple-element.16), calls=%async_computation | async-start | bytes 589824 | tf_op jit(solution)/shard_map/all_to_all | solution.py:456
  13.4 0.9 copy-start
  14.3 0.7 copy-start.2
  15.0 14.0 %copy-start.6 = (f32[32,384]{1,0:T(8,128)S(1)}, f32[32,384]{1,0:T(8,128)}, u32[]{:S(2)}) copy-start(f32[32,384]{1,0:T(8,128)} %get-tuple-element.18) | copy-start | bytes 147460
  16.1 19.9 %copy-start.1 = (s32[384]{0:T(512)S(1)}, s32[384]{0:T(512)}, u32[]{:S(2)}) copy-start(s32[384]{0:T(512)} %limit_ref.1) | copy-start | bytes 4612
  16.1 19.9 %copy-start.3 = (s32[2]{0:T(128)S(1)}, s32[2]{0:T(128)}, u32[]{:S(2)}) copy-start(s32[2]{0:T(128)} %dil_ref.3) | copy-start | bytes 28
  16.1 19.9 %copy-start.4 = (f32[32,256]{1,0:T(8,128)S(1)}, f32[32,256]{1,0:T(8,128)}, u32[]{:S(2)}) copy-start(f32[32,256]{1,0:T(8,128)} %bias_ref.1) | copy-start | bytes 98308
  16.2 19.9 %copy-start.5 = (f32[32]{0:T(128)S(1)}, f32[32]{0:T(128)}, u32[]{:S(2)}) copy-start(f32[32]{0:T(128)} %head_ref.1) | copy-start | bytes 388
  26.5 9.5 %collective-permute-start = (bf16[432,256]{1,0:T(8,128)(2,1)S(1)}, bf16[432,256]{1,0:T(8,128)(2,1)S(1)}, u32[]{:S(2)}, u32[]{:S(2)}) collective-permute-start(bf16[432,256]{1,0:T(8,128)(2,1)S(1)} %slice_dynamic-update-slice_fusion), channel_id=1, source_target_pairs={{8,0},{16,8},{24,16},{32,24},{40,32},{48,40},{56,48},{64,56},{72,6... | collective-permute-start | bytes 663560 | tf_op jit(solution)/shard_map/ppermute | solution.py:489
  29.0 7.0 %collective-permute-start.1 = (f32[112,128]{1,0:T(8,128)S(1)}, f32[112,128]{1,0:T(8,128)S(1)}, u32[]{:S(2)}, u32[]{:S(2)}) collective-permute-start(f32[112,128]{1,0:T(8,128)S(1)} %slice.78), channel_id=1, source_target_pairs={{0,8},{8,16},{16,24},{24,32},{32,40},{40,48},{48,56},{56,64},{64,7... | collective-permute-start | bytes 172040 | tf_op jit(solution)/shard_map/ppermute | solution.py:490
  51.0 24.4 %all-to-all-start.1 = ((f32[64,8,128]{2,1,0:T(8,128)}), f32[64,8,128]{2,1,0:T(8,128)S(1)}, u32[]{:S(2)}, u32[]{:S(2)}) async-start(f32[64,8,128]{2,1,0:T(8,128)} %bitcast.6), calls=%async_computation.1 | async-start | bytes 524288 | tf_op jit(solution)/shard_map/all_to_all | solution.py:498
  63.2 6.7 %collective-permute-start.2 = (bf16[32,256]{1,0:T(8,128)(2,1)S(1)}, bf16[32,256]{1,0:T(8,128)(2,1)S(1)}, u32[]{:S(2)}, u32[]{:S(2)}) collective-permute-start(bf16[32,256]{1,0:T(8,128)(2,1)S(1)} %get-tuple-element.22), channel_id=1, source_target_pairs={{0,8},{8,16},{16,24},{24,32},{32,40},{40,48},{48,56},{56,64},{64,7... | collective-permute-start | bytes 49160 | tf_op jit(solution)/shard_map/ppermute | solution.py:497
